TPU v7x, 32 devices: a whole 2x2x4 slice. The times are simulated.
32 devices in a mesh: dp: 8 (over y, x, core), mp: 4 (over z).
Axes of the slice: x: 2, y: 2, z: 4, core: 2. Of those that a mesh axis runs over, the one named last changes fastest.
Arguments:
- bytes_in: bfloat16 [32, 2048, 768], P('dp', 'mp'), may hold values from -6 to 6
- mask_ratio: int32 [32], P('dp'), may hold values from 5 to 39
- mask_starts: int32 [32, 3], P('dp'), may hold values from 0 to 2047
- mask_lengths: int32 [32, 3], P('dp'), may hold values from 1 to 512
- latents: bfloat16 [256, 1280], P('mp', 'dp'), may hold values from -6 to 6
- col: bfloat16 [6, 1280, 1280], P(None, 'dp', 'mp'), may hold values from -0.15625 to 0.15625
- attn_out: bfloat16 [2, 1280, 1280], P(None, 'dp', 'mp'), may hold values from -1.25 to 1.25
- mlp_down: bfloat16 [2, 1280, 1280], P(None, 'dp', 'mp'), may hold values from -0.15625 to 0.15625
- enc_kv: bfloat16 [2, 768, 1280], P(None, 'dp', 'mp'), may hold values from -0.21875 to 0.21875
- dec_kv: bfloat16 [2, 1280, 768], P(None, 'dp', 'mp'), may hold values from -0.15625 to 0.15625
- dec_queries: bfloat16 [2048, 768], P('mp', 'dp'), may hold values from -6 to 6
- dec_square: bfloat16 [2, 768, 768], P(None, ('dp', 'mp')), may hold values from -0.21875 to 0.21875
- vocab: bfloat16 [768, 262], P(('dp', 'mp')), may hold values from -1.75 to 1.75
- gains: bfloat16 [5, 1280], P(None, ('dp', 'mp')), may hold values from 0.5 to 1.5
- mask_vec: bfloat16 [768], P(('dp', 'mp')), may hold values from -6 to 6
- byte_gain: bfloat16 [768], P(('dp', 'mp')), may hold values from 0.5 to 1.5
- cotangent: bfloat16 [32, 2048, 262], P('dp', 'mp'), may hold values from -6 to 6
Outputs:
- logits: bfloat16 [32, 2048, 262], P('dp', 'mp')
- bytes_grad: float32 [32, 2048, 768], P('dp', 'mp')
- latents_grad: float32 [256, 1280], P('mp', 'dp')
- col_grad: float32 [6, 1280, 1280], P(None, 'dp', 'mp')
- attn_out_grad: float32 [2, 1280, 1280], P(None, 'dp', 'mp')
- mlp_down_grad: float32 [2, 1280, 1280], P(None, 'dp', 'mp')
- enc_kv_grad: float32 [2, 768, 1280], P(None, 'dp', 'mp')
- dec_kv_grad: float32 [2, 1280, 768], P(None, 'dp', 'mp')
- dec_queries_grad: float32 [2048, 768], P('mp', 'dp')
- dec_square_grad: float32 [2, 768, 768], P(None, ('dp', 'mp'))
- vocab_grad: float32 [768, 262], P(('dp', 'mp'))
- gains_grad: float32 [5, 1280], P(None, ('dp', 'mp'))
- mask_vec_grad: float32 [768], P(('dp', 'mp'))
- byte_gain_grad: float32 [768], P(('dp', 'mp'))
Inputs may be any that keep to these rules, and one draw needn't show every extreme that they name: `mask_starts`: spans may run past the last byte; only bytes inside the item are masked. Spans may intersect. `mask_ratio`: percent of positions masked by the spaced pattern.
All inputs are finite; a program needn't handle non-finite values.
Results may differ from a plain program's by a relative error of at most 0.035.
Values may be sent and summed in bfloat16 or wider, within the bound.
No kernel may reach another device: no remote copies, remote signals or barrier semaphores. Data moves between devices by JAX's collectives and lax.ppermute only.
A program may use at most 320 MiB of HBM per device.

v0:
```python
import jax
import jax.numpy as jnp
from jax import lax
from jax.sharding import PartitionSpec as P

D = 768
C = 1280
HEAD = 160
MICRO = 4


def shortened(array):
    return jax.tree.map(lambda a: a.astype(jnp.bfloat16) if a.dtype == jnp.float32 else a, array)


def dot(left, right):
    return jnp.dot(left, right, preferred_element_type=jnp.float32)


def dot_t(left, right):
    return lax.dot_general(
        left,
        right,
        (((left.ndim - 1,), (right.ndim - 1,)), ((), ())),
        preferred_element_type=jnp.float32,
    )


def dot_tn(left, right):
    return lax.dot_general(
        left, right, (((0,), (0,)), ((), ())), preferred_element_type=jnp.float32
    )


def layer_norm(value, gain):
    centre = value - jnp.mean(value, -1, keepdims=True)
    spread_sq = jnp.mean(centre * centre, -1, keepdims=True)
    return centre * lax.rsqrt(spread_sq + 1e-05) * gain


def norm_back(value, gain, grad):
    _, pull = jax.vjp(layer_norm, value, gain)
    return pull(grad)


def row_softmax(scores):
    top = jnp.max(scores, -1, keepdims=True)
    weights = jnp.exp(scores - top)
    total = jnp.sum(weights, -1, keepdims=True)
    return (weights / total, top + jnp.log(total))


def softmax_back(probs, grad):
    return probs * (grad - jnp.sum(grad * probs, -1, keepdims=True))


def masked_rows(ratio, starts, lengths, positions):
    spaced = positions * 73 % 100 < ratio
    within = (positions[:, None] >= starts[None, :]) & (
        positions[:, None] < starts[None, :] + lengths[None, :]
    )
    return jnp.where(spaced | jnp.any(within, axis=1), 1.0, 0.0).astype(jnp.float32)[:, None]


def spread(value):
    return jax.tree.map(
        lambda part, own: part.astype(own.dtype),
        lax.all_gather(shortened(value), "mp", axis=0, tiled=True),
        value,
    )


def collect(value):
    return jax.tree.map(
        lambda part: part.astype(jnp.float32),
        lax.psum_scatter(shortened(value), "mp", scatter_dimension=0, tiled=True),
    )


def gelu_exact(value):
    return jax.nn.gelu(value, approximate=False)


def ffn_forward(resid, gain, w_up, w_down):
    normed_all = spread(layer_norm(resid, gain).astype(jnp.bfloat16))
    hidden = dot(normed_all, w_up)
    active = gelu_exact(hidden).astype(jnp.bfloat16)
    return (resid + collect(dot_t(active, w_down)), (normed_all, hidden, active))


def ffn_backward(grad, resid, gain, w_up, w_down, saved):
    normed_all, hidden, active = saved
    grad_all = spread(grad.astype(jnp.bfloat16))
    d_down = dot_tn(grad_all, active)
    d_active = dot(grad_all, w_down)
    _, pull = jax.vjp(gelu_exact, hidden)
    d_hidden = pull(d_active)[0].astype(jnp.bfloat16)
    d_up = dot_tn(normed_all, d_hidden)
    d_normed = collect(dot_t(d_hidden, w_up))
    d_resid, d_gain = norm_back(resid, gain, d_normed)
    return (grad + d_resid, d_gain, d_up, d_down)


def self_forward(resid, gain, w_query, w_key, w_value, w_out):
    normed_all = spread(layer_norm(resid, gain).astype(jnp.bfloat16))
    count = normed_all.shape[0]
    query = (
        (dot(normed_all, w_query) * HEAD ** (-0.5)).astype(jnp.bfloat16).reshape(count, -1, HEAD)
    )
    keys = dot(normed_all, w_key).astype(jnp.bfloat16).reshape(count, -1, HEAD)
    values = dot(normed_all, w_value).astype(jnp.bfloat16).reshape(count, -1, HEAD)
    scores = jnp.einsum("qhe,khe->hqk", query, keys, preferred_element_type=jnp.float32)
    probs, lse = row_softmax(scores)
    mixed = jnp.einsum(
        "hqk,khe->qhe", probs.astype(jnp.bfloat16), values, preferred_element_type=jnp.float32
    )
    mixed = mixed.astype(jnp.bfloat16).reshape(count, -1)
    return (resid + collect(dot_t(mixed, w_out)), (normed_all, query, keys, values, lse, mixed))


def self_backward(grad, resid, gain, w_query, w_key, w_value, w_out, saved):
    normed_all, query, keys, values, lse, mixed = saved
    count = normed_all.shape[0]
    grad_all = spread(grad.astype(jnp.bfloat16))
    d_out = dot_tn(grad_all, mixed)
    d_mixed = dot(grad_all, w_out).astype(jnp.bfloat16).reshape(query.shape)
    probs = jnp.exp(
        jnp.einsum("qhe,khe->hqk", query, keys, preferred_element_type=jnp.float32) - lse
    )
    d_probs = jnp.einsum("qhe,khe->hqk", d_mixed, values, preferred_element_type=jnp.float32)
    d_scores = softmax_back(probs, d_probs).astype(jnp.bfloat16)
    d_values = jnp.einsum(
        "hqk,qhe->khe", probs.astype(jnp.bfloat16), d_mixed, preferred_element_type=jnp.float32
    )
    d_keys = jnp.einsum("hqk,qhe->khe", d_scores, query, preferred_element_type=jnp.float32)
    d_query = jnp.einsum("hqk,khe->qhe", d_scores, keys, preferred_element_type=jnp.float32)
    d_values = d_values.astype(jnp.bfloat16).reshape(count, -1)
    d_keys = d_keys.astype(jnp.bfloat16).reshape(count, -1)
    d_query = d_query.astype(jnp.bfloat16).reshape(count, -1)
    scale = HEAD ** (-0.5)
    d_wq = dot_tn(normed_all, d_query) * scale
    d_wk = dot_tn(normed_all, d_keys)
    d_wv = dot_tn(normed_all, d_values)
    d_normed = collect(
        dot_t(d_query, w_query) * scale + dot_t(d_keys, w_key) + dot_t(d_values, w_value)
    )
    d_resid, d_gain = norm_back(resid, gain, d_normed)
    return (grad + d_resid, d_gain, d_wq, d_wk, d_wv, d_out)


def item_pass(layer, shared, item):
    latents, col, attn_out, mlp_down, enc_kv, dec_kv, dec_queries = layer
    dec_square, vocab, gains, mask_vec, byte_gain = shared
    bytes_rows, ratio, starts, lengths, cot_rows = item
    gains = gains.astype(jnp.float32)
    mask_vec = mask_vec.astype(jnp.float32)
    byte_gain = byte_gain.astype(jnp.float32)
    rows = bytes_rows.shape[0]
    positions = lax.axis_index("mp") * rows + jnp.arange(rows, dtype=jnp.int32)
    masked = masked_rows(ratio, starts, lengths, positions)
    raw = bytes_rows.astype(jnp.float32)
    start = raw + masked * (mask_vec - raw)
    lat_own = latents.astype(jnp.float32)
    enc_scale = C ** (-0.5)
    byte_all, lat_all = spread(
        (
            layer_norm(start, byte_gain).astype(jnp.bfloat16),
            layer_norm(lat_own, gains[0]).astype(jnp.bfloat16),
        )
    )
    query = (dot(lat_all, col[0]) * enc_scale).astype(jnp.bfloat16)
    keys = dot(byte_all, enc_kv[0]).astype(jnp.bfloat16)
    values = dot(byte_all, enc_kv[1]).astype(jnp.bfloat16)
    scores = lax.psum(dot_t(query, keys).astype(jnp.bfloat16), "mp").astype(jnp.float32)
    probs, lse = row_softmax(scores)
    attended = dot(probs.astype(jnp.bfloat16), values).astype(jnp.bfloat16)
    first = lat_own + collect(dot_t(attended, attn_out[0]))
    second, saved_one = ffn_forward(first, gains[1], col[1], mlp_down[0])
    third, saved_self = self_forward(second, gains[2], col[2], col[3], col[4], attn_out[1])
    fourth, saved_two = ffn_forward(third, gains[3], col[5], mlp_down[1])
    key_all = spread(layer_norm(fourth, gains[4]).astype(jnp.bfloat16))
    dec_keys, dec_values = (
        lax.all_gather(dot(key_all, dec_kv[0]).astype(jnp.bfloat16), "mp", axis=1, tiled=True),
        lax.all_gather(dot(key_all, dec_kv[1]).astype(jnp.bfloat16), "mp", axis=1, tiled=True),
    )
    dec_scale = D ** (-0.5)
    dec_query = (dot(dec_queries, dec_square[0]) * dec_scale).astype(jnp.bfloat16)
    dec_probs, dec_lse = row_softmax(dot_t(dec_query, dec_keys))
    dec_mixed = dot(dec_probs.astype(jnp.bfloat16), dec_values).astype(jnp.bfloat16)
    decoded = dot(dec_mixed, dec_square[1]).astype(jnp.bfloat16)
    logit_rows = dot(decoded, vocab).astype(jnp.bfloat16)
    grad_logits = (cot_rows.astype(jnp.float32) * masked).astype(jnp.bfloat16)
    d_vocab = dot_tn(decoded, grad_logits)
    d_decoded = dot_t(grad_logits, vocab).astype(jnp.bfloat16)
    d_dec_out = dot_tn(dec_mixed, d_decoded)
    d_dec_mixed = dot_t(d_decoded, dec_square[1]).astype(jnp.bfloat16)
    dec_probs = jnp.exp(dot_t(dec_query, dec_keys) - dec_lse)
    d_dec_scores = softmax_back(dec_probs, dot_t(d_dec_mixed, dec_values)).astype(jnp.bfloat16)
    d_key_part = dot_tn(d_dec_scores, dec_query)
    d_value_part = dot_tn(dec_probs.astype(jnp.bfloat16), d_dec_mixed)
    d_dec_query = dot(d_dec_scores, dec_keys).astype(jnp.bfloat16)
    d_dec_in = dot_tn(dec_queries, d_dec_query) * dec_scale
    d_queries = dot_t(d_dec_query, dec_square[0]) * dec_scale
    d_keys_own, d_values_own = (
        lax.psum_scatter(
            d_key_part.astype(jnp.bfloat16), "mp", scatter_dimension=1, tiled=True
        ).astype(jnp.float32),
        lax.psum_scatter(
            d_value_part.astype(jnp.bfloat16), "mp", scatter_dimension=1, tiled=True
        ).astype(jnp.float32),
    )
    d_keys_own = d_keys_own.astype(jnp.bfloat16)
    d_values_own = d_values_own.astype(jnp.bfloat16)
    d_dec_kv = jnp.stack([dot_tn(key_all, d_keys_own), dot_tn(key_all, d_values_own)])
    d_key_norm = collect(dot_t(d_keys_own, dec_kv[0]) + dot_t(d_values_own, dec_kv[1]))
    d_fourth, d_gain_four = norm_back(fourth, gains[4], d_key_norm)
    d_third, d_gain_three, d_up_two, d_down_two = ffn_backward(
        d_fourth, third, gains[3], col[5], mlp_down[1], saved_two
    )
    d_second, d_gain_two, d_self_q, d_self_k, d_self_v, d_self_out = self_backward(
        d_third, second, gains[2], col[2], col[3], col[4], attn_out[1], saved_self
    )
    d_first, d_gain_one, d_up_one, d_down_one = ffn_backward(
        d_second, first, gains[1], col[1], mlp_down[0], saved_one
    )
    grad_all = spread(d_first.astype(jnp.bfloat16))
    d_enc_out = dot_tn(grad_all, attended)
    d_attended = dot(grad_all, attn_out[0]).astype(jnp.bfloat16)
    d_probs = lax.psum(dot_t(d_attended, values).astype(jnp.bfloat16), "mp").astype(jnp.float32)
    enc_probs = jnp.exp(
        lax.psum(dot_t(query, keys).astype(jnp.bfloat16), "mp").astype(jnp.float32) - lse
    )
    d_scores = softmax_back(enc_probs, d_probs).astype(jnp.bfloat16)
    d_values = dot_tn(enc_probs.astype(jnp.bfloat16), d_attended).astype(jnp.bfloat16)
    d_keys = dot_tn(d_scores, query).astype(jnp.bfloat16)
    d_query = dot(d_scores, keys).astype(jnp.bfloat16)
    d_enc_q = dot_tn(lat_all, d_query) * enc_scale
    d_enc_kv = jnp.stack([dot_tn(byte_all, d_keys), dot_tn(byte_all, d_values)])
    d_lat_norm, d_byte_norm = collect(
        (dot_t(d_query, col[0]) * enc_scale, dot_t(d_keys, enc_kv[0]) + dot_t(d_values, enc_kv[1]))
    )
    d_lat_extra, d_gain_zero = norm_back(lat_own, gains[0], d_lat_norm)
    d_latents = d_first + d_lat_extra
    d_start, d_byte_gain = norm_back(start, byte_gain, d_byte_norm)
    d_bytes = d_start * (1.0 - masked)
    d_mask = jnp.sum(d_start * masked, 0)
    layer_part = (
        d_latents,
        jnp.stack([d_enc_q, d_up_one, d_self_q, d_self_k, d_self_v, d_up_two]),
        jnp.stack([d_enc_out, d_self_out]),
        jnp.stack([d_down_one, d_down_two]),
        d_enc_kv,
        d_dec_kv,
        d_queries,
    )
    shared_part = (
        jnp.stack([d_dec_in, d_dec_out]),
        d_vocab,
        jnp.stack([d_gain_zero, d_gain_one, d_gain_two, d_gain_three, d_gain_four]),
        d_mask,
        d_byte_gain,
    )
    return (logit_rows, d_bytes, layer_part, shared_part)


def add_trees(left, right):
    return jax.tree.map(lambda a, b: a + b, left, right)


def per_device(
    bytes_in,
    mask_ratio,
    mask_starts,
    mask_lengths,
    latents,
    col,
    attn_out,
    mlp_down,
    enc_kv,
    dec_kv,
    dec_queries,
    dec_square,
    vocab,
    gains,
    mask_vec,
    byte_gain,
    cotangent,
):
    per_micro = bytes_in.shape[0] // MICRO
    layer_args = (latents, col, attn_out, mlp_down, enc_kv, dec_kv, dec_queries)
    shared_args = (dec_square, vocab, gains, mask_vec, byte_gain)
    layer_total = None
    shared_total = None
    logit_parts = []
    grad_parts = []
    for micro in range(MICRO):
        layer = (
            lax.all_gather(layer_args[0], "dp", axis=1, tiled=True),
            lax.all_gather(layer_args[1], "dp", axis=1, tiled=True),
            lax.all_gather(layer_args[2], "dp", axis=1, tiled=True),
            lax.all_gather(layer_args[3], "dp", axis=1, tiled=True),
            lax.all_gather(layer_args[4], "dp", axis=1, tiled=True),
            lax.all_gather(layer_args[5], "dp", axis=1, tiled=True),
            lax.all_gather(layer_args[6], "dp", axis=1, tiled=True),
        )
        shared = (
            lax.all_gather(shared_args[0], ("dp", "mp"), axis=1, tiled=True),
            lax.all_gather(shared_args[1], ("dp", "mp"), axis=0, tiled=True),
            lax.all_gather(shared_args[2], ("dp", "mp"), axis=1, tiled=True),
            lax.all_gather(shared_args[3], ("dp", "mp"), axis=0, tiled=True),
            lax.all_gather(shared_args[4], ("dp", "mp"), axis=0, tiled=True),
        )
        zero_shapes = [w.shape for w in layer]
        layer_zero = tuple((jnp.zeros(shape, jnp.float32) for shape in zero_shapes))
        shared_zero = tuple((jnp.zeros(w.shape, jnp.float32) for w in shared))
        first_item = micro * per_micro
        items = (
            bytes_in[first_item : first_item + per_micro],
            mask_ratio[first_item : first_item + per_micro],
            mask_starts[first_item : first_item + per_micro],
            mask_lengths[first_item : first_item + per_micro],
            cotangent[first_item : first_item + per_micro],
        )

        def item_step(carry, item):
            logit_rows, d_bytes, layer_part, shared_part = item_pass(layer, shared, item)
            return (
                (add_trees(carry[0], layer_part), add_trees(carry[1], shared_part)),
                (logit_rows, d_bytes),
            )

        (layer_sum, shared_sum), (logit_rows, byte_rows) = lax.scan(
            item_step, (layer_zero, shared_zero), items
        )
        logit_parts.append(logit_rows)
        grad_parts.append(byte_rows)
        layer_sum = jax.tree.map(
            lambda part: part.astype(jnp.float32),
            lax.psum_scatter(shortened(layer_sum), "dp", scatter_dimension=1, tiled=True),
        )
        shared_sum = (
            lax.psum_scatter(shared_sum[0], ("dp", "mp"), scatter_dimension=1, tiled=True),
            lax.psum_scatter(shared_sum[1], ("dp", "mp"), scatter_dimension=0, tiled=True),
            lax.psum_scatter(shared_sum[2], ("dp", "mp"), scatter_dimension=1, tiled=True),
            lax.psum_scatter(shared_sum[3], ("dp", "mp"), scatter_dimension=0, tiled=True),
            lax.psum_scatter(shared_sum[4], ("dp", "mp"), scatter_dimension=0, tiled=True),
        )
        if micro == 0:
            layer_total, shared_total = (layer_sum, shared_sum)
        else:
            layer_total = add_trees(layer_total, layer_sum)
            shared_total = add_trees(shared_total, shared_sum)
    logits = jnp.concatenate(logit_parts, 0)
    bytes_grad = jnp.concatenate(grad_parts, 0)
    return (
        logits,
        bytes_grad,
        layer_total[0],
        layer_total[1],
        layer_total[2],
        layer_total[3],
        layer_total[4],
        layer_total[5],
        layer_total[6],
        shared_total[0],
        shared_total[1],
        shared_total[2],
        shared_total[3],
        shared_total[4],
    )


def solution(mesh):
    return jax.shard_map(
        per_device,
        mesh=mesh,
        in_specs=(
            P("dp", "mp", None),
            P("dp"),
            P("dp", None),
            P("dp", None),
            P("mp", "dp"),
            P(None, "dp", "mp"),
            P(None, "dp", "mp"),
            P(None, "dp", "mp"),
            P(None, "dp", "mp"),
            P(None, "dp", "mp"),
            P("mp", "dp"),
            P(None, ("dp", "mp"), None),
            P(("dp", "mp"), None),
            P(None, ("dp", "mp")),
            P(("dp", "mp")),
            P(("dp", "mp")),
            P("dp", "mp", None),
        ),
        out_specs=(
            P("dp", "mp", None),
            P("dp", "mp", None),
            P("mp", "dp"),
            P(None, "dp", "mp"),
            P(None, "dp", "mp"),
            P(None, "dp", "mp"),
            P(None, "dp", "mp"),
            P(None, "dp", "mp"),
            P("mp", "dp"),
            P(None, ("dp", "mp"), None),
            P(("dp", "mp"), None),
            P(None, ("dp", "mp")),
            P(("dp", "mp")),
            P(("dp", "mp")),
        ),
        check_vma=False,
    )
```

profile of v0, /device:TPU:11, one launch (start us, length us, event | category | flops | bytes accessed | tf_op | source)
XLA Modules:
  0.0 3580.9 jit_solution(4850732273799495641)
XLA Ops:
  9.8 39.5 %all-reduce.24 = (bf16[768]{0:T(1024)(128)(2,1)S(1)}, bf16[768]{0:T(1024)(128)(2,1)S(1)}) all-reduce(bf16[768]{0:T(1024)(128)(2,1)S(1)} %dynamic-update-slice, bf16[768]{0:T(1024)(128)(2,1)S(1)} %dynamic-update-slice.1), channel_id=1, replica_groups=mesh['dp'=8,'mp'=4] {'dp','mp'}, use_global_device_ids=true, to_apply=%add | all-reduce | flops 1536 | bytes 6144
  65.7 61.8 %all-gather.1 = bf16[32,40,5]{1,2,0:T(8,128)(2,1)S(1)} all-gather(bf16[1,40,5]{1,2,0:T(8,128)(2,1)S(1)} %bitcast.1074), channel_id=1, replica_groups=mesh['dp'=8,'mp'=4] {'dp','mp'}, dimensions={0}, use_global_device_ids=true | all-gather | bytes 13200 | tf_op jit(solution)/shard_map/all_gather | solution.py:309
  155.4 25.3 all_gather.262
  206.1 43.1 %all-gather.13.cloned.1.call-done = bf16[6,1280,320]{2,1,0:T(8,128)(2,1)} async-done(((bf16[6,160,320]{2,1,0:T(8,128)(2,1)}), bf16[6,1280,320]{2,1,0:T(8,128)(2,1)}) %all-gather.13.cloned.1.call-update) | async-done | bytes 4915216 | tf_op jit(solution)/shard_map/all_gather | solution.py:299
  259.7 79.9 %all-reduce.47.cloned.1.call-done = (bf16[256,2048]{1,0:T(8,128)(2,1)}, bf16[256,2048]{1,0:T(8,128)(2,1)}) async-done(((bf16[256,2048]{1,0:T(8,128)(2,1)}, bf16[256,2048]{1,0:T(8,128)(2,1)}), (bf16[256,2048]{1,0:T(8,128)(2,1)}, bf16[256,2048]{1,0:T(8,128)(2,1)})) %all-reduce.47.cloned.1.call-update) | async-done | bytes 2097168 | tf_op jit(solution)/shard_map/while/body/eval_jaxpr/psum | solution.py:174
  345.5 24.5 all-gather.17.cloned.1.call-done
  391.5 23.6 reduce-scatter.97.cloned.1.call-done
  449.6 22.4 all_gather.269
  478.0 20.2 reduce-scatter.83.cloned.1.call-done
  544.7 18.4 all_gather.258
  563.1 72.2 %all_gather.277 = bf16[768,262]{1,0:T(8,128)(2,1)} all-gather(bf16[24,262]{1,0:T(8,128)(2,1)S(1)} %copy-done.378), channel_id=1, replica_groups=mesh['dp'=8,'mp'=4] {'dp','mp'}, dimensions={0}, use_global_device_ids=true | all-gather | bytes 415008 | tf_op jit(solution)/shard_map/all_gather | solution.py:308
  773.2 19.4 reduce-scatter.115.cloned.1.call-done
  819.1 20.5 reduce-scatter.117.cloned.1.call-done
  891.2 23.8 reduce-scatter.141.cloned.1.call-done
  917.3 19.4 reduce-scatter.143.cloned.1.call-done
  940.1 20.9 reduce-scatter.145.cloned.1.call-done
  1015.2 21.9 reduce-scatter.119.cloned.1.call-done
  1108.1 23.9 reduce-scatter.121.cloned.1.call-done
  1186.9 22.5 reduce-scatter.123.cloned.1.call-done
  1253.8 89.2 %all-reduce.45.cloned.1.call-done = (bf16[256,2048]{1,0:T(8,128)(2,1)}, bf16[256,2048]{1,0:T(8,128)(2,1)}) async-done(((bf16[256,2048]{1,0:T(8,128)(2,1)}, bf16[256,2048]{1,0:T(8,128)(2,1)}), (bf16[256,2048]{1,0:T(8,128)(2,1)}, bf16[256,2048]{1,0:T(8,128)(2,1)})) %all-reduce.45.cloned.1.call-update) | async-done | bytes 2097168 | tf_op jit(solution)/shard_map/while/body/eval_jaxpr/psum | solution.py:229
  1366.6 46.9 %reduce-scatter.125.cloned.1.call-done = bf16[512,768]{1,0:T(8,128)(2,1)} async-done(((bf16[2048,768]{1,0:T(8,128)(2,1)}), bf16[512,768]{1,0:T(8,128)(2,1)}) %reduce-scatter.125.cloned.1.call-update) | async-done | bytes 786448 | tf_op jit(solution)/shard_map/while/body/eval_jaxpr/reduce_scatter | solution.py:76
  1413.5 63.2 %reduce-scatter.153.cloned.1.call-done = bf16[512,768]{1,0:T(8,128)(2,1)} async-done(((bf16[2048,768]{1,0:T(8,128)(2,1)}), bf16[512,768]{1,0:T(8,128)(2,1)}) %reduce-scatter.153.cloned.1.call-update) | async-done | bytes 786448 | tf_op jit(solution)/shard_map/while/body/eval_jaxpr/reduce_scatter | solution.py:76
  1493.0 55.9 %all-gather.25.cloned.1.call-done = bf16[2048,768]{1,0:T(8,128)(2,1)} async-done(((bf16[512,768]{1,0:T(8,128)(2,1)}), bf16[2048,768]{1,0:T(8,128)(2,1)}) %all-gather.25.cloned.1.call-update) | async-done | bytes 3145744 | tf_op jit(solution)/shard_map/while/body/eval_jaxpr/all_gather | solution.py:68
  1554.9 58.3 %all-gather.21.cloned.1.call-done = bf16[2048,768]{1,0:T(8,128)(2,1)} async-done(((bf16[512,768]{1,0:T(8,128)(2,1)}), bf16[2048,768]{1,0:T(8,128)(2,1)}) %all-gather.21.cloned.1.call-update) | async-done | bytes 3145744 | tf_op jit(solution)/shard_map/while/body/eval_jaxpr/all_gather | solution.py:68
  1623.4 82.2 %all-reduce.43.cloned.1.call-done = (bf16[256,2048]{1,0:T(8,128)(2,1)}, bf16[256,2048]{1,0:T(8,128)(2,1)}) async-done(((bf16[256,2048]{1,0:T(8,128)(2,1)}, bf16[256,2048]{1,0:T(8,128)(2,1)}), (bf16[256,2048]{1,0:T(8,128)(2,1)}, bf16[256,2048]{1,0:T(8,128)(2,1)})) %all-reduce.43.cloned.1.call-update) | async-done | bytes 2097168 | tf_op jit(solution)/shard_map/while/body/eval_jaxpr/psum | solution.py:174
  1733.6 23.5 reduce-scatter.105.cloned.1.call-done
  1810.3 21.0 reduce-scatter.91.cloned.1.call-done
  1899.5 21.9 reduce-scatter.93.cloned.1.call-done
  2044.9 18.4 reduce-scatter.129.cloned.1.call-done
  2090.1 20.6 reduce-scatter.131.cloned.1.call-done
  2161.8 23.4 reduce-scatter.155.cloned.1.call-done
  2187.5 18.7 reduce-scatter.157.cloned.1.call-done
  2208.9 21.6 reduce-scatter.159.cloned.1.call-done
  2281.4 21.9 reduce-scatter.133.cloned.1.call-done
  2354.1 18.5 reduce-scatter.163.cloned.1.call-done
  2372.6 24.1 reduce-scatter.135.cloned.1.call-done
  2448.6 22.3 reduce-scatter.137.cloned.1.call-done
  2523.0 80.0 %all-reduce.41.cloned.1.call-done = (bf16[256,2048]{1,0:T(8,128)(2,1)}, bf16[256,2048]{1,0:T(8,128)(2,1)}) async-done(((bf16[256,2048]{1,0:T(8,128)(2,1)}, bf16[256,2048]{1,0:T(8,128)(2,1)}), (bf16[256,2048]{1,0:T(8,128)(2,1)}, bf16[256,2048]{1,0:T(8,128)(2,1)})) %all-reduce.41.cloned.1.call-update) | async-done | bytes 2097168 | tf_op jit(solution)/shard_map/while/body/eval_jaxpr/psum | solution.py:229
  2672.5 30.3 reduce-scatter.171.cloned.1.call-done
  2982.8 47.4 %reduce-scatter.187.cloned.1.call-done = bf16[160,64]{1,0:T(8,128)(2,1)} async-done(((bf16[1280,64]{1,0:T(8,128)(2,1)}), bf16[160,64]{1,0:T(8,128)(2,1)}) %reduce-scatter.187.cloned.1.call-update) | async-done | bytes 20496
  3031.7 60.9 %reduce-scatter.139.cloned.1.call-done = bf16[512,768]{1,0:T(8,128)(2,1)} async-done(((bf16[2048,768]{1,0:T(8,128)(2,1)}), bf16[512,768]{1,0:T(8,128)(2,1)}) %reduce-scatter.139.cloned.1.call-update) | async-done | bytes 786448 | tf_op jit(solution)/shard_map/while/body/eval_jaxpr/reduce_scatter | solution.py:76
  3092.6 62.5 %reduce-scatter.167.cloned.1.call-done = bf16[512,768]{1,0:T(8,128)(2,1)} async-done(((bf16[2048,768]{1,0:T(8,128)(2,1)}), bf16[512,768]{1,0:T(8,128)(2,1)}) %reduce-scatter.167.cloned.1.call-update) | async-done | bytes 786448 | tf_op jit(solution)/shard_map/while/body/eval_jaxpr/reduce_scatter | solution.py:76
  3164.3 40.2 %all-reduce.23 = (f32[5,1280]{1,0:T(8,128)S(1)}, f32[768]{0:T(1024)S(1)}, f32[768]{0:T(1024)S(1)}) all-reduce(f32[5,1280]{1,0:T(8,128)S(1)} %add_add_fusion.36, f32[768]{0:T(1024)S(1)} %add_add_fusion.38, f32[768]{0:T(1024)S(1)} %add_add_fusion.37), channel_id=95, replica_groups=mesh['dp'=8,'mp'=4] {'dp','mp'}, use_global_device_ids=true, to_apply=%region_227.228.clone | all-reduce | flops 7936 | bytes 63488
  3210.7 33.0 reduce-scatter.181.cloned.1.call-done
  3243.7 82.7 %reduce-scatter.177.cloned.1.call-done = bf16[6,160,320]{2,0,1:T(8,128)(2,1)} async-done(((bf16[6,1280,320]{2,0,1:T(8,128)(2,1)}), bf16[6,160,320]{2,0,1:T(8,128)(2,1)}) %reduce-scatter.177.cloned.1.call-update) | async-done | bytes 614416 | tf_op jit(solution)/shard_map/reduce_scatter | solution.py:339
  3326.4 72.7 %reduce-scatter.183.cloned.1.call-done = bf16[6,160,320]{2,0,1:T(8,128)(2,1)} async-done(((bf16[6,1280,320]{2,0,1:T(8,128)(2,1)}), bf16[6,160,320]{2,0,1:T(8,128)(2,1)}) %reduce-scatter.183.cloned.1.call-update) | async-done | bytes 614416 | tf_op jit(solution)/shard_map/reduce_scatter | solution.py:339
  3399.2 73.2 %reduce-scatter.179.cloned.1.call-done = bf16[6,160,320]{2,0,1:T(8,128)(2,1)} async-done(((bf16[6,1280,320]{2,0,1:T(8,128)(2,1)}), bf16[6,160,320]{2,0,1:T(8,128)(2,1)}) %reduce-scatter.179.cloned.1.call-update) | async-done | bytes 614416 | tf_op jit(solution)/shard_map/reduce_scatter | solution.py:339
  3485.8 87.5 %reduce-scatter.201.cloned.1.call-done = f32[24,262]{1,0:T(8,128)} async-done(((f32[768,262]{1,0:T(8,128)}), f32[24,262]{1,0:T(8,128)}) %reduce-scatter.201.cloned.1.call-update) | async-done | bytes 25168
  (1925 shorter events, 1631.2 us)
Async XLA Ops:
  8.0 172.7 %all-gather.23.cloned.1.call-start = ((), (), s32[]{:S(2)}) async-start(), calls=%async_computation.75 | async-start | bytes 3932160 | tf_op jit(solution)/shard_map/while/body/eval_jaxpr/all_gather | solution.py:68
  64.1 137.8 %all-gather.15.cloned.1.call-start = ((), (), s32[]{:S(2)}) async-start(), calls=%async_computation.63 | async-start | bytes 3932160 | tf_op jit(solution)/shard_map/while/body/eval_jaxpr/all_gather | solution.py:68
  64.9 184.3 %all-gather.13.cloned.1.call-start = ((), (), s32[]{:S(2)}) async-start(), calls=%async_computation.62 | async-start | bytes 6635520 | tf_op jit(solution)/shard_map/all_gather | solution.py:299
  65.6 273.9 %all-reduce.47.cloned.1.call-start = ((), (), s32[]{:S(2)}) async-start(), calls=%async_computation.135 | async-start | bytes 4194304 | tf_op jit(solution)/shard_map/while/body/eval_jaxpr/psum | solution.py:174
  254.6 115.5 %all-gather.17.cloned.1.call-start = ((), (), s32[]{:S(2)}) async-start(), calls=%async_computation.64 | async-start | bytes 2211840 | tf_op jit(solution)/shard_map/all_gather | solution.py:300
  255.2 136.4 %reduce-scatter.81.cloned.1.call-start = ((), (), s32[]{:S(2)}) async-start(), calls=%async_computation.65 | async-start | bytes 819200 | tf_op jit(solution)/shard_map/while/body/eval_jaxpr/reduce_scatter | solution.py:76
  382.7 94.0 %reduce-scatter.99.cloned.1.call-start = ((), (), s32[]{:S(2)}) async-start(), calls=%async_computation.77 | async-start | bytes 819200 | tf_op jit(solution)/shard_map/while/body/eval_jaxpr/reduce_scatter | solution.py:76
  476.6 176.0 %reduce-scatter.101.cloned.1.call-start = ((), (), s32[]{:S(2)}) async-start(), calls=%async_computation.78 | async-start | bytes 819200 | tf_op jit(solution)/shard_map/while/body/eval_jaxpr/reduce_scatter | solution.py:76
  535.9 118.1 %reduce-scatter.85.cloned.1.call-start = ((), (), s32[]{:S(2)}) async-start(), calls=%async_computation.68 | async-start | bytes 819200 | tf_op jit(solution)/shard_map/while/body/eval_jaxpr/reduce_scatter | solution.py:76
  544.1 141.4 %all-gather.11.cloned.1.call-start = ((), (), s32[]{:S(2)}) async-start(), calls=%async_computation.61 | async-start | bytes 2433024 | tf_op jit(solution)/shard_map/all_gather | solution.py:307
  544.7 153.1 %reduce-scatter.87.cloned.1.call-start = ((), (), s32[]{:S(2)}) async-start(), calls=%async_computation.69 | async-start | bytes 819200 | tf_op jit(solution)/shard_map/while/body/eval_jaxpr/reduce_scatter | solution.py:76
  676.8 94.0 %reduce-scatter.113.cloned.1.call-start = ((), (), s32[]{:S(2)}) async-start(), calls=%async_computation.85 | async-start | bytes 491520 | tf_op jit(solution)/shard_map/while/body/eval_jaxpr/reduce_scatter | solution.py:205
  795.2 119.8 %reduce-scatter.141.cloned.1.call-start = ((), (), s32[]{:S(2)}) async-start(), calls=%async_computation.99 | async-start | bytes 491520 | tf_op jit(solution)/shard_map/while/body/eval_jaxpr/reduce_scatter | solution.py:205
  1008.5 99.6 %reduce-scatter.149.cloned.1.call-start = ((), (), s32[]{:S(2)}) async-start(), calls=%async_computation.103 | async-start | bytes 819200 | tf_op jit(solution)/shard_map/while/body/eval_jaxpr/reduce_scatter | solution.py:76
  1089.8 95.8 %reduce-scatter.151.cloned.1.call-start = ((), (), s32[]{:S(2)}) async-start(), calls=%async_computation.104 | async-start | bytes 819200 | tf_op jit(solution)/shard_map/while/body/eval_jaxpr/reduce_scatter | solution.py:76
  1179.9 163.0 %all-reduce.45.cloned.1.call-start = ((), (), s32[]{:S(2)}) async-start(), calls=%async_computation.134 | async-start | bytes 4194304 | tf_op jit(solution)/shard_map/while/body/eval_jaxpr/psum | solution.py:229
  1250.1 163.4 %reduce-scatter.125.cloned.1.call-start = ((), (), s32[]{:S(2)}) async-start(), calls=%async_computation.91 | async-start | bytes 3932160 | tf_op jit(solution)/shard_map/while/body/eval_jaxpr/reduce_scatter | solution.py:76
  1352.8 123.9 %reduce-scatter.153.cloned.1.call-start = ((), (), s32[]{:S(2)}) async-start(), calls=%async_computation.105 | async-start | bytes 3932160 | tf_op jit(solution)/shard_map/while/body/eval_jaxpr/reduce_scatter | solution.py:76
  1363.6 185.3 %all-gather.25.cloned.1.call-start = ((), (), s32[]{:S(2)}) async-start(), calls=%async_computation.80 | async-start | bytes 3932160 | tf_op jit(solution)/shard_map/while/body/eval_jaxpr/all_gather | solution.py:68
  1487.2 126.1 %all-gather.21.cloned.1.call-start = ((), (), s32[]{:S(2)}) async-start(), calls=%async_computation.70 | async-start | bytes 3932160 | tf_op jit(solution)/shard_map/while/body/eval_jaxpr/all_gather | solution.py:68
  1493.0 212.7 %all-reduce.43.cloned.1.call-start = ((), (), s32[]{:S(2)}) async-start(), calls=%async_computation.133 | async-start | bytes 4194304 | tf_op jit(solution)/shard_map/while/body/eval_jaxpr/psum | solution.py:174
  1619.2 114.4 %reduce-scatter.89.cloned.1.call-start = ((), (), s32[]{:S(2)}) async-start(), calls=%async_computation.71 | async-start | bytes 819200 | tf_op jit(solution)/shard_map/while/body/eval_jaxpr/reduce_scatter | solution.py:76
  1802.7 94.7 %reduce-scatter.109.cloned.1.call-start = ((), (), s32[]{:S(2)}) async-start(), calls=%async_computation.83 | async-start | bytes 819200 | tf_op jit(solution)/shard_map/while/body/eval_jaxpr/reduce_scatter | solution.py:76
  1945.3 97.3 %reduce-scatter.127.cloned.1.call-start = ((), (), s32[]{:S(2)}) async-start(), calls=%async_computation.92 | async-start | bytes 491520 | tf_op jit(solution)/shard_map/while/body/eval_jaxpr/reduce_scatter | solution.py:205
  2066.0 119.2 %reduce-scatter.155.cloned.1.call-start = ((), (), s32[]{:S(2)}) async-start(), calls=%async_computation.106 | async-start | bytes 491520 | tf_op jit(solution)/shard_map/while/body/eval_jaxpr/reduce_scatter | solution.py:205
  2274.9 97.7 %reduce-scatter.163.cloned.1.call-start = ((), (), s32[]{:S(2)}) async-start(), calls=%async_computation.110 | async-start | bytes 819200 | tf_op jit(solution)/shard_map/while/body/eval_jaxpr/reduce_scatter | solution.py:76
  2354.0 93.4 %reduce-scatter.165.cloned.1.call-start = ((), (), s32[]{:S(2)}) async-start(), calls=%async_computation.111 | async-start | bytes 819200 | tf_op jit(solution)/shard_map/while/body/eval_jaxpr/reduce_scatter | solution.py:76
  2442.1 160.9 %all-reduce.41.cloned.1.call-start = ((), (), s32[]{:S(2)}) async-start(), calls=%async_computation.132 | async-start | bytes 4194304 | tf_op jit(solution)/shard_map/while/body/eval_jaxpr/psum | solution.py:229
  2510.1 161.6 %reduce-scatter.169.cloned.1.call-start = ((), (), s32[]{:S(2)}) async-start(), calls=%async_computation.113 | async-start | bytes 819200 | tf_op jit(solution)/shard_map/while/body/eval_jaxpr/reduce_scatter | solution.py:76
  2517.3 154.5 %reduce-scatter.173.cloned.1.call-start = ((), (), s32[]{:S(2)}) async-start(), calls=%async_computation.115 | async-start | bytes 819200 | tf_op jit(solution)/shard_map/while/body/eval_jaxpr/reduce_scatter | solution.py:76
  2522.9 149.6 %reduce-scatter.175.cloned.1.call-start = ((), (), s32[]{:S(2)}) async-start(), calls=%async_computation.116 | async-start | bytes 819200 | tf_op jit(solution)/shard_map/while/body/eval_jaxpr/reduce_scatter | solution.py:76
  2616.1 315.4 %reduce-scatter.193.cloned.1.call-start = ((), (), s32[]{:S(2)}) async-start(), calls=%async_computation.125 | async-start | bytes 884736
  2622.0 315.6 %reduce-scatter.197.cloned.1.call-start = ((), (), s32[]{:S(2)}) async-start(), calls=%async_computation.127 | async-start | bytes 884736
  2629.0 324.5 %reduce-scatter.195.cloned.1.call-start = ((), (), s32[]{:S(2)}) async-start(), calls=%async_computation.126 | async-start | bytes 884736
  2639.9 322.6 %reduce-scatter.199.cloned.1.call-start = ((), (), s32[]{:S(2)}) async-start(), calls=%async_computation.128 | async-start | bytes 884736
  2650.6 316.3 %all-reduce.37.cloned.1.call-start = ((), (), s32[]{:S(2)}) async-start(), calls=%async_computation.129 | async-start | bytes 9437184
  2668.8 309.1 %reduce-scatter.189.cloned.1.call-start = ((), (), s32[]{:S(2)}) async-start(), calls=%async_computation.123 | async-start | bytes 368640
  2710.5 268.4 %reduce-scatter.185.cloned.1.call-start = ((), (), s32[]{:S(2)}) async-start(), calls=%async_computation.121 | async-start | bytes 368640
  2714.7 267.2 %reduce-scatter.191.cloned.1.call-start = ((), (), s32[]{:S(2)}) async-start(), calls=%async_computation.124 | async-start | bytes 368640
  2718.9 311.3 %reduce-scatter.187.cloned.1.call-start = ((), (), s32[]{:S(2)}) async-start(), calls=%async_computation.122 | async-start | bytes 368640
  2725.9 366.7 %reduce-scatter.139.cloned.1.call-start = ((), (), s32[]{:S(2)}) async-start(), calls=%async_computation.98 | async-start | bytes 3932160 | tf_op jit(solution)/shard_map/while/body/eval_jaxpr/reduce_scatter | solution.py:76
  2732.6 422.5 %reduce-scatter.167.cloned.1.call-start = ((), (), s32[]{:S(2)}) async-start(), calls=%async_computation.112 | async-start | bytes 3932160 | tf_op jit(solution)/shard_map/while/body/eval_jaxpr/reduce_scatter | solution.py:76
  2742.9 500.8 %reduce-scatter.181.cloned.1.call-start = ((), (), s32[]{:S(2)}) async-start(), calls=%async_computation.119 | async-start | bytes 8847360 | tf_op jit(solution)/shard_map/reduce_scatter | solution.py:339
  2761.9 564.5 %reduce-scatter.177.cloned.1.call-start = ((), (), s32[]{:S(2)}) async-start(), calls=%async_computation.117 | async-start | bytes 8847360 | tf_op jit(solution)/shard_map/reduce_scatter | solution.py:339
  2780.7 618.4 %reduce-scatter.183.cloned.1.call-start = ((), (), s32[]{:S(2)}) async-start(), calls=%async_computation.120 | async-start | bytes 8847360 | tf_op jit(solution)/shard_map/reduce_scatter | solution.py:339
  2799.7 672.7 %reduce-scatter.179.cloned.1.call-start = ((), (), s32[]{:S(2)}) async-start(), calls=%async_computation.118 | async-start | bytes 8847360 | tf_op jit(solution)/shard_map/reduce_scatter | solution.py:339
  2845.1 631.2 %all-reduce.39.cloned.1.call-start = ((), (), s32[]{:S(2)}) async-start(), calls=%async_computation.131 | async-start | bytes 51380224
  2924.3 649.0 %reduce-scatter.201.cloned.1.call-start = ((), (), s32[]{:S(2)}) async-start(), calls=%async_computation.130 | async-start | bytes 1216512
  (566 other events, 9329.9 us)
Sparse Core Ops, SparseCore 0:
  64.3 62.8 all-gather.22
  129.3 72.5 all-gather.14
  203.8 45.2 all-gather.12
  254.7 84.8 all-reduce.46
  341.5 28.4 all-gather.16
  417.2 29.6 all-gather.18
  449.6 26.6 reduce-scatter.98
  536.0 26.8 reduce-scatter.100
  565.7 24.0 reduce-scatter.84
  743.0 27.7 reduce-scatter.112
  794.8 21.6 reduce-scatter.102
  888.7 26.2 reduce-scatter.140
  984.5 28.7 reduce-scatter.146
  1080.5 27.5 reduce-scatter.148
  1156.5 29.1 reduce-scatter.150
  1250.2 92.6 all-reduce.44
  1352.9 60.5 reduce-scatter.124
  1416.4 60.2 reduce-scatter.152
  1487.3 61.5 all-gather.24
  1551.1 62.1 all-gather.20
  1619.3 86.3 all-reduce.42
  1780.3 27.7 reduce-scatter.106
  1871.2 26.1 reduce-scatter.108
  1945.4 23.7 reduce-scatter.94
  2014.5 28.0 reduce-scatter.126
  2065.8 21.5 reduce-scatter.110
  2159.3 25.8 reduce-scatter.154
  2209.0 21.4 reduce-scatter.158
  2252.4 27.6 reduce-scatter.160
  2345.2 27.3 reduce-scatter.162
  2419.6 27.7 reduce-scatter.164
  2510.3 92.7 all-reduce.40
  2674.8 27.9 reduce-scatter.170
  2705.8 37.3 reduce-scatter.192
  2746.2 35.8 reduce-scatter.196
  2785.2 36.0 reduce-scatter.194
  2824.5 34.9 reduce-scatter.198
  2863.1 33.5 reduce-scatter.188
  2899.5 33.7 reduce-scatter.184
  2936.8 45.0 reduce-scatter.190
  2985.5 44.5 reduce-scatter.186
  3032.3 60.2 reduce-scatter.138
  3094.7 60.2 reduce-scatter.166
  3158.5 85.1 reduce-scatter.180
  3247.5 78.8 reduce-scatter.176
  3329.7 69.4 reduce-scatter.182
  3403.0 69.3 reduce-scatter.178
  3478.7 94.5 reduce-scatter.200
  (24 shorter events, 485.3 us)
Sparse Core Ops, SparseCore 1:
  548.1 68.4 all-gather.10
  2668.9 153.4 all-reduce.36
  2924.4 380.9 all-reduce.38
where the time goes:
time: 3600 us; the launch traced here: 3580 us
  waiting for transfers between devices  1830 us (51%)
  blocking collectives  877 us (24%)
  matrix products  428 us (12%)
  local copies, waits for them, and re-layouts  235 us (7%)
  other arithmetic  176 us (5%)
    reduce_scatter x40, waiting for transfers between devices, collect(): lax.psum_scatter(shortened(value), 'mp', scatter_dimension=0, tiled=True)  749 us
    all_gather x33, blocking collectives, spread(): lax.all_gather(shortened(value), 'mp', axis=0, tiled=True)  502 us
    reduce_scatter x4, waiting for transfers between devices, per_device(): lax.psum_scatter(shortened(layer_sum), 'dp', scatter_dimension=1, tiled=T...  262 us
    psum x2, waiting for transfers between devices, item_pass(): lax.psum(dot_t(d_attended, values).astype(jnp.bfloat16), 'mp')  169 us
    dot_general x84, matrix products, dot_t(): lax.dot_general(left, right, (((left.ndim - 1,), (right.ndim - 1,)), ((),...  163 us
    psum x2, waiting for transfers between devices, item_pass(): lax.psum(dot_t(query, keys).astype(jnp.bfloat16), 'mp').astype(jnp.float32)  162 us
    unnamed x86, waiting for transfers between devices  141 us
    dot_general x78, matrix products, dot(): return jnp.dot(left, right, preferred_element_type=jnp.float32)  140 us
  transfers between devices with their start and end apart: 75, of which 60 were waited for; matrix products, arithmetic and copies ran while one was open for 16% of the time, Pallas kernels for 0%

commit v1 on v0

v1 whole, which is shorter than its diff:
```python
import functools
import math

import jax
import jax.numpy as jnp
from jax import lax
from jax.sharding import PartitionSpec as P

HEAD = 160
BF = jnp.bfloat16
F32 = jnp.float32


def dot(left, right):
    return jnp.dot(left, right, preferred_element_type=F32)


def dot_t(left, right):
    return lax.dot_general(
        left,
        right,
        (((left.ndim - 1,), (right.ndim - 1,)), ((), ())),
        preferred_element_type=F32,
    )


def dot_tn(left, right):
    return lax.dot_general(left, right, (((0,), (0,)), ((), ())), preferred_element_type=F32)


def layer_norm(value, gain):
    centre = value - jnp.mean(value, -1, keepdims=True)
    spread_sq = jnp.mean(centre * centre, -1, keepdims=True)
    return centre * lax.rsqrt(spread_sq + 1e-05) * gain


def norm_back(value, gain, grad):
    centre = value - jnp.mean(value, -1, keepdims=True)
    inv = lax.rsqrt(jnp.mean(centre * centre, -1, keepdims=True) + 1e-05)
    unit = centre * inv
    scaled = grad * gain
    d_value = inv * (
        scaled
        - jnp.mean(scaled, -1, keepdims=True)
        - unit * jnp.mean(scaled * unit, -1, keepdims=True)
    )
    return d_value, grad * unit


def masked_rows(ratio, starts, lengths, positions):
    spaced = positions * 73 % 100 < ratio
    within = (positions[:, None] >= starts[None, :]) & (
        positions[:, None] < starts[None, :] + lengths[None, :]
    )
    return jnp.where(spaced | jnp.any(within, axis=1), 1.0, 0.0).astype(F32)


def gelu_exact(value):
    return jax.nn.gelu(value, approximate=False)


def gelu_slope(value):
    return 0.5 * (1.0 + lax.erf(value * 0.7071067811865476)) + value * 0.3989422804014327 * jnp.exp(
        -0.5 * value * value
    )


def nothing_of(value):
    return value[0, 0].astype(F32) * 0.0


class Links:
    def __init__(self, dn, mn):
        self.dn, self.mn = dn, mn
        self.bits = dn.bit_length() - 1
        assert 1 << self.bits == dn and mn & (mn - 1) == 0
        self.chips = [1 << b for b in range(1, self.bits)]
        self.d = lax.axis_index("dp")
        self.z = lax.axis_index("mp")

    def z_of(self, t):
        return (self.z - t) % self.mn

    def ring(self, value):
        parts = [value]
        for _ in range(self.mn - 1):
            parts += yield [("z", 1, parts[-1])]
        return parts

    def direct(self, values):
        got = yield [("z", t, values[t]) for t in range(1, self.mn)]
        return [values[0]] + list(got)

    def natural_z(self, parts):
        shape = parts[0].shape
        size = math.prod(shape[:-1])
        around = [parts[(-k) % self.mn].reshape(size, shape[-1]) for k in range(self.mn)] * 2
        first = ((self.mn - self.z) % self.mn) * size
        whole = lax.dynamic_slice_in_dim(jnp.concatenate(around, 0), first, self.mn * size, 0)
        return [whole[k * size : (k + 1) * size].reshape(shape) for k in range(self.mn)]

    def natural_rows(self, parts):
        size = parts[0].shape[0]
        around = jnp.concatenate([parts[(-k) % self.mn] for k in range(self.mn)] * 2, 0)
        return lax.dynamic_slice_in_dim(
            around, ((self.mn - self.z) % self.mn) * size, self.mn * size, 0
        )

    def natural_columns(self, parts):
        size = parts[0].shape[1]
        around = jnp.concatenate([parts[(-k) % self.mn] for k in range(self.mn)] * 2, 1)
        return lax.dynamic_slice_in_dim(
            around, ((self.mn - self.z) % self.mn) * size, self.mn * size, 1
        )

    def free(self, steps):
        got = None
        while True:
            try:
                sends = steps.send(got)
            except StopIteration as end:
                return end.value
            got = [self.send(*send) for send in sends]

    def send(self, lane, move, value):
        if lane == "z":
            pairs = [(i, (i + move) % self.mn) for i in range(self.mn)]
            return lax.ppermute(value, "mp", pairs)
        return lax.ppermute(value, "dp", [(i, i ^ lane) for i in range(self.dn)])

    def by_index(self, value):
        value = value.reshape((2,) * self.bits + value.shape[1:])
        for axis in range(self.bits):
            up = (self.d >> (self.bits - 1 - axis)) & 1
            value = jnp.where(up == 1, jnp.flip(value, axis), value)
        return value.reshape((self.dn,) + value.shape[self.bits :])

    def spread(self, piece, turned):
        pieces = {0: piece}
        ready = []
        for bit in turned:
            for key in list(pieces):
                mates, ready = ready, []
                got = yield [(bit, 0, pieces[key])] + [(1, 0, pieces[k]) for k in mates]
                pieces[key ^ bit] = got[0]
                pieces.update({k ^ 1: v for k, v in zip(mates, got[1:])})
                ready = [key ^ bit] + ([0] if key == 0 and bit == turned[0] else [])
        got = yield [(1, 0, pieces[k]) for k in ready]
        pieces.update({k ^ 1: v for k, v in zip(ready, got)})
        return pieces

    def sum_ring(self, block):
        total = block(1).astype(BF)
        for t in range(2, self.mn):
            (got,) = yield [("z", 1, total)]
            total = (got.astype(F32) + block(t).astype(F32)).astype(BF)
        (got,) = yield [("z", 1, total)]
        return got.astype(F32) + block(0).astype(F32)

    def sum_mp(self, value):
        got = yield from self.direct([value] * self.mn)
        return sum(self.natural_z(got))

    def sum_mp_rows(self, value):
        size = value.shape[0] // self.mn
        parts = [
            lax.dynamic_slice_in_dim(value, ((self.z + t) % self.mn) * size, size, 0).astype(BF)
            for t in range(self.mn)
        ]
        got = yield from self.direct(parts)
        total = sum(part.astype(F32) for part in got).astype(BF)
        got = yield from self.direct([total] * self.mn)
        return self.natural_rows(got)

    def sum_all(self, value):
        for bit in [1] + self.chips:
            (got,) = yield [(bit, 0, value)]
            value = value + got
        return (yield from self.sum_mp(value))

    def sum_all_rows(self, value):
        for b in range(self.bits):
            half = value.shape[0] // 2
            low, high = value[:half], value[half:]
            up = (self.d >> b) & 1
            give = jnp.where(up == 1, low, high).astype(BF)
            (got,) = yield [(1 << b, 0, give)]
            value = jnp.where(up == 1, high, low) + got.astype(F32)
        value = value.astype(BF)
        value = yield from self.direct([value] * self.mn)
        size = value[0].shape[0]
        value = self.natural_rows(value).astype(F32)
        value = sum(value[k * size : (k + 1) * size] for k in range(self.mn)).astype(BF)
        for b in reversed(range(self.bits)):
            (other,) = yield [(1 << b, 0, value)]
            up = (self.d >> b) & 1
            value = jnp.concatenate(
                [jnp.where(up == 1, other, value), jnp.where(up == 1, value, other)], 0
            )
        return value


def heads_of(value):
    return value.reshape(value.shape[0], -1, HEAD)


def per_device(
    dn,
    mn,
    bytes_in,
    mask_ratio,
    mask_starts,
    mask_lengths,
    latents,
    col,
    attn_out,
    mlp_down,
    enc_kv,
    dec_kv,
    dec_queries,
    dec_square,
    vocab,
    gains,
    mask_vec,
    byte_gain,
    cotangent,
):
    links = Links(dn, mn)
    d, z = links.d, links.z
    items, rows, wide_in = bytes_in.shape
    repeat = mn // items
    assert repeat * items == mn
    seq = rows * mn
    mine = z % items
    chan = col.shape[1] * dn
    enc_scale = chan ** (-0.5)
    dec_scale = wide_in ** (-0.5)

    n_gain, own_gain = gains.shape
    own_in = mask_vec.shape[0]
    in_rows = enc_kv.shape[1]
    col_rows, col_wide = col.shape[1:]
    own_lat, lat_cols = latents.shape
    small = jnp.concatenate([gains.reshape(-1), mask_vec, byte_gain])
    n_small = small.shape[0]
    line = jnp.pad(small, (0, -n_small % lat_cols)).reshape(-1, lat_cols)
    line = jnp.pad(line, ((0, -line.shape[0] % max(16 // mn, 1)), (0, 0)))
    chips = links.chips

    def head_task():
        early = yield from links.direct([jnp.concatenate([latents, line], 0)] * mn)
        early = links.natural_z(early)
        lat = [part[:own_lat] for part in early]
        tall = jnp.concatenate([part[own_lat:] for part in early] + lat, 0)
        n_line = tall.shape[0] - own_lat * mn
        heavy = jnp.concatenate([col[0], enc_kv[0]], 0)
        heavy = jnp.pad(heavy, ((n_line, own_lat * mn - heavy.shape[0]), (0, 0)))
        return (yield from links.spread(jnp.concatenate([tall, heavy], 1), chips))

    cat = lambda parts: jnp.concatenate(parts, -1)

    own_sq = dec_square.shape[1]
    n_voc = vocab.shape[1]
    deck_wide = dec_kv.shape[2]
    own_query, own_pos = dec_queries.T.shape

    def gathered(parts, wide):
        parts = [jnp.pad(p, ((0, -p.shape[0] % 16), (0, wide - p.shape[1]))) for p in parts]
        whole = jnp.concatenate(parts, 0)
        tall = whole.shape[0]
        whole = lax.all_gather(whole, ("dp", "mp"), axis=0, tiled=True)
        whole = whole.reshape(dn, mn, tall, wide)
        edges = [0]
        for p in parts:
            edges.append(edges[-1] + p.shape[0])
        return whole, edges

    def beside(got, row, col, size, wide):
        parts = [got[:, m, row : row + size, col : col + wide] for m in range(mn)]
        return jnp.concatenate([part.reshape(dn * size, wide) for part in parts], 1)

    side = lambda *parts: jnp.concatenate(parts, 1)
    w_one, at_one = gathered(
        [
            side(attn_out[0], col[1]),
            side(mlp_down[0], col[2]),
            side(col[3], col[4]),
            side(attn_out[1], jnp.pad(enc_kv[1], ((0, col_rows - in_rows), (0, 0)))),
        ],
        2 * col_wide,
    )
    late_wide = 2 * (col_wide + deck_wide)
    sq = side(dec_square[0], dec_square[1], vocab)
    sq = jnp.pad(sq, ((0, -own_sq % 16), (0, -sq.shape[1] % late_wide)))
    halves = 2 if own_query % 32 == 0 and 2 * own_pos <= late_wide else 1
    part_rows = own_query // halves
    def first_weight(k):
        return beside(w_one, at_one[k // 2], (k % 2) * col_wide, col_rows, col_wide)

    def last_weights():
        edge = 0
        out = []
        for wide in (col_wide, col_wide, deck_wide, deck_wide):
            out.append(beside(w_two, 0, edge, col_rows, wide))
            edge += wide
        query = [
            w_two[:, :, at_two[1] : at_two[1] + part_rows, h * own_pos : (h + 1) * own_pos]
            for h in range(halves)
        ]
        query = jnp.stack(query, 1).transpose(0, 1, 3, 2, 4).reshape(dn * own_query, seq)
        lines = jnp.concatenate(
            [w_two[:, :, row : row + own_sq] for row in at_two[2:-1]], -1
        ).reshape(dn * mn * own_sq, -1)
        return out + [
            query,
            lines[:, :wide_in],
            lines[:, wide_in : 2 * wide_in],
            lines[:, 2 * wide_in : 2 * wide_in + n_voc],
        ]

    steps = jnp.arange(rows, dtype=jnp.int32)
    masked = jax.vmap(lambda a, b, c: masked_rows(a, b, c, z * rows + steps))(
        mask_ratio, mask_starts, mask_lengths
    )[:, :, None]
    masked_item = masked_rows(
        mask_ratio[mine], mask_starts[mine], mask_lengths[mine], jnp.arange(seq, dtype=jnp.int32)
    )
    cot = cotangent.swapaxes(1, 2)
    head = links.free(head_task())
    held = links.by_index(jnp.stack([head[r] for r in range(dn)]))

    late_parts = [
        side(col[5], mlp_down[1], dec_kv[0], dec_kv[1]),
        jnp.concatenate(jnp.split(dec_queries.T, halves, 0), 1),
    ] + jnp.split(sq, sq.shape[1] // late_wide, 1)
    n_lat = own_lat * mn
    n_line = line.shape[0] * mn
    smalls = held[:, :n_line, :lat_cols].reshape(dn, mn, -1)[:, :, :n_small].astype(F32)
    gain = smalls[:, :, : n_gain * own_gain].reshape(dn, mn, n_gain, own_gain)
    gain = gain.transpose(2, 0, 1, 3).reshape(n_gain, -1)
    vecs = smalls[:, :, n_gain * own_gain :]
    mask_all = vecs[:, :, :own_in].reshape(-1)
    byte_gain_all = vecs[:, :, own_in:].reshape(-1)
    lat = held[:, n_line:, :lat_cols].transpose(1, 0, 2).reshape(n_lat, -1).astype(F32)
    col_zero = held[:, n_line : n_line + col_rows, lat_cols:].reshape(dn * col_rows, -1)
    key_w = held[:, n_line + col_rows : n_line + col_rows + in_rows, lat_cols:]
    key_w = key_w.reshape(dn * in_rows, -1)
    lat_norm = layer_norm(lat, gain[0]).astype(BF)
    query_m = (dot(lat_norm, col_zero) * enc_scale).astype(BF)
    query_key = dot_t(query_m, key_w)
    query_key = links.free(links.sum_mp_rows(query_key))

    raw = bytes_in.astype(F32)
    start = raw + masked * (mask_all - raw)
    byte_norm = layer_norm(start, byte_gain_all).astype(BF)

    scores = jnp.einsum("ld,ird->ilr", query_key, byte_norm, preferred_element_type=F32)
    top = jnp.max(scores, -1)
    weights = jnp.exp(scores - top[:, :, None])
    below = jnp.sum(weights, -1)
    mix = jnp.einsum("ilr,ird->ild", weights.astype(BF), byte_norm, preferred_element_type=F32)
    mix = mix.astype(BF)

    def mix_task(mix, top, below):
        block = lambda t: lax.dynamic_index_in_dim(mix, links.z_of(t) % items, 0, False)
        pack = jnp.stack([top, below])
        got = yield [("z", t, pack) for t in range(1, mn)] + [("z", 1, block(1))]
        stats = jnp.stack([pack] + list(got[: mn - 1]))
        top_all = jnp.max(stats[:, 0], 0)
        shares = jnp.exp(stats[:, 0] - top_all)
        total = sum(links.natural_z(list(stats[:, 1] * shares)))
        pick = lambda t, i: lax.dynamic_index_in_dim(shares[t], i % items, 0, False)[:, None]
        arrived = got[-1].astype(F32) * pick(1 % mn, links.z_of(2))
        for t in range(2, mn):
            arrived = (arrived + block(t).astype(F32) * pick(0, links.z_of(t))).astype(BF)
            (arrived,) = yield [("z", 1, arrived)]
            arrived = arrived.astype(F32)
        whole = arrived + block(0).astype(F32) * pick(0, z)
        whole = whole / lax.dynamic_index_in_dim(total, mine, 0, False)[:, None]
        return whole.astype(BF), shares[0] / total

    assert mn > 2
    mix, share = links.free(mix_task(mix, top, below))
    def cot_task():
        parts = [lax.dynamic_index_in_dim(cot, (z + t) % mn % items, 0, False) for t in range(mn)]
        parts = yield from links.direct(parts)
        return (links.natural_columns(parts).astype(F32) * (masked_item / repeat)[None, :]).astype(BF)

    w_out0, w_up0, w_down0, w_q, w_k, w_v, w_out1 = (first_weight(k) for k in range(7))
    w_value = beside(w_one, at_one[3], col_wide, in_rows, col_wide)
    late_parts[0] = late_parts[0] + (nothing_of(w_one[0, 0]) + nothing_of(mix)).astype(BF)
    w_two, at_two = gathered(
        late_parts,
        late_wide,
    )


    attended = dot(mix, w_value).astype(BF)
    first = lat + dot_t(attended, w_out0)
    norm1 = layer_norm(first, gain[1]).astype(BF)
    hidden1 = dot(norm1, w_up0)
    active1 = gelu_exact(hidden1).astype(BF)
    second = first + dot_t(active1, w_down0)
    norm2 = layer_norm(second, gain[2]).astype(BF)
    query = heads_of((dot(norm2, w_q) * HEAD ** (-0.5)).astype(BF))
    keys = heads_of(dot(norm2, w_k).astype(BF))
    values = heads_of(dot(norm2, w_v).astype(BF))
    s = jnp.einsum("qhe,khe->hqk", query, keys, preferred_element_type=F32)
    probs = jnp.exp(s - jnp.max(s, -1, keepdims=True))
    probs = probs / jnp.sum(probs, -1, keepdims=True)
    mixed = jnp.einsum("hqk,khe->qhe", probs.astype(BF), values, preferred_element_type=F32)
    mixed = mixed.astype(BF).reshape(n_lat, -1)
    third = second + dot_t(mixed, w_out1)
    norm3 = layer_norm(third, gain[3]).astype(BF)
    w_up1, w_down1, w_dk, w_dv, x_query, w_dq, w_do, w_voc = last_weights()
    hidden3 = dot(norm3, w_up1)
    active3 = gelu_exact(hidden3).astype(BF)
    fourth = third + dot_t(active3, w_down1)
    norm4 = layer_norm(fourth, gain[4]).astype(BF)
    grad_logits = links.free(cot_task())

    dec_keys = dot(norm4, w_dk).astype(BF)
    dec_values = dot(norm4, w_dv).astype(BF)
    key_query = (dot_t(dec_keys, w_dq) * dec_scale).astype(BF)
    value_out = dot(dec_values, w_do).astype(BF)
    value_voc = dot(value_out, w_voc).astype(BF)
    s = dot(key_query, x_query)
    p = jnp.exp(s - jnp.max(s, 0, keepdims=True))
    p = p / jnp.sum(p, 0, keepdims=True)
    p_low = p.astype(BF)
    logits_t = dot_tn(value_voc, p_low).astype(BF)
    d_p = dot(value_voc, grad_logits)
    d_s = (p * (d_p - jnp.sum(d_p * p, 0, keepdims=True))).astype(BF)
    d_vv = dot_t(p_low, grad_logits).astype(BF)
    d_kq = (dot_t(d_s, x_query) * dec_scale).astype(BF)
    d_vo = dot_t(d_vv, w_voc).astype(BF)
    d_dk = dot(d_kq, w_dq).astype(BF)
    d_dv = dot_t(d_vo, w_do).astype(BF)

    def logits_task():
        part = lambda t: lax.dynamic_slice_in_dim(logits_t, links.z_of(t) * rows, rows, 1)
        own = part(0)
        got = yield [("z", mn - t, part(t)) for t in range(1, items)]
        out = jnp.concatenate(([own] + list(got)) * 2, 1)
        first = ((items - mine) % items) * rows
        out = lax.dynamic_slice_in_dim(out, first, items * rows, 1)
        return out.reshape(-1, items, rows).transpose(1, 2, 0)

    def by_columns(value, t):
        size = value.shape[-1] // mn
        return lax.slice_in_dim(value, t * size, (t + 1) * size, axis=value.ndim - 1)

    def by_own_columns(value, t):
        size = value.shape[-1] // mn
        return lax.dynamic_slice_in_dim(value, links.z_of(t) * size, size, value.ndim - 1)

    def by_own_rows(value, t):
        size = value.shape[-2] // mn
        return lax.dynamic_slice_in_dim(value, links.z_of(t) * size, size, value.ndim - 2)

    def summed(*terms):
        whole = jnp.concatenate([term.astype(BF) for term in terms], 1)
        ready = nothing_of(whole)
        whole = lax.psum_scatter(whole, "dp", scatter_dimension=0, tiled=True)
        edge, out = 0, []
        for term in terms:
            out.append(whole[:, edge : edge + term.shape[1]])
            edge += term.shape[1]
        return ready, out

    def columns(terms):
        return links.free(
            links.sum_ring(lambda t: jnp.concatenate([by_own_columns(v, t) for v in terms], 1))
        )

    d_res, d_gain4 = norm_back(fourth, gain[4], dot_t(d_dk, w_dk) + dot_t(d_dv, w_dv))
    d_gain4 = jnp.sum(d_gain4, 0)
    ready, rows_a = summed(
        dot_tn(key_query, d_s),
        dot_tn(d_kq, dec_keys),
        dot_tn(dec_values, d_vo),
        dot_tn(value_out, d_vv),
    )
    d_res = d_res + ready
    g_deck = [dot_tn(norm4, d_dk), dot_tn(norm4, d_dv)]

    def ffn_back(d_res, resid, gain, w_up, w_down, normed, hidden, active):
        branch = d_res.astype(BF)
        d_hidden = (dot(branch, w_down) * gelu_slope(hidden)).astype(BF)
        grads = [dot_tn(normed, d_hidden), dot_tn(branch, active)]
        extra, d_gain = norm_back(resid, gain, dot_t(d_hidden, w_up))
        return d_res + extra, jnp.sum(d_gain, 0), grads

    d_res, d_gain3, g_ffn1 = ffn_back(
        d_res, third, gain[3], w_up1, w_down1, norm3, hidden3, active3
    )

    branch = d_res.astype(BF)
    d_mixed = heads_of(dot(branch, w_out1).astype(BF))
    d_probs = jnp.einsum("qhe,khe->hqk", d_mixed, values, preferred_element_type=F32)
    d_s = (probs * (d_probs - jnp.sum(d_probs * probs, -1, keepdims=True))).astype(BF)
    d_values = jnp.einsum("hqk,qhe->khe", probs.astype(BF), d_mixed, preferred_element_type=F32)
    d_keys = jnp.einsum("hqk,qhe->khe", d_s, query, preferred_element_type=F32)
    d_query = jnp.einsum("hqk,khe->qhe", d_s, keys, preferred_element_type=F32)
    d_values = d_values.astype(BF).reshape(n_lat, -1)
    d_keys = d_keys.astype(BF).reshape(n_lat, -1)
    d_query = (d_query * HEAD ** (-0.5)).astype(BF).reshape(n_lat, -1)
    ready, rows_b = summed(
        *g_deck,
        *g_ffn1,
        dot_tn(norm2, d_values),
        dot_tn(branch, mixed),
        dot_tn(norm2, d_query),
        dot_tn(norm2, d_keys),
    )
    extra, d_gain2 = norm_back(
        second, gain[2], dot_t(d_query, w_q) + dot_t(d_keys, w_k) + dot_t(d_values, w_v)
    )
    d_res, d_gain2 = d_res + extra + ready, jnp.sum(d_gain2, 0)
    d_res, d_gain1, g_ffn0 = ffn_back(
        d_res, first, gain[1], w_up0, w_down0, norm1, hidden1, active1
    )

    branch = d_res.astype(BF)
    d_attended = dot(branch, w_out0).astype(BF)
    mix_grad = dot_t(d_attended, w_value)
    value_term = dot_tn(mix, d_attended).astype(BF).reshape(dn, in_rows, chan)
    value_term = jnp.pad(value_term, ((0, 0), (0, col_rows - in_rows), (0, 0)))
    value_term = value_term.reshape(dn * col_rows, chan)
    ready, rows_c = summed(*g_ffn0, dot_tn(branch, attended), value_term)
    around = links.free(links.ring((mix_grad * repeat + ready).astype(BF)))

    def latents_task():
        value = yield from links.sum_ring(lambda t: by_own_rows(branch, t))
        for bit in chips[::-1] + [1]:
            half = value.shape[1] // 2
            low, high = value[:, :half], value[:, half:]
            up = (d & bit) != 0
            (got,) = yield [(bit, 0, jnp.where(up, low, high).astype(BF))]
            value = jnp.where(up, high, low) + got.astype(F32)
        return value

    g_lat = links.free(latents_task())

    e_all = links.natural_rows(around).reshape(mn, n_lat, -1)[:items]
    norm_probs = weights * share[:, :, None]
    d_probs = jnp.einsum("ild,ird->ilr", e_all, byte_norm, preferred_element_type=F32)
    delta = jnp.sum(norm_probs * d_probs, -1)
    delta = links.free(links.sum_mp(delta))
    d_scores = (norm_probs * (d_probs - delta[:, :, None])).astype(BF)
    d_qk = jnp.einsum("ilr,ird->ld", d_scores, byte_norm, preferred_element_type=F32)
    d_qk = links.free(links.sum_all_rows(d_qk))
    d_bn = jnp.einsum("ilr,ld->ird", d_scores, query_key, preferred_element_type=F32)
    d_bn = d_bn + jnp.einsum(
        "ilr,ild->ird", norm_probs.astype(BF), e_all, preferred_element_type=F32
    )
    d_start, d_byte_gain = norm_back(start, byte_gain_all, d_bn)
    d_bytes = d_start * (1.0 - masked)
    d_mask = jnp.sum(d_start * masked, (0, 1))
    d_byte_gain = jnp.sum(d_byte_gain, (0, 1))
    logits = links.free(logits_task())

    d_query_m = (dot(d_qk, key_w) * enc_scale).astype(BF)
    d_lat_norm = links.free(
        links.sum_ring(
            lambda t, value=dot_t(d_query_m, col_zero).astype(BF): by_own_rows(value, t)
        )
    )
    d_qk_own = lax.dynamic_index_in_dim(d_qk.reshape(n_lat, dn, in_rows), d, 1, False)
    g_key = dot_tn(d_qk_own, query_m)
    lat_mine = lax.dynamic_slice_in_dim(lat_norm, d * col_rows, col_rows, 1)
    g_col0 = dot_tn(lat_mine, d_query_m)
    lat_own = lax.dynamic_slice_in_dim(lat, z * own_lat, own_lat, 0)
    d_lat, d_gain0 = norm_back(lat_own, gain[0], d_lat_norm)

    d_gains = jnp.stack([jnp.sum(d_gain0, 0) / dn, d_gain1, d_gain2, d_gain3, d_gain4])
    sums = jnp.concatenate([d_gains.reshape(-1), d_mask, d_byte_gain]).reshape(-1, 128)
    sums = links.free(links.sum_all(sums)).reshape(-1)
    place = d * mn + z
    g_gains = lax.dynamic_slice_in_dim(
        sums[: n_gain * chan].reshape(n_gain, chan), place * own_gain, own_gain, 1
    )
    g_mask = lax.dynamic_slice_in_dim(sums, n_gain * chan + place * own_in, own_in, 0)
    g_byte_gain = lax.dynamic_slice_in_dim(
        sums, n_gain * chan + wide_in + place * own_in, own_in, 0
    )
    g_lat = g_lat + lax.dynamic_slice_in_dim(d_lat, d * lat_cols, lat_cols, 1)
    split = lambda value, *wides: jnp.split(value, [sum(wides[: i + 1]) for i in range(len(wides) - 1)], 1)

    def rows_task(terms):
        value = jnp.concatenate(terms, 1)
        return links.sum_ring(lambda t: by_own_rows(value, t))

    g_xq, g_dq, g_do, g_voc = rows_a
    g_xq = columns([g_xq])
    g_sq = links.free(rows_task([g_dq, g_do, g_voc]))
    after = nothing_of(g_sq).astype(BF)
    g_b = columns([term + after for term in rows_b])
    g_dk, g_dv, g_up1, g_down1, g_v, g_out1, g_q, g_k = split(
        g_b, *([deck_wide] * 2 + [col_wide] * 6)
    )
    after = nothing_of(g_b).astype(BF)
    g_up0, g_down0, g_out0, g_value = split(columns([term + after for term in rows_c]), *[col_wide] * 4)
    g_value = g_value[:in_rows]
    return (
        logits,
        d_bytes,
        g_lat,
        jnp.stack([g_col0, g_up0, g_q, g_k, g_v, g_up1]),
        jnp.stack([g_out0, g_out1]),
        jnp.stack([g_down0, g_down1]),
        jnp.stack([g_key, g_value]),
        jnp.stack([g_dk, g_dv]),
        g_xq.T,
        jnp.stack([g_sq[:, :wide_in], g_sq[:, wide_in : 2 * wide_in]]),
        g_sq[:, 2 * wide_in :],
        g_gains,
        g_mask,
        g_byte_gain,
    )


def solution(mesh):
    return jax.shard_map(
        functools.partial(per_device, mesh.shape["dp"], mesh.shape["mp"]),
        mesh=mesh,
        in_specs=(
            P("dp", "mp", None),
            P("dp"),
            P("dp", None),
            P("dp", None),
            P("mp", "dp"),
            P(None, "dp", "mp"),
            P(None, "dp", "mp"),
            P(None, "dp", "mp"),
            P(None, "dp", "mp"),
            P(None, "dp", "mp"),
            P("mp", "dp"),
            P(None, ("dp", "mp"), None),
            P(("dp", "mp"), None),
            P(None, ("dp", "mp")),
            P(("dp", "mp")),
            P(("dp", "mp")),
            P("dp", "mp", None),
        ),
        out_specs=(
            P("dp", "mp", None),
            P("dp", "mp", None),
            P("mp", "dp"),
            P(None, "dp", "mp"),
            P(None, "dp", "mp"),
            P(None, "dp", "mp"),
            P(None, "dp", "mp"),
            P(None, "dp", "mp"),
            P("mp", "dp"),
            P(None, ("dp", "mp"), None),
            P(("dp", "mp"), None),
            P(None, ("dp", "mp")),
            P(("dp", "mp")),
            P(("dp", "mp")),
        ),
        check_vma=False,
    )
```

time: 3600 us -> 863 us (0.24)
  the two profiles are of different devices: /device:TPU:11 before, /device:TPU:0 now
where the time goes in v1:
time: 863 us; the launch traced here: 852 us
  waiting for transfers between devices  287 us (33%)
  local copies, waits for them, and re-layouts  234 us (27%)
  matrix products  143 us (17%)
  starting transfers between devices  89.6 us (10%)
  other arithmetic  75.5 us (9%)
  between operations  22.2 us (3%)
    ppermute x51, waiting for transfers between devices, send(): return lax.ppermute(value, 'mp', pairs)  225 us
    ppermute x51, starting transfers between devices, send(): return lax.ppermute(value, 'mp', pairs)  71.1 us
    concatenate x10, local copies, waits for them, and re-layouts, beside(): return jnp.concatenate([part.reshape(dn * size, wide) for part in parts], 1)  65.7 us
    unnamed x366, local copies, waits for them, and re-layouts  53.4 us
    dot_general x19, matrix products, dot_tn(): lax.dot_general(left, right, (((0,), (0,)), ((), ())), preferred_element_...  39.6 us
    dot_general x19, matrix products, dot_t(): lax.dot_general(left, right, (((left.ndim - 1,), (right.ndim - 1,)), ((),...  37 us
    dot_general x19, matrix products, dot(): return jnp.dot(left, right, preferred_element_type=F32)  36.1 us
    slice x5, local copies, waits for them, and re-layouts, beside(): parts = [got[:, m, row:row + size, col:col + wide] for m in range(mn)]  35.9 us
  transfers between devices with their start and end apart: 75, of which 42 were waited for; matrix products, arithmetic and copies ran while one was open for 39% of the time, Pallas kernels for 0%

profile of v1, /device:TPU:0, one launch (start us, length us, event | category | flops | bytes accessed | tf_op | source)
XLA Modules:
  0.0 851.5 jit_solution(7755780255259398296)
XLA Ops:
  27.9 9.1 %collective-permute-done.4 = bf16[272,480]{1,0:T(8,128)(2,1)S(1)} collective-permute-done((bf16[272,480]{1,0:T(8,128)(2,1)}, bf16[272,480]{1,0:T(8,128)(2,1)S(1)}, u32[]{:S(2)}, u32[]{:S(2)}) %collective-permute-start.4) | collective-permute-done | bytes 261152 | tf_op jit(solution)/shard_map/ppermute | solution.py:129
  67.9 12.1 %collective-permute-done.11 = bf16[64,768]{1,0:T(8,128)(2,1)S(1)} collective-permute-done((bf16[64,768]{1,0:T(8,128)(2,1)S(1)}, bf16[64,768]{1,0:T(8,128)(2,1)S(1)}, u32[]{:S(2)}, u32[]{:S(2)}) %collective-permute-start.11) | collective-permute-done | bytes 98336 | tf_op jit(solution)/shard_map/ppermute | solution.py:128
  85.6 7.9 collective-permute-done.13
  94.1 7.5 collective-permute-done.14
  109.9 4.6 collective-permute-start.17
  119.7 19.6 %collective-permute-done.16 = bf16[256,768]{1,0:T(8,128)(2,1)S(1)} collective-permute-done((bf16[256,768]{1,0:T(8,128)(2,1)S(1)}, bf16[256,768]{1,0:T(8,128)(2,1)S(1)}, u32[]{:S(2)}, u32[]{:S(2)}) %collective-permute-start.16) | collective-permute-done | bytes 393248 | tf_op jit(solution)/shard_map/ppermute | solution.py:128
  139.5 6.6 collective-permute-start.20
  146.1 20.0 %collective-permute-done.20 = bf16[256,768]{1,0:T(8,128)(2,1)S(1)} collective-permute-done((bf16[256,768]{1,0:T(8,128)(2,1)S(1)}, bf16[256,768]{1,0:T(8,128)(2,1)S(1)}, u32[]{:S(2)}, u32[]{:S(2)}) %collective-permute-start.20) | collective-permute-done | bytes 393248 | tf_op jit(solution)/shard_map/ppermute | solution.py:128
  166.3 10.9 %collective-permute-start.21 = (bf16[256,768]{1,0:T(8,128)(2,1)S(1)}, bf16[256,768]{1,0:T(8,128)(2,1)S(1)}, u32[]{:S(2)}, u32[]{:S(2)}) collective-permute-start(bf16[256,768]{1,0:T(8,128)(2,1)S(1)} %fusion.85), channel_id=1, source_target_pairs={{0,1},{1,2},{2,3},{3,0},{4,5},{5,6},{6,7},{7,4},{8,9},{9,10},{10,1... | collective-permute-start | bytes 1179656 | tf_op jit(solution)/shard_map/ppermute | solution.py:128
  178.0 16.5 %collective-permute-done.21 = bf16[256,768]{1,0:T(8,128)(2,1)S(1)} collective-permute-done((bf16[256,768]{1,0:T(8,128)(2,1)S(1)}, bf16[256,768]{1,0:T(8,128)(2,1)S(1)}, u32[]{:S(2)}, u32[]{:S(2)}) %collective-permute-start.21) | collective-permute-done | bytes 393248 | tf_op jit(solution)/shard_map/ppermute | solution.py:128
  197.0 18.5 %all-gather.3.cloned.1.call-done = bf16[20480,640]{1,0:T(8,128)(2,1)} async-done(((bf16[640,640]{1,0:T(8,128)(2,1)}), bf16[20480,640]{1,0:T(8,128)(2,1)}) %all-gather.3.cloned.1.call-update) | async-done | bytes 26214416 | tf_op jit(solution)/shard_map/all_gather | solution.py:271
  233.5 25.4 %collective-permute-done.26 = bf16[262,512]{1,0:T(8,128)(2,1)S(1)} collective-permute-done((bf16[262,512]{1,0:T(8,128)(2,1)S(1)}, bf16[262,512]{1,0:T(8,128)(2,1)S(1)}, u32[]{:S(2)}, u32[]{:S(2)}) %collective-permute-start.26) | collective-permute-done | bytes 268320 | tf_op jit(solution)/shard_map/ppermute | solution.py:128
  273.2 4.3 concatenate.169
  277.6 6.5 fusion.185
  284.0 12.4 %fusion.184 = (bf16[8,1,160,320]{3,2,1,0:T(8,128)(2,1)}, bf16[8,1,160,320]{3,2,1,0:T(8,128)(2,1)}, bf16[8,1,160,320]{3,2,1,0:T(8,128)(2,1)}, bf16[8,1,160,320]{3...) fusion(bf16[8,4,640,640]{3,2,1,0:T(8,128)(2,1)} %bitcast.423), kind=kLoop, calls=%fused_computation.620 | loop fusion | bytes 31129600 | tf_op jit(solution)/shard_map/slice | solution.py:279
  296.4 7.1 concatenate.172
  303.6 6.8 concatenate.171
  310.3 6.6 concatenate.170
  316.9 6.9 concatenate.175
  329.7 4.7 fusion.31
  341.0 6.7 concatenate.174
  353.9 6.8 concatenate.173
  366.8 6.7 concatenate.176
  392.0 6.2 fusion.188
  398.3 6.7 fusion.190
  412.4 6.7 concatenate.181
  419.1 4.5 fusion.175
  423.6 7.1 concatenate.182
  430.8 6.6 fusion.201
  507.5 5.7 fusion.5
  566.6 6.3 pad_maximum_fusion
  584.9 4.7 collective-permute-done.36
  589.8 6.9 collective-permute-done.29
  599.7 8.5 collective-permute-done.30
  635.1 5.0 collective-permute-done.41
  652.1 4.5 collective-permute-done.44
  664.2 5.3 collective-permute-done.47
  669.7 5.4 multiply_reduce_fusion.1
  680.0 5.0 collective-permute-done.52
  691.5 5.3 collective-permute-done.50
  717.7 12.6 %collective-permute-done.55 = bf16[160,2304]{1,0:T(8,128)(2,1)S(1)} collective-permute-done((bf16[160,2304]{1,0:T(8,128)(2,1)S(1)}, bf16[160,2304]{1,0:T(8,128)(2,1)S(1)}, u32[]{:S(2)}, u32[]{:S(2)}) %collective-permute-start.55) | collective-permute-done | bytes 737312 | tf_op jit(solution)/shard_map/ppermute | solution.py:128
  741.1 7.9 collective-permute-done.56
  751.4 4.3 collective-permute-start.68
  757.4 12.9 %collective-permute-done.69 = f32[62,128]{1,0:T(8,128)S(1)} collective-permute-done((f32[62,128]{1,0:T(8,128)S(1)}, f32[62,128]{1,0:T(8,128)S(1)}, u32[]{:S(2)}, u32[]{:S(2)}) %collective-permute-start.69) | collective-permute-done | bytes 31776 | tf_op jit(solution)/shard_map/ppermute | solution.py:128
  778.2 10.1 %reduce-scatter.4.cloned.1.call-done = bf16[160,5120]{1,0:T(8,128)(2,1)} async-done(((bf16[1280,5120]{1,0:T(8,128)(2,1)}), bf16[160,5120]{1,0:T(8,128)(2,1)}) %reduce-scatter.4.cloned.1.call-update) | async-done | bytes 1638416 | tf_op jit(solution)/shard_map/reduce_scatter | solution.py:464
  800.6 10.0 %collective-permute-done.62 = bf16[96,512]{1,0:T(8,128)(2,1)S(1)} collective-permute-done((bf16[96,512]{1,0:T(8,128)(2,1)S(1)}, bf16[96,512]{1,0:T(8,128)(2,1)S(1)}, u32[]{:S(2)}, u32[]{:S(2)}) %collective-permute-start.62) | collective-permute-done | bytes 98336 | tf_op jit(solution)/shard_map/ppermute | solution.py:128
  820.8 6.2 collective-permute-done.59
  830.1 10.3 %collective-permute-done.60 = bf16[160,1280]{1,0:T(8,128)(2,1)} collective-permute-done((bf16[160,1280]{1,0:T(8,128)(2,1)}, bf16[160,1280]{1,0:T(8,128)(2,1)}, u32[]{:S(2)}, u32[]{:S(2)}) %collective-permute-start.60) | collective-permute-done | bytes 409632 | tf_op jit(solution)/shard_map/ppermute | solution.py:128
  (817 shorter events, 420.5 us)
Async XLA Ops:
  7.2 208.3 %all-gather.3.cloned.1.call-start = ((), (), s32[]{:S(2)}) async-start(), calls=%async_computation.3 | async-start | bytes 27033600 | tf_op jit(solution)/shard_map/all_gather | solution.py:271
  11.8 373.9 %all-gather.5.cloned.1.call-start = ((), (), s32[]{:S(2)}) async-start(), calls=%async_computation.4 | async-start | bytes 18382848 | tf_op jit(solution)/shard_map/all_gather | solution.py:271
  23.6 13.4 %collective-permute-start.4 = (bf16[272,480]{1,0:T(8,128)(2,1)}, bf16[272,480]{1,0:T(8,128)(2,1)S(1)}, u32[]{:S(2)}, u32[]{:S(2)}) collective-permute-start(bf16[272,480]{1,0:T(8,128)(2,1)} %get-tuple-element.44), channel_id=1, source_target_pairs={{0,8},{4,12},{8,0},{12,4},{16,24},{20,28},{24,16},{28,20},{1,9},{5... | collective-permute-start | bytes 783368 | tf_op jit(solution)/shard_map/ppermute | solution.py:129
  25.1 13.9 %collective-permute-start.3 = (bf16[272,480]{1,0:T(8,128)(2,1)}, bf16[272,480]{1,0:T(8,128)(2,1)}, u32[]{:S(2)}, u32[]{:S(2)}) collective-permute-start(bf16[272,480]{1,0:T(8,128)(2,1)} %get-tuple-element.44), channel_id=1, source_target_pairs={{0,4},{4,0},{8,12},{12,8},{16,20},{20,16},{24,28},{28,24},{1,5},{5... | collective-permute-start | bytes 783368 | tf_op jit(solution)/shard_map/ppermute | solution.py:129
  25.1 13.3 %collective-permute-start.6 = (bf16[272,480]{1,0:T(8,128)(2,1)}, bf16[272,480]{1,0:T(8,128)(2,1)S(1)}, u32[]{:S(2)}, u32[]{:S(2)}) collective-permute-start(bf16[272,480]{1,0:T(8,128)(2,1)} %get-tuple-element.44), channel_id=1, source_target_pairs={{0,16},{4,20},{8,24},{12,28},{16,0},{20,4},{24,8},{28,12},{1,17},{... | collective-permute-start | bytes 783368 | tf_op jit(solution)/shard_map/ppermute | solution.py:129
  55.0 9.6 %collective-permute-start.10 = (bf16[64,768]{1,0:T(8,128)(2,1)S(1)}, bf16[64,768]{1,0:T(8,128)(2,1)S(1)}, u32[]{:S(2)}, u32[]{:S(2)}) collective-permute-start(bf16[64,768]{1,0:T(8,128)(2,1)S(1)} %get-tuple-element.172), channel_id=1, source_target_pairs={{0,1},{1,2},{2,3},{3,0},{4,5},{5,6},{6,7},{7,4},{8,9},{9,10},{10,1... | collective-permute-start | bytes 294920 | tf_op jit(solution)/shard_map/ppermute | solution.py:128
  56.5 11.4 %collective-permute-start.12 = (bf16[64,768]{1,0:T(8,128)(2,1)S(1)}, bf16[64,768]{1,0:T(8,128)(2,1)S(1)}, u32[]{:S(2)}, u32[]{:S(2)}) collective-permute-start(bf16[64,768]{1,0:T(8,128)(2,1)S(1)} %get-tuple-element.173), channel_id=1, source_target_pairs={{0,3},{1,0},{2,1},{3,2},{4,7},{5,4},{6,5},{7,6},{8,11},{9,8},{10,9... | collective-permute-start | bytes 294920 | tf_op jit(solution)/shard_map/ppermute | solution.py:128
  58.8 21.2 %collective-permute-start.11 = (bf16[64,768]{1,0:T(8,128)(2,1)S(1)}, bf16[64,768]{1,0:T(8,128)(2,1)S(1)}, u32[]{:S(2)}, u32[]{:S(2)}) collective-permute-start(bf16[64,768]{1,0:T(8,128)(2,1)S(1)} %get-tuple-element.174), channel_id=1, source_target_pairs={{0,2},{1,3},{2,0},{3,1},{4,6},{5,7},{6,4},{7,5},{8,10},{9,11},{10,... | collective-permute-start | bytes 294920 | tf_op jit(solution)/shard_map/ppermute | solution.py:128
  80.7 12.7 %collective-permute-start.13 = (bf16[64,768]{1,0:T(8,128)(2,1)}, bf16[64,768]{1,0:T(8,128)(2,1)S(1)}, u32[]{:S(2)}, u32[]{:S(2)}) collective-permute-start(bf16[64,768]{1,0:T(8,128)(2,1)} %get-tuple-element.42), channel_id=1, source_target_pairs={{0,3},{1,0},{2,1},{3,2},{4,7},{5,4},{6,5},{7,6},{8,11},{9,8},{10,9... | collective-permute-start | bytes 294920 | tf_op jit(solution)/shard_map/ppermute | solution.py:128
  83.8 18.4 %collective-permute-start.15 = (bf16[64,768]{1,0:T(8,128)(2,1)}, bf16[64,768]{1,0:T(8,128)(2,1)S(1)}, u32[]{:S(2)}, u32[]{:S(2)}) collective-permute-start(bf16[64,768]{1,0:T(8,128)(2,1)} %get-tuple-element.42), channel_id=1, source_target_pairs={{0,1},{1,2},{2,3},{3,0},{4,5},{5,6},{6,7},{7,4},{8,9},{9,10},{10,1... | collective-permute-start | bytes 294920 | tf_op jit(solution)/shard_map/ppermute | solution.py:128
  85.6 16.1 %collective-permute-start.14 = (bf16[64,768]{1,0:T(8,128)(2,1)}, bf16[64,768]{1,0:T(8,128)(2,1)S(1)}, u32[]{:S(2)}, u32[]{:S(2)}) collective-permute-start(bf16[64,768]{1,0:T(8,128)(2,1)} %get-tuple-element.42), channel_id=1, source_target_pairs={{0,2},{1,3},{2,0},{3,1},{4,6},{5,7},{6,4},{7,5},{8,10},{9,11},{10,... | collective-permute-start | bytes 294920 | tf_op jit(solution)/shard_map/ppermute | solution.py:128
  109.8 9.7 %collective-permute-start.18 = (f32[2,4,256]{2,1,0:T(4,128)S(1)}, f32[2,4,256]{2,1,0:T(4,128)S(1)}, u32[]{:S(2)}, u32[]{:S(2)}) collective-permute-start(f32[2,4,256]{2,1,0:T(4,128)S(1)} %get-tuple-element.227), channel_id=1, source_target_pairs={{0,2},{1,3},{2,0},{3,1},{4,6},{5,7},{6,4},{7,5},{8,10},{9,11},{10,... | collective-permute-start | bytes 24584 | tf_op jit(solution)/shard_map/ppermute | solution.py:128
  109.9 9.7 %collective-permute-start.17 = (f32[2,4,256]{2,1,0:T(4,128)S(1)}, f32[2,4,256]{2,1,0:T(4,128)S(1)}, u32[]{:S(2)}, u32[]{:S(2)}) collective-permute-start(f32[2,4,256]{2,1,0:T(4,128)S(1)} %get-tuple-element.227), channel_id=1, source_target_pairs={{0,1},{1,2},{2,3},{3,0},{4,5},{5,6},{6,7},{7,4},{8,9},{9,10},{10,1... | collective-permute-start | bytes 24584 | tf_op jit(solution)/shard_map/ppermute | solution.py:128
  117.5 21.8 %collective-permute-start.16 = (bf16[256,768]{1,0:T(8,128)(2,1)S(1)}, bf16[256,768]{1,0:T(8,128)(2,1)S(1)}, u32[]{:S(2)}, u32[]{:S(2)}) collective-permute-start(bf16[256,768]{1,0:T(8,128)(2,1)S(1)} %dynamic-slice_bitcast_fusion), channel_id=1, source_target_pairs={{0,1},{1,2},{2,3},{3,0},{4,5},{5,6},{6,7},{7,4},{8,9},{9,10},{10,1... | collective-permute-start | bytes 1179656 | tf_op jit(solution)/shard_map/ppermute | solution.py:128
  139.5 26.6 %collective-permute-start.20 = (bf16[256,768]{1,0:T(8,128)(2,1)S(1)}, bf16[256,768]{1,0:T(8,128)(2,1)S(1)}, u32[]{:S(2)}, u32[]{:S(2)}) collective-permute-start(bf16[256,768]{1,0:T(8,128)(2,1)S(1)} %fusion.87), channel_id=1, source_target_pairs={{0,1},{1,2},{2,3},{3,0},{4,5},{5,6},{6,7},{7,4},{8,9},{9,10},{10,1... | collective-permute-start | bytes 1179656 | tf_op jit(solution)/shard_map/ppermute | solution.py:128
  166.3 28.1 %collective-permute-start.21 = (bf16[256,768]{1,0:T(8,128)(2,1)S(1)}, bf16[256,768]{1,0:T(8,128)(2,1)S(1)}, u32[]{:S(2)}, u32[]{:S(2)}) collective-permute-start(bf16[256,768]{1,0:T(8,128)(2,1)S(1)} %fusion.85), channel_id=1, source_target_pairs={{0,1},{1,2},{2,3},{3,0},{4,5},{5,6},{6,7},{7,4},{8,9},{9,10},{10,1... | collective-permute-start | bytes 1179656 | tf_op jit(solution)/shard_map/ppermute | solution.py:128
  219.5 457.3 %reduce-scatter.8.cloned.1.call-start = ((), (), s32[]{:S(2)}) async-start(), calls=%async_computation.7 | async-start | bytes 6856704 | tf_op jit(solution)/shard_map/reduce_scatter | solution.py:464
  221.9 10.8 %collective-permute-start.25 = (bf16[262,512]{1,0:T(8,128)(2,1)S(1)}, bf16[262,512]{1,0:T(8,128)(2,1)S(1)}, u32[]{:S(2)}, u32[]{:S(2)}) collective-permute-start(bf16[262,512]{1,0:T(8,128)(2,1)S(1)} %bitcast.532), channel_id=1, source_target_pairs={{0,3},{1,0},{2,1},{3,2},{4,7},{5,4},{6,5},{7,6},{8,11},{9,8},{10,9... | collective-permute-start | bytes 804872 | tf_op jit(solution)/shard_map/ppermute | solution.py:128
  223.7 35.2 %collective-permute-start.26 = (bf16[262,512]{1,0:T(8,128)(2,1)S(1)}, bf16[262,512]{1,0:T(8,128)(2,1)S(1)}, u32[]{:S(2)}, u32[]{:S(2)}) collective-permute-start(bf16[262,512]{1,0:T(8,128)(2,1)S(1)} %bitcast.533), channel_id=1, source_target_pairs={{0,2},{1,3},{2,0},{3,1},{4,6},{5,7},{6,4},{7,5},{8,10},{9,11},{10,... | collective-permute-start | bytes 804872 | tf_op jit(solution)/shard_map/ppermute | solution.py:128
  223.8 35.9 %collective-permute-start.27 = (bf16[262,512]{1,0:T(8,128)(2,1)S(1)}, bf16[262,512]{1,0:T(8,128)(2,1)S(1)}, u32[]{:S(2)}, u32[]{:S(2)}) collective-permute-start(bf16[262,512]{1,0:T(8,128)(2,1)S(1)} %bitcast.534), channel_id=1, source_target_pairs={{0,1},{1,2},{2,3},{3,0},{4,5},{5,6},{6,7},{7,4},{8,9},{9,10},{10,1... | collective-permute-start | bytes 804872 | tf_op jit(solution)/shard_map/ppermute | solution.py:128
  470.6 228.5 %reduce-scatter.6.cloned.1.call-start = ((), (), s32[]{:S(2)}) async-start(), calls=%async_computation.6 | async-start | bytes 26542080 | tf_op jit(solution)/shard_map/reduce_scatter | solution.py:464
  524.9 263.4 %reduce-scatter.4.cloned.1.call-start = ((), (), s32[]{:S(2)}) async-start(), calls=%async_computation.5 | async-start | bytes 14745600 | tf_op jit(solution)/shard_map/reduce_scatter | solution.py:464
  538.5 37.6 %collective-permute-start.24 = (bf16[262,512]{1,0:T(8,128)(2,1)}, bf16[262,512]{1,0:T(8,128)(2,1)S(1)}, u32[]{:S(2)}, u32[]{:S(2)}) collective-permute-start(bf16[262,512]{1,0:T(8,128)(2,1)} %get-tuple-element.114), channel_id=1, source_target_pairs={{0,1},{1,2},{2,3},{3,0},{4,5},{5,6},{6,7},{7,4},{8,9},{9,10},{10,1... | collective-permute-start | bytes 804872 | tf_op jit(solution)/shard_map/ppermute | solution.py:128
  538.5 36.8 %collective-permute-start.23 = (bf16[262,512]{1,0:T(8,128)(2,1)}, bf16[262,512]{1,0:T(8,128)(2,1)S(1)}, u32[]{:S(2)}, u32[]{:S(2)}) collective-permute-start(bf16[262,512]{1,0:T(8,128)(2,1)} %get-tuple-element.116), channel_id=1, source_target_pairs={{0,2},{1,3},{2,0},{3,1},{4,6},{5,7},{6,4},{7,5},{8,10},{9,11},{10,... | collective-permute-start | bytes 804872 | tf_op jit(solution)/shard_map/ppermute | solution.py:128
  541.5 33.1 %collective-permute-start.22 = (bf16[262,512]{1,0:T(8,128)(2,1)}, bf16[262,512]{1,0:T(8,128)(2,1)S(1)}, u32[]{:S(2)}, u32[]{:S(2)}) collective-permute-start(bf16[262,512]{1,0:T(8,128)(2,1)} %get-tuple-element.117), channel_id=1, source_target_pairs={{0,3},{1,0},{2,1},{3,2},{4,7},{5,4},{6,5},{7,6},{8,11},{9,8},{10,9... | collective-permute-start | bytes 804872 | tf_op jit(solution)/shard_map/ppermute | solution.py:128
  555.4 17.5 %collective-permute-start.34 = (bf16[64,1280]{1,0:T(8,128)(2,1)}, bf16[64,1280]{1,0:T(8,128)(2,1)}, u32[]{:S(2)}, u32[]{:S(2)}) collective-permute-start(bf16[64,1280]{1,0:T(8,128)(2,1)} %constant_dynamic-slice_fusion.65), channel_id=1, source_target_pairs={{0,1},{1,2},{2,3},{3,0},{4,5},{5,6},{6,7},{7,4},{8,9},{9,10},{10,1... | collective-permute-start | bytes 491528 | tf_op jit(solution)/shard_map/ppermute | solution.py:128
  561.6 22.7 %collective-permute-start.28 = (bf16[256,768]{1,0:T(8,128)(2,1)S(1)}, bf16[256,768]{1,0:T(8,128)(2,1)S(1)}, u32[]{:S(2)}, u32[]{:S(2)}) collective-permute-start(bf16[256,768]{1,0:T(8,128)(2,1)S(1)} %get-tuple-element.260), channel_id=1, source_target_pairs={{0,1},{1,2},{2,3},{3,0},{4,5},{5,6},{6,7},{7,4},{8,9},{9,10},{10,1... | collective-permute-start | bytes 1179656 | tf_op jit(solution)/shard_map/ppermute | solution.py:128
  581.1 8.5 %collective-permute-start.36 = (bf16[64,1280]{1,0:T(8,128)(2,1)S(1)}, bf16[64,1280]{1,0:T(8,128)(2,1)S(1)}, u32[]{:S(2)}, u32[]{:S(2)}) collective-permute-start(bf16[64,1280]{1,0:T(8,128)(2,1)S(1)} %add_convert_fusion.7), channel_id=1, source_target_pairs={{0,1},{1,2},{2,3},{3,0},{4,5},{5,6},{6,7},{7,4},{8,9},{9,10},{10,1... | collective-permute-start | bytes 491528 | tf_op jit(solution)/shard_map/ppermute | solution.py:128
  584.3 12.4 %collective-permute-start.29 = (bf16[256,768]{1,0:T(8,128)(2,1)S(1)}, bf16[256,768]{1,0:T(8,128)(2,1)S(1)}, u32[]{:S(2)}, u32[]{:S(2)}) collective-permute-start(bf16[256,768]{1,0:T(8,128)(2,1)S(1)} %collective-permute-done.28), channel_id=1, source_target_pairs={{0,1},{1,2},{2,3},{3,0},{4,5},{5,6},{6,7},{7,4},{8,9},{9,10},{10,1... | collective-permute-start | bytes 1179656 | tf_op jit(solution)/shard_map/ppermute | solution.py:128
  589.7 10.0 %collective-permute-start.37 = (bf16[64,640]{1,0:T(8,128)(2,1)S(1)}, bf16[64,640]{1,0:T(8,128)(2,1)S(1)}, u32[]{:S(2)}, u32[]{:S(2)}) collective-permute-start(bf16[64,640]{1,0:T(8,128)(2,1)S(1)} %select_convert_fusion.2), channel_id=1, source_target_pairs={{0,16},{4,20},{8,24},{12,28},{16,0},{20,4},{24,8},{28,12},{1,17},{... | collective-permute-start | bytes 245768 | tf_op jit(solution)/shard_map/ppermute | solution.py:129
  596.7 11.5 %collective-permute-start.30 = (bf16[256,768]{1,0:T(8,128)(2,1)S(1)}, bf16[256,768]{1,0:T(8,128)(2,1)S(1)}, u32[]{:S(2)}, u32[]{:S(2)}) collective-permute-start(bf16[256,768]{1,0:T(8,128)(2,1)S(1)} %collective-permute-done.29), channel_id=1, source_target_pairs={{0,1},{1,2},{2,3},{3,0},{4,5},{5,6},{6,7},{7,4},{8,9},{9,10},{10,1... | collective-permute-start | bytes 1179656 | tf_op jit(solution)/shard_map/ppermute | solution.py:128
  635.1 120.6 %collective-permute-start.39 = (bf16[64,160]{1,0:T(8,128)(2,1)}, bf16[64,160]{1,0:T(8,128)(2,1)}, u32[]{:S(2)}, u32[]{:S(2)}) collective-permute-start(bf16[64,160]{1,0:T(8,128)(2,1)} %select_convert_fusion.5), channel_id=1, source_target_pairs={{0,4},{4,0},{8,12},{12,8},{16,20},{20,16},{24,28},{28,24},{1,5},{5... | collective-permute-start | bytes 61448 | tf_op jit(solution)/shard_map/ppermute | solution.py:129
  680.0 8.3 collective-permute-start.49
  688.4 8.5 %collective-permute-start.50 = (bf16[64,1280]{1,0:T(8,128)(2,1)S(1)}, bf16[64,1280]{1,0:T(8,128)(2,1)S(1)}, u32[]{:S(2)}, u32[]{:S(2)}) collective-permute-start(bf16[64,1280]{1,0:T(8,128)(2,1)S(1)} %add_convert_fusion.6), channel_id=1, source_target_pairs={{0,1},{1,2},{2,3},{3,0},{4,5},{5,6},{6,7},{7,4},{8,9},{9,10},{10,1... | collective-permute-start | bytes 491528 | tf_op jit(solution)/shard_map/ppermute | solution.py:128
  697.6 15.6 %collective-permute-start.51 = (bf16[64,1280]{1,0:T(8,128)(2,1)}, bf16[64,1280]{1,0:T(8,128)(2,1)}, u32[]{:S(2)}, u32[]{:S(2)}) collective-permute-start(bf16[64,1280]{1,0:T(8,128)(2,1)} %add_convert_fusion.5), channel_id=1, source_target_pairs={{0,1},{1,2},{2,3},{3,0},{4,5},{5,6},{6,7},{7,4},{8,9},{9,10},{10,1... | collective-permute-start | bytes 491528 | tf_op jit(solution)/shard_map/ppermute | solution.py:128
  711.2 19.2 %collective-permute-start.55 = (bf16[160,2304]{1,0:T(8,128)(2,1)S(1)}, bf16[160,2304]{1,0:T(8,128)(2,1)S(1)}, u32[]{:S(2)}, u32[]{:S(2)}) collective-permute-start(bf16[160,2304]{1,0:T(8,128)(2,1)S(1)} %concatenate.197), channel_id=1, source_target_pairs={{0,1},{1,2},{2,3},{3,0},{4,5},{5,6},{6,7},{7,4},{8,9},{9,10},{10,1... | collective-permute-start | bytes 2211848 | tf_op jit(solution)/shard_map/ppermute | solution.py:128
  716.5 15.2 %collective-permute-start.64 = (f32[62,128]{1,0:T(8,128)}, f32[62,128]{1,0:T(8,128)}, u32[]{:S(2)}, u32[]{:S(2)}) collective-permute-start(f32[62,128]{1,0:T(8,128)} %maximum_bitcast_fusion), channel_id=1, source_target_pairs={{0,4},{4,0},{8,12},{12,8},{16,20},{20,16},{24,28},{28,24},{1,5},{5... | collective-permute-start | bytes 95240 | tf_op jit(solution)/shard_map/ppermute | solution.py:129
  730.6 18.4 %collective-permute-start.56 = (bf16[160,2304]{1,0:T(8,128)(2,1)S(1)}, bf16[160,2304]{1,0:T(8,128)(2,1)}, u32[]{:S(2)}, u32[]{:S(2)}) collective-permute-start(bf16[160,2304]{1,0:T(8,128)(2,1)S(1)} %add_convert_fusion.1), channel_id=1, source_target_pairs={{0,1},{1,2},{2,3},{3,0},{4,5},{5,6},{6,7},{7,4},{8,9},{9,10},{10,1... | collective-permute-start | bytes 2211848 | tf_op jit(solution)/shard_map/ppermute | solution.py:128
  737.9 13.4 %collective-permute-start.66 = (f32[62,128]{1,0:T(8,128)S(1)}, f32[62,128]{1,0:T(8,128)S(1)}, u32[]{:S(2)}, u32[]{:S(2)}) collective-permute-start(f32[62,128]{1,0:T(8,128)S(1)} %fusion.308), channel_id=1, source_target_pairs={{0,16},{4,20},{8,24},{12,28},{16,0},{20,4},{24,8},{28,12},{1,17},{... | collective-permute-start | bytes 95240 | tf_op jit(solution)/shard_map/ppermute | solution.py:129
  751.2 24.6 %collective-permute-start.57 = (bf16[160,2304]{1,0:T(8,128)(2,1)}, bf16[160,2304]{1,0:T(8,128)(2,1)}, u32[]{:S(2)}, u32[]{:S(2)}) collective-permute-start(bf16[160,2304]{1,0:T(8,128)(2,1)} %add_convert_fusion), channel_id=1, source_target_pairs={{0,1},{1,2},{2,3},{3,0},{4,5},{5,6},{6,7},{7,4},{8,9},{9,10},{10,1... | collective-permute-start | bytes 2211848 | tf_op jit(solution)/shard_map/ppermute | solution.py:128
  751.3 19.0 %collective-permute-start.69 = (f32[62,128]{1,0:T(8,128)S(1)}, f32[62,128]{1,0:T(8,128)S(1)}, u32[]{:S(2)}, u32[]{:S(2)}) collective-permute-start(f32[62,128]{1,0:T(8,128)S(1)} %add.905), channel_id=1, source_target_pairs={{0,1},{1,2},{2,3},{3,0},{4,5},{5,6},{6,7},{7,4},{8,9},{9,10},{10,1... | collective-permute-start | bytes 95240 | tf_op jit(solution)/shard_map/ppermute | solution.py:128
  751.4 19.6 %collective-permute-start.68 = (f32[62,128]{1,0:T(8,128)S(1)}, f32[62,128]{1,0:T(8,128)S(1)}, u32[]{:S(2)}, u32[]{:S(2)}) collective-permute-start(f32[62,128]{1,0:T(8,128)S(1)} %add.905), channel_id=1, source_target_pairs={{0,2},{1,3},{2,0},{3,1},{4,6},{5,7},{6,4},{7,5},{8,10},{9,11},{10,... | collective-permute-start | bytes 95240 | tf_op jit(solution)/shard_map/ppermute | solution.py:128
  755.7 15.3 %collective-permute-start.67 = (f32[62,128]{1,0:T(8,128)S(1)}, f32[62,128]{1,0:T(8,128)S(1)}, u32[]{:S(2)}, u32[]{:S(2)}) collective-permute-start(f32[62,128]{1,0:T(8,128)S(1)} %add.905), channel_id=1, source_target_pairs={{0,3},{1,0},{2,1},{3,2},{4,7},{5,4},{6,5},{7,6},{8,11},{9,8},{10,9... | collective-permute-start | bytes 95240 | tf_op jit(solution)/shard_map/ppermute | solution.py:128
  774.1 22.7 %collective-permute-start.61 = (bf16[96,512]{1,0:T(8,128)(2,1)}, bf16[96,512]{1,0:T(8,128)(2,1)}, u32[]{:S(2)}, u32[]{:S(2)}) collective-permute-start(bf16[96,512]{1,0:T(8,128)(2,1)} %constant_dynamic-slice_fusion.14), channel_id=1, source_target_pairs={{0,1},{1,2},{2,3},{3,0},{4,5},{5,6},{6,7},{7,4},{8,9},{9,10},{10,1... | collective-permute-start | bytes 294920 | tf_op jit(solution)/shard_map/ppermute | solution.py:128
  795.3 17.3 %collective-permute-start.58 = (bf16[160,1280]{1,0:T(8,128)(2,1)}, bf16[160,1280]{1,0:T(8,128)(2,1)}, u32[]{:S(2)}, u32[]{:S(2)}) collective-permute-start(bf16[160,1280]{1,0:T(8,128)(2,1)} %concatenate.201), channel_id=1, source_target_pairs={{0,1},{1,2},{2,3},{3,0},{4,5},{5,6},{6,7},{7,4},{8,9},{9,10},{10,1... | collective-permute-start | bytes 1228808 | tf_op jit(solution)/shard_map/ppermute | solution.py:128
  797.7 12.9 %collective-permute-start.62 = (bf16[96,512]{1,0:T(8,128)(2,1)S(1)}, bf16[96,512]{1,0:T(8,128)(2,1)S(1)}, u32[]{:S(2)}, u32[]{:S(2)}) collective-permute-start(bf16[96,512]{1,0:T(8,128)(2,1)S(1)} %add_convert_fusion.10), channel_id=1, source_target_pairs={{0,1},{1,2},{2,3},{3,0},{4,5},{5,6},{6,7},{7,4},{8,9},{9,10},{10,1... | collective-permute-start | bytes 294920 | tf_op jit(solution)/shard_map/ppermute | solution.py:128
  814.4 12.6 %collective-permute-start.59 = (bf16[160,1280]{1,0:T(8,128)(2,1)}, bf16[160,1280]{1,0:T(8,128)(2,1)}, u32[]{:S(2)}, u32[]{:S(2)}) collective-permute-start(bf16[160,1280]{1,0:T(8,128)(2,1)} %add_convert_fusion.4), channel_id=1, source_target_pairs={{0,1},{1,2},{2,3},{3,0},{4,5},{5,6},{6,7},{7,4},{8,9},{9,10},{10,1... | collective-permute-start | bytes 1228808 | tf_op jit(solution)/shard_map/ppermute | solution.py:128
  828.8 11.6 %collective-permute-start.60 = (bf16[160,1280]{1,0:T(8,128)(2,1)}, bf16[160,1280]{1,0:T(8,128)(2,1)}, u32[]{:S(2)}, u32[]{:S(2)}) collective-permute-start(bf16[160,1280]{1,0:T(8,128)(2,1)} %add_convert_fusion.3), channel_id=1, source_target_pairs={{0,1},{1,2},{2,3},{3,0},{4,5},{5,6},{6,7},{7,4},{8,9},{9,10},{10,1... | collective-permute-start | bytes 1228808 | tf_op jit(solution)/shard_map/ppermute | solution.py:128
  (186 other events, 1374.2 us)
Sparse Core Ops, SparseCore 0:
  11.9 203.4 all-gather.2
  219.7 134.8 all-gather.4
  470.7 60.5 reduce-scatter.7
  534.8 153.6 reduce-scatter.5
  692.3 95.8 reduce-scatter.3

commit v2 on v1

--- a/solution.py
+++ b/solution.py
@@ -156,6 +156,10 @@
             total = (got.astype(F32) + block(t).astype(F32)).astype(BF)
         (got,) = yield [("z", 1, total)]
         return got.astype(F32) + block(0).astype(F32)
+
+    def sum_split(self, block):
+        got = yield [("z", t, block(self.mn - t).astype(BF)) for t in range(1, self.mn)]
+        return block(0).astype(F32) + sum(part.astype(F32) for part in got)
 
     def sum_mp(self, value):
         got = yield from self.direct([value] * self.mn)
@@ -381,11 +385,6 @@
 
     assert mn > 2
     mix, share = links.free(mix_task(mix, top, below))
-    def cot_task():
-        parts = [lax.dynamic_index_in_dim(cot, (z + t) % mn % items, 0, False) for t in range(mn)]
-        parts = yield from links.direct(parts)
-        return (links.natural_columns(parts).astype(F32) * (masked_item / repeat)[None, :]).astype(BF)
-
     w_out0, w_up0, w_down0, w_q, w_k, w_v, w_out1 = (first_weight(k) for k in range(7))
     w_value = beside(w_one, at_one[3], col_wide, in_rows, col_wide)
     late_parts[0] = late_parts[0] + (nothing_of(w_one[0, 0]) + nothing_of(mix)).astype(BF)
@@ -394,6 +393,12 @@
         late_wide,
     )
 
+
+    def cot_task():
+        held = cot + nothing_of(w_two[0, 0]).astype(BF)
+        parts = [lax.dynamic_index_in_dim(held, (z + t) % mn % items, 0, False) for t in range(mn)]
+        parts = yield from links.direct(parts)
+        return (links.natural_columns(parts).astype(F32) * (masked_item / repeat)[None, :]).astype(BF)
 
     attended = dot(mix, w_value).astype(BF)
     first = lat + dot_t(attended, w_out0)
@@ -468,6 +473,11 @@
             edge += term.shape[1]
         return ready, out
 
+    def last_columns(terms):
+        return links.free(
+            links.sum_split(lambda t: jnp.concatenate([by_own_columns(v, t) for v in terms], 1))
+        )
+
     def columns(terms):
         return links.free(
             links.sum_ring(lambda t: jnp.concatenate([by_own_columns(v, t) for v in terms], 1))
@@ -600,7 +610,7 @@
         g_b, *([deck_wide] * 2 + [col_wide] * 6)
     )
     after = nothing_of(g_b).astype(BF)
-    g_up0, g_down0, g_out0, g_value = split(columns([term + after for term in rows_c]), *[col_wide] * 4)
+    g_up0, g_down0, g_out0, g_value = split(last_columns([term + after for term in rows_c]), *[col_wide] * 4)
     g_value = g_value[:in_rows]
     return (
         logits,

time: 863 us -> 843 us (0.977)
  the two profiles are of different devices: /device:TPU:0 before, /device:TPU:11 now
where the time goes in v2:
time: 843 us; the launch traced here: 832 us
  waiting for transfers between devices  247 us (29%)
  local copies, waits for them, and re-layouts  230 us (27%)
  matrix products  151 us (18%)
  starting transfers between devices  112 us (13%)
  other arithmetic  68.1 us (8%)
  between operations  23.1 us (3%)
    ppermute x51, waiting for transfers between devices, send(): return lax.ppermute(value, 'mp', pairs)  204 us
    ppermute x51, starting transfers between devices, send(): return lax.ppermute(value, 'mp', pairs)  81.3 us
    concatenate x10, local copies, waits for them, and re-layouts, beside(): return jnp.concatenate([part.reshape(dn * size, wide) for part in parts], 1)  65.6 us
    unnamed x405, local copies, waits for them, and re-layouts  49.9 us
    dot_general x19, matrix products, dot(): return jnp.dot(left, right, preferred_element_type=F32)  48 us
    dot_general x19, matrix products, dot_tn(): lax.dot_general(left, right, (((0,), (0,)), ((), ())), preferred_element_...  38.2 us
    slice x5, local copies, waits for them, and re-layouts, beside(): parts = [got[:, m, row:row + size, col:col + wide] for m in range(mn)]  36 us
    dot_general x19, matrix products, dot_t(): lax.dot_general(left, right, (((left.ndim - 1,), (right.ndim - 1,)), ((),...  35.4 us
  transfers between devices with their start and end apart: 75, of which 40 were waited for; matrix products, arithmetic and copies ran while one was open for 43% of the time, Pallas kernels for 0%

profile of v2, /device:TPU:11, one launch (start us, length us, event | category | flops | bytes accessed | tf_op | source)
XLA Modules:
  0.0 831.8 jit_solution(5654879603759190234)
XLA Ops:
  24.6 6.9 collective-permute-done.4
  61.5 5.3 collective-permute-done.12
  66.8 6.1 collective-permute-done.11
  73.7 4.5 collective-permute-start.13
  81.0 4.0 collective-permute-start.14
  85.6 13.5 %collective-permute-done.14 = bf16[64,768]{1,0:T(8,128)(2,1)S(1)} collective-permute-done((bf16[64,768]{1,0:T(8,128)(2,1)}, bf16[64,768]{1,0:T(8,128)(2,1)S(1)}, u32[]{:S(2)}, u32[]{:S(2)}) %collective-permute-start.14) | collective-permute-done | bytes 98336 | tf_op jit(solution)/shard_map/ppermute | solution.py:128
  115.7 22.4 %collective-permute-done.16 = bf16[256,768]{1,0:T(8,128)(2,1)S(1)} collective-permute-done((bf16[256,768]{1,0:T(8,128)(2,1)S(1)}, bf16[256,768]{1,0:T(8,128)(2,1)S(1)}, u32[]{:S(2)}, u32[]{:S(2)}) %collective-permute-start.16) | collective-permute-done | bytes 393248 | tf_op jit(solution)/shard_map/ppermute | solution.py:128
  142.1 21.9 %collective-permute-done.20 = bf16[256,768]{1,0:T(8,128)(2,1)S(1)} collective-permute-done((bf16[256,768]{1,0:T(8,128)(2,1)S(1)}, bf16[256,768]{1,0:T(8,128)(2,1)S(1)}, u32[]{:S(2)}, u32[]{:S(2)}) %collective-permute-start.20) | collective-permute-done | bytes 393248 | tf_op jit(solution)/shard_map/ppermute | solution.py:128
  164.2 7.2 collective-permute-start.21
  172.2 24.5 %collective-permute-done.21 = bf16[256,768]{1,0:T(8,128)(2,1)S(1)} collective-permute-done((bf16[256,768]{1,0:T(8,128)(2,1)S(1)}, bf16[256,768]{1,0:T(8,128)(2,1)S(1)}, u32[]{:S(2)}, u32[]{:S(2)}) %collective-permute-start.21) | collective-permute-done | bytes 393248 | tf_op jit(solution)/shard_map/ppermute | solution.py:128
  199.2 13.4 %all-gather.3.cloned.1.call-done = bf16[20480,640]{1,0:T(8,128)(2,1)} async-done(((bf16[640,640]{1,0:T(8,128)(2,1)}), bf16[20480,640]{1,0:T(8,128)(2,1)}) %all-gather.3.cloned.1.call-update) | async-done | bytes 26214416 | tf_op jit(solution)/shard_map/all_gather | solution.py:275
  226.0 4.2 fusion.186
  230.2 4.3 concatenate.169
  234.5 6.5 fusion.185
  241.0 12.3 %fusion.184 = (bf16[8,1,160,320]{3,2,1,0:T(8,128)(2,1)}, bf16[8,1,160,320]{3,2,1,0:T(8,128)(2,1)}, bf16[8,1,160,320]{3,2,1,0:T(8,128)(2,1)}, bf16[8,1,160,320]{3...) fusion(bf16[8,4,640,640]{3,2,1,0:T(8,128)(2,1)} %bitcast.419), kind=kLoop, calls=%fused_computation.615 | loop fusion | bytes 31129600 | tf_op jit(solution)/shard_map/slice | solution.py:283
  253.4 6.8 concatenate.172
  260.1 6.7 concatenate.171
  266.9 6.5 concatenate.170
  273.4 6.8 concatenate.175
  286.8 16.4 %fusion.31 = (bf16[256,1280]{1,0:T(8,128)(2,1)S(1)}, f32[256,1280]{1,0:T(8,128)}) fusion(bf16[1280,1280]{1,0:T(8,128)(2,1)S(1)} %copy-done.40, f32[256,1280]{1,0:T(8,128)S(1)} %get-tuple-element.237, f32[1280]{0:T(1024)S(1)} %mul.784, f32[256]{0:T(256)S(1)} %add_rsqrt_fusion.4, f32[256]{0:T(256)S(1)} %broadcast_multiply_fusion.16), kind=kOutput, calls=%fused_computation.113 | convolution fusion | flops 861470720 | bytes 6560768 | tf_op jit(solution)/shard_map/dot_general | solution.py:15
  309.8 6.8 concatenate.174
  316.6 4.0 fusion.14
  323.0 7.1 concatenate.173
  330.1 4.0 convolution_convert_fusion.19
  336.2 6.8 concatenate.176
  356.8 4.0 fusion.188
  363.1 6.3 fusion.187
  369.4 6.6 fusion.189
  388.6 6.7 concatenate.181
  395.3 4.5 fusion.175
  399.8 7.1 concatenate.182
  406.9 6.6 fusion.200
  453.0 4.1 multiply_reduce_fusion.7
  488.2 5.5 fusion.5
  548.0 6.1 pad_maximum_fusion
  575.8 7.3 collective-permute-done.30
  606.8 4.7 collective-permute-start.40
  616.5 4.1 collective-permute-done.41
  639.1 5.8 collective-permute-done.47
  651.1 5.9 multiply_reduce_fusion.1
  677.1 4.2 collective-permute-start.64
  683.8 4.1 collective-permute-done.54
  717.2 8.2 collective-permute-done.67
  730.5 17.8 %collective-permute-done.61 = bf16[96,512]{1,0:T(8,128)(2,1)S(1)} collective-permute-done((bf16[96,512]{1,0:T(8,128)(2,1)S(1)}, bf16[96,512]{1,0:T(8,128)(2,1)S(1)}, u32[]{:S(2)}, u32[]{:S(2)}) %collective-permute-start.61) | collective-permute-done | bytes 98336 | tf_op jit(solution)/shard_map/ppermute | solution.py:128
  754.2 16.5 %collective-permute-done.63 = bf16[96,512]{1,0:T(8,128)(2,1)S(1)} collective-permute-done((bf16[96,512]{1,0:T(8,128)(2,1)S(1)}, bf16[96,512]{1,0:T(8,128)(2,1)S(1)}, u32[]{:S(2)}, u32[]{:S(2)}) %collective-permute-start.63) | collective-permute-done | bytes 98336 | tf_op jit(solution)/shard_map/ppermute | solution.py:128
  780.2 4.6 collective-permute-start.59
  789.2 23.2 %collective-permute-done.59 = bf16[160,1280]{1,0:T(8,128)(2,1)S(1)} collective-permute-done((bf16[160,1280]{1,0:T(8,128)(2,1)}, bf16[160,1280]{1,0:T(8,128)(2,1)S(1)}, u32[]{:S(2)}, u32[]{:S(2)}) %collective-permute-start.59) | collective-permute-done | bytes 409632 | tf_op jit(solution)/shard_map/ppermute | solution.py:128
  812.4 8.0 collective-permute-done.60
  (858 shorter events, 407.6 us)
Async XLA Ops:
  7.2 205.4 %all-gather.3.cloned.1.call-start = ((), (), s32[]{:S(2)}) async-start(), calls=%async_computation.3 | async-start | bytes 27033600 | tf_op jit(solution)/shard_map/all_gather | solution.py:275
  11.8 343.9 %all-gather.5.cloned.1.call-start = ((), (), s32[]{:S(2)}) async-start(), calls=%async_computation.4 | async-start | bytes 18382848 | tf_op jit(solution)/shard_map/all_gather | solution.py:275
  19.9 11.6 %collective-permute-start.4 = (bf16[272,480]{1,0:T(8,128)(2,1)}, bf16[272,480]{1,0:T(8,128)(2,1)S(1)}, u32[]{:S(2)}, u32[]{:S(2)}) collective-permute-start(bf16[272,480]{1,0:T(8,128)(2,1)} %get-tuple-element.44), channel_id=1, source_target_pairs={{0,8},{4,12},{8,0},{12,4},{16,24},{20,28},{24,16},{28,20},{1,9},{5... | collective-permute-start | bytes 783368 | tf_op jit(solution)/shard_map/ppermute | solution.py:129
  20.0 17.3 %collective-permute-start.3 = (bf16[272,480]{1,0:T(8,128)(2,1)}, bf16[272,480]{1,0:T(8,128)(2,1)}, u32[]{:S(2)}, u32[]{:S(2)}) collective-permute-start(bf16[272,480]{1,0:T(8,128)(2,1)} %get-tuple-element.44), channel_id=1, source_target_pairs={{0,4},{4,0},{8,12},{12,8},{16,20},{20,16},{24,28},{28,24},{1,5},{5... | collective-permute-start | bytes 783368 | tf_op jit(solution)/shard_map/ppermute | solution.py:129
  22.0 14.6 %collective-permute-start.6 = (bf16[272,480]{1,0:T(8,128)(2,1)}, bf16[272,480]{1,0:T(8,128)(2,1)S(1)}, u32[]{:S(2)}, u32[]{:S(2)}) collective-permute-start(bf16[272,480]{1,0:T(8,128)(2,1)} %get-tuple-element.44), channel_id=1, source_target_pairs={{0,16},{4,20},{8,24},{12,28},{16,0},{20,4},{24,8},{28,12},{1,17},{... | collective-permute-start | bytes 783368 | tf_op jit(solution)/shard_map/ppermute | solution.py:129
  31.5 9.9 %collective-permute-start.8 = (bf16[272,480]{1,0:T(8,128)(2,1)S(1)}, bf16[272,480]{1,0:T(8,128)(2,1)S(1)}, u32[]{:S(2)}, u32[]{:S(2)}) collective-permute-start(bf16[272,480]{1,0:T(8,128)(2,1)S(1)} %collective-permute-done.4), channel_id=1, source_target_pairs={{0,16},{4,20},{8,24},{12,28},{16,0},{20,4},{24,8},{28,12},{1,17},{... | collective-permute-start | bytes 783368 | tf_op jit(solution)/shard_map/ppermute | solution.py:129
  32.9 10.3 %collective-permute-start.5 = (bf16[272,480]{1,0:T(8,128)(2,1)S(1)}, bf16[272,480]{1,0:T(8,128)(2,1)S(1)}, u32[]{:S(2)}, u32[]{:S(2)}) collective-permute-start(bf16[272,480]{1,0:T(8,128)(2,1)S(1)} %collective-permute-done.4), channel_id=1, source_target_pairs={{0,4},{4,0},{8,12},{12,8},{16,20},{20,16},{24,28},{28,24},{1,5},{5... | collective-permute-start | bytes 783368 | tf_op jit(solution)/shard_map/ppermute | solution.py:129
  53.6 7.9 collective-permute-start.10
  54.6 12.2 %collective-permute-start.12 = (bf16[64,768]{1,0:T(8,128)(2,1)S(1)}, bf16[64,768]{1,0:T(8,128)(2,1)S(1)}, u32[]{:S(2)}, u32[]{:S(2)}) collective-permute-start(bf16[64,768]{1,0:T(8,128)(2,1)S(1)} %get-tuple-element.172), channel_id=1, source_target_pairs={{0,3},{1,0},{2,1},{3,2},{4,7},{5,4},{6,5},{7,6},{8,11},{9,8},{10,9... | collective-permute-start | bytes 294920 | tf_op jit(solution)/shard_map/ppermute | solution.py:128
  55.1 17.8 %collective-permute-start.11 = (bf16[64,768]{1,0:T(8,128)(2,1)S(1)}, bf16[64,768]{1,0:T(8,128)(2,1)S(1)}, u32[]{:S(2)}, u32[]{:S(2)}) collective-permute-start(bf16[64,768]{1,0:T(8,128)(2,1)S(1)} %get-tuple-element.173), channel_id=1, source_target_pairs={{0,2},{1,3},{2,0},{3,1},{4,6},{5,7},{6,4},{7,5},{8,10},{9,11},{10,... | collective-permute-start | bytes 294920 | tf_op jit(solution)/shard_map/ppermute | solution.py:128
  73.7 11.3 %collective-permute-start.13 = (bf16[64,768]{1,0:T(8,128)(2,1)}, bf16[64,768]{1,0:T(8,128)(2,1)S(1)}, u32[]{:S(2)}, u32[]{:S(2)}) collective-permute-start(bf16[64,768]{1,0:T(8,128)(2,1)} %get-tuple-element.42), channel_id=1, source_target_pairs={{0,3},{1,0},{2,1},{3,2},{4,7},{5,4},{6,5},{7,6},{8,11},{9,8},{10,9... | collective-permute-start | bytes 294920 | tf_op jit(solution)/shard_map/ppermute | solution.py:128
  80.7 19.0 %collective-permute-start.15 = (bf16[64,768]{1,0:T(8,128)(2,1)}, bf16[64,768]{1,0:T(8,128)(2,1)S(1)}, u32[]{:S(2)}, u32[]{:S(2)}) collective-permute-start(bf16[64,768]{1,0:T(8,128)(2,1)} %get-tuple-element.42), channel_id=1, source_target_pairs={{0,1},{1,2},{2,3},{3,0},{4,5},{5,6},{6,7},{7,4},{8,9},{9,10},{10,1... | collective-permute-start | bytes 294920 | tf_op jit(solution)/shard_map/ppermute | solution.py:128
  81.0 18.1 %collective-permute-start.14 = (bf16[64,768]{1,0:T(8,128)(2,1)}, bf16[64,768]{1,0:T(8,128)(2,1)S(1)}, u32[]{:S(2)}, u32[]{:S(2)}) collective-permute-start(bf16[64,768]{1,0:T(8,128)(2,1)} %get-tuple-element.42), channel_id=1, source_target_pairs={{0,2},{1,3},{2,0},{3,1},{4,6},{5,7},{6,4},{7,5},{8,10},{9,11},{10,... | collective-permute-start | bytes 294920 | tf_op jit(solution)/shard_map/ppermute | solution.py:128
  107.3 8.2 collective-permute-start.18
  115.4 22.6 %collective-permute-start.16 = (bf16[256,768]{1,0:T(8,128)(2,1)S(1)}, bf16[256,768]{1,0:T(8,128)(2,1)S(1)}, u32[]{:S(2)}, u32[]{:S(2)}) collective-permute-start(bf16[256,768]{1,0:T(8,128)(2,1)S(1)} %dynamic-slice_bitcast_fusion), channel_id=1, source_target_pairs={{0,1},{1,2},{2,3},{3,0},{4,5},{5,6},{6,7},{7,4},{8,9},{9,10},{10,1... | collective-permute-start | bytes 1179656 | tf_op jit(solution)/shard_map/ppermute | solution.py:128
  138.3 25.8 %collective-permute-start.20 = (bf16[256,768]{1,0:T(8,128)(2,1)S(1)}, bf16[256,768]{1,0:T(8,128)(2,1)S(1)}, u32[]{:S(2)}, u32[]{:S(2)}) collective-permute-start(bf16[256,768]{1,0:T(8,128)(2,1)S(1)} %fusion.87), channel_id=1, source_target_pairs={{0,1},{1,2},{2,3},{3,0},{4,5},{5,6},{6,7},{7,4},{8,9},{9,10},{10,1... | collective-permute-start | bytes 1179656 | tf_op jit(solution)/shard_map/ppermute | solution.py:128
  164.2 32.4 %collective-permute-start.21 = (bf16[256,768]{1,0:T(8,128)(2,1)S(1)}, bf16[256,768]{1,0:T(8,128)(2,1)S(1)}, u32[]{:S(2)}, u32[]{:S(2)}) collective-permute-start(bf16[256,768]{1,0:T(8,128)(2,1)S(1)} %fusion.85), channel_id=1, source_target_pairs={{0,1},{1,2},{2,3},{3,0},{4,5},{5,6},{6,7},{7,4},{8,9},{9,10},{10,1... | collective-permute-start | bytes 1179656 | tf_op jit(solution)/shard_map/ppermute | solution.py:128
  216.7 454.4 %reduce-scatter.8.cloned.1.call-start = ((), (), s32[]{:S(2)}) async-start(), calls=%async_computation.7 | async-start | bytes 6856704 | tf_op jit(solution)/shard_map/reduce_scatter | solution.py:469
  378.6 48.4 %collective-permute-start.27 = (bf16[262,512]{1,0:T(8,128)(2,1)}, bf16[262,512]{1,0:T(8,128)(2,1)S(1)}, u32[]{:S(2)}, u32[]{:S(2)}) collective-permute-start(bf16[262,512]{1,0:T(8,128)(2,1)} %get-tuple-element.114), channel_id=1, source_target_pairs={{0,1},{1,2},{2,3},{3,0},{4,5},{5,6},{6,7},{7,4},{8,9},{9,10},{10,1... | collective-permute-start | bytes 804872 | tf_op jit(solution)/shard_map/ppermute | solution.py:128
  380.8 45.2 %collective-permute-start.26 = (bf16[262,512]{1,0:T(8,128)(2,1)}, bf16[262,512]{1,0:T(8,128)(2,1)}, u32[]{:S(2)}, u32[]{:S(2)}) collective-permute-start(bf16[262,512]{1,0:T(8,128)(2,1)} %get-tuple-element.115), channel_id=1, source_target_pairs={{0,2},{1,3},{2,0},{3,1},{4,6},{5,7},{6,4},{7,5},{8,10},{9,11},{10,... | collective-permute-start | bytes 804872 | tf_op jit(solution)/shard_map/ppermute | solution.py:128
  383.0 42.0 %collective-permute-start.25 = (bf16[262,512]{1,0:T(8,128)(2,1)}, bf16[262,512]{1,0:T(8,128)(2,1)}, u32[]{:S(2)}, u32[]{:S(2)}) collective-permute-start(bf16[262,512]{1,0:T(8,128)(2,1)} %get-tuple-element.116), channel_id=1, source_target_pairs={{0,3},{1,0},{2,1},{3,2},{4,7},{5,4},{6,5},{7,6},{8,11},{9,8},{10,9... | collective-permute-start | bytes 804872 | tf_op jit(solution)/shard_map/ppermute | solution.py:128
  452.3 236.8 %reduce-scatter.6.cloned.1.call-start = ((), (), s32[]{:S(2)}) async-start(), calls=%async_computation.6 | async-start | bytes 26542080 | tf_op jit(solution)/shard_map/reduce_scatter | solution.py:469
  505.1 269.1 %reduce-scatter.4.cloned.1.call-start = ((), (), s32[]{:S(2)}) async-start(), calls=%async_computation.5 | async-start | bytes 14745600 | tf_op jit(solution)/shard_map/reduce_scatter | solution.py:469
  512.3 31.8 %collective-permute-start.24 = (bf16[262,512]{1,0:T(8,128)(2,1)S(1)}, bf16[262,512]{1,0:T(8,128)(2,1)S(1)}, u32[]{:S(2)}, u32[]{:S(2)}) collective-permute-start(bf16[262,512]{1,0:T(8,128)(2,1)S(1)} %get-tuple-element.117), channel_id=1, source_target_pairs={{0,1},{1,2},{2,3},{3,0},{4,5},{5,6},{6,7},{7,4},{8,9},{9,10},{10,1... | collective-permute-start | bytes 804872 | tf_op jit(solution)/shard_map/ppermute | solution.py:128
  514.1 29.9 %collective-permute-start.23 = (bf16[262,512]{1,0:T(8,128)(2,1)S(1)}, bf16[262,512]{1,0:T(8,128)(2,1)S(1)}, u32[]{:S(2)}, u32[]{:S(2)}) collective-permute-start(bf16[262,512]{1,0:T(8,128)(2,1)S(1)} %get-tuple-element.119), channel_id=1, source_target_pairs={{0,2},{1,3},{2,0},{3,1},{4,6},{5,7},{6,4},{7,5},{8,10},{9,11},{10,... | collective-permute-start | bytes 804872 | tf_op jit(solution)/shard_map/ppermute | solution.py:128
  517.5 26.5 %collective-permute-start.22 = (bf16[262,512]{1,0:T(8,128)(2,1)S(1)}, bf16[262,512]{1,0:T(8,128)(2,1)S(1)}, u32[]{:S(2)}, u32[]{:S(2)}) collective-permute-start(bf16[262,512]{1,0:T(8,128)(2,1)S(1)} %get-tuple-element.120), channel_id=1, source_target_pairs={{0,3},{1,0},{2,1},{3,2},{4,7},{5,4},{6,5},{7,6},{8,11},{9,8},{10,9... | collective-permute-start | bytes 804872 | tf_op jit(solution)/shard_map/ppermute | solution.py:128
  534.5 22.1 %collective-permute-start.34 = (bf16[64,1280]{1,0:T(8,128)(2,1)}, bf16[64,1280]{1,0:T(8,128)(2,1)}, u32[]{:S(2)}, u32[]{:S(2)}) collective-permute-start(bf16[64,1280]{1,0:T(8,128)(2,1)} %constant_dynamic-slice_fusion.65), channel_id=1, source_target_pairs={{0,1},{1,2},{2,3},{3,0},{4,5},{5,6},{6,7},{7,4},{8,9},{9,10},{10,1... | collective-permute-start | bytes 491528 | tf_op jit(solution)/shard_map/ppermute | solution.py:128
  543.2 19.4 %collective-permute-start.28 = (bf16[256,768]{1,0:T(8,128)(2,1)S(1)}, bf16[256,768]{1,0:T(8,128)(2,1)S(1)}, u32[]{:S(2)}, u32[]{:S(2)}) collective-permute-start(bf16[256,768]{1,0:T(8,128)(2,1)S(1)} %get-tuple-element.259), channel_id=1, source_target_pairs={{0,1},{1,2},{2,3},{3,0},{4,5},{5,6},{6,7},{7,4},{8,9},{9,10},{10,1... | collective-permute-start | bytes 1179656 | tf_op jit(solution)/shard_map/ppermute | solution.py:128
  562.7 8.4 %collective-permute-start.29 = (bf16[256,768]{1,0:T(8,128)(2,1)S(1)}, bf16[256,768]{1,0:T(8,128)(2,1)S(1)}, u32[]{:S(2)}, u32[]{:S(2)}) collective-permute-start(bf16[256,768]{1,0:T(8,128)(2,1)S(1)} %collective-permute-done.28), channel_id=1, source_target_pairs={{0,1},{1,2},{2,3},{3,0},{4,5},{5,6},{6,7},{7,4},{8,9},{9,10},{10,1... | collective-permute-start | bytes 1179656 | tf_op jit(solution)/shard_map/ppermute | solution.py:128
  563.1 11.5 %collective-permute-start.36 = (bf16[64,1280]{1,0:T(8,128)(2,1)S(1)}, bf16[64,1280]{1,0:T(8,128)(2,1)S(1)}, u32[]{:S(2)}, u32[]{:S(2)}) collective-permute-start(bf16[64,1280]{1,0:T(8,128)(2,1)S(1)} %add_convert_fusion.5), channel_id=1, source_target_pairs={{0,1},{1,2},{2,3},{3,0},{4,5},{5,6},{6,7},{7,4},{8,9},{9,10},{10,1... | collective-permute-start | bytes 491528 | tf_op jit(solution)/shard_map/ppermute | solution.py:128
  571.1 12.1 %collective-permute-start.30 = (bf16[256,768]{1,0:T(8,128)(2,1)S(1)}, bf16[256,768]{1,0:T(8,128)(2,1)S(1)}, u32[]{:S(2)}, u32[]{:S(2)}) collective-permute-start(bf16[256,768]{1,0:T(8,128)(2,1)S(1)} %collective-permute-done.29), channel_id=1, source_target_pairs={{0,1},{1,2},{2,3},{3,0},{4,5},{5,6},{6,7},{7,4},{8,9},{9,10},{10,1... | collective-permute-start | bytes 1179656 | tf_op jit(solution)/shard_map/ppermute | solution.py:128
  574.6 25.2 %collective-permute-start.37 = (bf16[64,640]{1,0:T(8,128)(2,1)S(1)}, bf16[64,640]{1,0:T(8,128)(2,1)S(1)}, u32[]{:S(2)}, u32[]{:S(2)}) collective-permute-start(bf16[64,640]{1,0:T(8,128)(2,1)S(1)} %select_convert_fusion.2), channel_id=1, source_target_pairs={{0,16},{4,20},{8,24},{12,28},{16,0},{20,4},{24,8},{28,12},{1,17},{... | collective-permute-start | bytes 245768 | tf_op jit(solution)/shard_map/ppermute | solution.py:129
  612.7 8.0 collective-permute-start.41
  623.1 88.5 %collective-permute-start.39 = (bf16[64,160]{1,0:T(8,128)(2,1)}, bf16[64,160]{1,0:T(8,128)(2,1)}, u32[]{:S(2)}, u32[]{:S(2)}) collective-permute-start(bf16[64,160]{1,0:T(8,128)(2,1)} %select_convert_fusion.5), channel_id=1, source_target_pairs={{0,4},{4,0},{8,12},{12,8},{16,20},{20,16},{24,28},{28,24},{1,5},{5... | collective-permute-start | bytes 61448 | tf_op jit(solution)/shard_map/ppermute | solution.py:129
  626.6 7.2 collective-permute-start.45
  677.1 6.5 collective-permute-start.64
  683.7 18.4 %collective-permute-start.65 = (f32[62,128]{1,0:T(8,128)S(1)}, f32[62,128]{1,0:T(8,128)}, u32[]{:S(2)}, u32[]{:S(2)}) collective-permute-start(f32[62,128]{1,0:T(8,128)S(1)} %fusion.306), channel_id=1, source_target_pairs={{0,8},{4,12},{8,0},{12,4},{16,24},{20,28},{24,16},{28,20},{1,9},{5... | collective-permute-start | bytes 95240 | tf_op jit(solution)/shard_map/ppermute | solution.py:129
  700.7 26.9 %collective-permute-start.55 = (bf16[160,2304]{1,0:T(8,128)(2,1)S(1)}, bf16[160,2304]{1,0:T(8,128)(2,1)}, u32[]{:S(2)}, u32[]{:S(2)}) collective-permute-start(bf16[160,2304]{1,0:T(8,128)(2,1)S(1)} %concatenate.197), channel_id=1, source_target_pairs={{0,1},{1,2},{2,3},{3,0},{4,5},{5,6},{6,7},{7,4},{8,9},{9,10},{10,1... | collective-permute-start | bytes 2211848 | tf_op jit(solution)/shard_map/ppermute | solution.py:128
  705.7 9.2 %collective-permute-start.69 = (f32[62,128]{1,0:T(8,128)S(1)}, f32[62,128]{1,0:T(8,128)S(1)}, u32[]{:S(2)}, u32[]{:S(2)}) collective-permute-start(f32[62,128]{1,0:T(8,128)S(1)} %add.914), channel_id=1, source_target_pairs={{0,1},{1,2},{2,3},{3,0},{4,5},{5,6},{6,7},{7,4},{8,9},{9,10},{10,1... | collective-permute-start | bytes 95240 | tf_op jit(solution)/shard_map/ppermute | solution.py:128
  707.6 9.6 %collective-permute-start.68 = (f32[62,128]{1,0:T(8,128)S(1)}, f32[62,128]{1,0:T(8,128)S(1)}, u32[]{:S(2)}, u32[]{:S(2)}) collective-permute-start(f32[62,128]{1,0:T(8,128)S(1)} %add.914), channel_id=1, source_target_pairs={{0,2},{1,3},{2,0},{3,1},{4,6},{5,7},{6,4},{7,5},{8,10},{9,11},{10,... | collective-permute-start | bytes 95240 | tf_op jit(solution)/shard_map/ppermute | solution.py:128
  710.3 15.1 %collective-permute-start.67 = (f32[62,128]{1,0:T(8,128)S(1)}, f32[62,128]{1,0:T(8,128)S(1)}, u32[]{:S(2)}, u32[]{:S(2)}) collective-permute-start(f32[62,128]{1,0:T(8,128)S(1)} %add.914), channel_id=1, source_target_pairs={{0,3},{1,0},{2,1},{3,2},{4,7},{5,4},{6,5},{7,6},{8,11},{9,8},{10,9... | collective-permute-start | bytes 95240 | tf_op jit(solution)/shard_map/ppermute | solution.py:128
  728.9 21.8 %collective-permute-start.56 = (bf16[160,2304]{1,0:T(8,128)(2,1)S(1)}, bf16[160,2304]{1,0:T(8,128)(2,1)S(1)}, u32[]{:S(2)}, u32[]{:S(2)}) collective-permute-start(bf16[160,2304]{1,0:T(8,128)(2,1)S(1)} %add_convert_fusion.1), channel_id=1, source_target_pairs={{0,1},{1,2},{2,3},{3,0},{4,5},{5,6},{6,7},{7,4},{8,9},{9,10},{10,1... | collective-permute-start | bytes 2211848 | tf_op jit(solution)/shard_map/ppermute | solution.py:128
  729.8 18.5 %collective-permute-start.61 = (bf16[96,512]{1,0:T(8,128)(2,1)S(1)}, bf16[96,512]{1,0:T(8,128)(2,1)S(1)}, u32[]{:S(2)}, u32[]{:S(2)}) collective-permute-start(bf16[96,512]{1,0:T(8,128)(2,1)S(1)} %constant_dynamic-slice_fusion.14), channel_id=1, source_target_pairs={{0,1},{1,2},{2,3},{3,0},{4,5},{5,6},{6,7},{7,4},{8,9},{9,10},{10,1... | collective-permute-start | bytes 294920 | tf_op jit(solution)/shard_map/ppermute | solution.py:128
  751.8 21.0 %collective-permute-start.57 = (bf16[160,2304]{1,0:T(8,128)(2,1)}, bf16[160,2304]{1,0:T(8,128)(2,1)S(1)}, u32[]{:S(2)}, u32[]{:S(2)}) collective-permute-start(bf16[160,2304]{1,0:T(8,128)(2,1)} %add_convert_fusion), channel_id=1, source_target_pairs={{0,1},{1,2},{2,3},{3,0},{4,5},{5,6},{6,7},{7,4},{8,9},{9,10},{10,1... | collective-permute-start | bytes 2211848 | tf_op jit(solution)/shard_map/ppermute | solution.py:128
  752.6 18.1 %collective-permute-start.63 = (bf16[96,512]{1,0:T(8,128)(2,1)S(1)}, bf16[96,512]{1,0:T(8,128)(2,1)S(1)}, u32[]{:S(2)}, u32[]{:S(2)}) collective-permute-start(bf16[96,512]{1,0:T(8,128)(2,1)S(1)} %add_convert_fusion.7), channel_id=1, source_target_pairs={{0,1},{1,2},{2,3},{3,0},{4,5},{5,6},{6,7},{7,4},{8,9},{9,10},{10,1... | collective-permute-start | bytes 294920 | tf_op jit(solution)/shard_map/ppermute | solution.py:128
  779.2 10.0 %collective-permute-start.58 = (bf16[160,1280]{1,0:T(8,128)(2,1)}, bf16[160,1280]{1,0:T(8,128)(2,1)}, u32[]{:S(2)}, u32[]{:S(2)}) collective-permute-start(bf16[160,1280]{1,0:T(8,128)(2,1)} %concatenate.202), channel_id=1, source_target_pairs={{0,1},{1,2},{2,3},{3,0},{4,5},{5,6},{6,7},{7,4},{8,9},{9,10},{10,1... | collective-permute-start | bytes 1228808 | tf_op jit(solution)/shard_map/ppermute | solution.py:128
  780.2 32.2 %collective-permute-start.59 = (bf16[160,1280]{1,0:T(8,128)(2,1)}, bf16[160,1280]{1,0:T(8,128)(2,1)S(1)}, u32[]{:S(2)}, u32[]{:S(2)}) collective-permute-start(bf16[160,1280]{1,0:T(8,128)(2,1)} %concatenate.203), channel_id=1, source_target_pairs={{0,2},{1,3},{2,0},{3,1},{4,6},{5,7},{6,4},{7,5},{8,10},{9,11},{10,... | collective-permute-start | bytes 1228808 | tf_op jit(solution)/shard_map/ppermute | solution.py:128
  785.8 34.7 %collective-permute-start.60 = (bf16[160,1280]{1,0:T(8,128)(2,1)}, bf16[160,1280]{1,0:T(8,128)(2,1)}, u32[]{:S(2)}, u32[]{:S(2)}) collective-permute-start(bf16[160,1280]{1,0:T(8,128)(2,1)} %concatenate.204), channel_id=1, source_target_pairs={{0,3},{1,0},{2,1},{3,2},{4,7},{5,4},{6,5},{7,6},{8,11},{9,8},{10,9... | collective-permute-start | bytes 1228808 | tf_op jit(solution)/shard_map/ppermute | solution.py:128
  (208 other events, 1352.8 us)
Sparse Core Ops, SparseCore 0:
  11.9 200.5 all-gather.2
  216.9 119.3 all-gather.4
  452.5 61.3 reduce-scatter.7
  517.3 152.7 reduce-scatter.5
  674.0 96.5 reduce-scatter.3

commit v3 on v2

--- a/solution.py
+++ b/solution.py
@@ -538,7 +538,7 @@
     value_term = jnp.pad(value_term, ((0, 0), (0, col_rows - in_rows), (0, 0)))
     value_term = value_term.reshape(dn * col_rows, chan)
     ready, rows_c = summed(*g_ffn0, dot_tn(branch, attended), value_term)
-    around = links.free(links.ring((mix_grad * repeat + ready).astype(BF)))
+    around = links.free(links.direct([(mix_grad * repeat + ready).astype(BF)] * mn))
 
     def latents_task():
         value = yield from links.sum_ring(lambda t: by_own_rows(branch, t))
@@ -604,7 +604,7 @@
     g_xq, g_dq, g_do, g_voc = rows_a
     g_xq = columns([g_xq])
     g_sq = links.free(rows_task([g_dq, g_do, g_voc]))
-    after = nothing_of(g_sq).astype(BF)
+    after = (nothing_of(g_sq) + nothing_of(g_xq)).astype(BF)
     g_b = columns([term + after for term in rows_b])
     g_dk, g_dv, g_up1, g_down1, g_v, g_out1, g_q, g_k = split(
         g_b, *([deck_wide] * 2 + [col_wide] * 6)

time: 843 us -> 824 us (0.977)
  waiting for transfers between devices: 247 us -> 228 us
    dot_general x19, matrix products: 48 us -> 36.4 us  [dot(): return jnp.dot(left, right, preferred_element_type=F32)]
    ppermute x51, waiting for transfers between devices: 204 us -> 193 us  [send(): return lax.ppermute(value, 'mp', pairs)]
    unnamed x405 -> x407, local copies, waits for them, and re-layouts: 49.9 us -> 49.3 us
  transfers between devices with their start and end apart: 75 -> 75, of which waited for: 40 -> 35; matrix products, arithmetic and copies ran while one was open for 43% -> 43% of each run, Pallas kernels for 0% -> 0%
where the time goes in v3:
time: 824 us; the launch traced here: 812 us
  local copies, waits for them, and re-layouts  232 us (28%)
  waiting for transfers between devices  228 us (28%)
  matrix products  143 us (17%)
  starting transfers between devices  119 us (14%)
  other arithmetic  66.1 us (8%)
  between operations  23.6 us (3%)
    ppermute x51, waiting for transfers between devices, send(): return lax.ppermute(value, 'mp', pairs)  193 us
    ppermute x51, starting transfers between devices, send(): return lax.ppermute(value, 'mp', pairs)  88.4 us
    concatenate x10, local copies, waits for them, and re-layouts, beside(): return jnp.concatenate([part.reshape(dn * size, wide) for part in parts], 1)  65.1 us
    unnamed x407, local copies, waits for them, and re-layouts  49.3 us
    dot_general x19, matrix products, dot_tn(): lax.dot_general(left, right, (((0,), (0,)), ((), ())), preferred_element_...  39.1 us
    dot_general x19, matrix products, dot(): return jnp.dot(left, right, preferred_element_type=F32)  36.4 us
    dot_general x19, matrix products, dot_t(): lax.dot_general(left, right, (((left.ndim - 1,), (right.ndim - 1,)), ((),...  36 us
    slice x5, local copies, waits for them, and re-layouts, beside(): parts = [got[:, m, row:row + size, col:col + wide] for m in range(mn)]  35.9 us
  transfers between devices with their start and end apart: 75, of which 35 were waited for; matrix products, arithmetic and copies ran while one was open for 43% of the time, Pallas kernels for 0%

profile of v3, /device:TPU:11, one launch (start us, length us, event | category | flops | bytes accessed | tf_op | source)
XLA Modules:
  0.0 812.2 jit_solution(7375231343104615425)
XLA Ops:
  24.6 6.9 collective-permute-done.4
  61.5 5.3 collective-permute-done.12
  66.8 6.2 collective-permute-done.11
  73.7 4.4 collective-permute-start.13
  80.7 11.6 %collective-permute-start.15 = (bf16[64,768]{1,0:T(8,128)(2,1)}, bf16[64,768]{1,0:T(8,128)(2,1)S(1)}, u32[]{:S(2)}, u32[]{:S(2)}) collective-permute-start(bf16[64,768]{1,0:T(8,128)(2,1)} %get-tuple-element.42), channel_id=1, source_target_pairs={{0,1},{1,2},{2,3},{3,0},{4,5},{5,6},{6,7},{7,4},{8,9},{9,10},{10,1... | collective-permute-start | bytes 294920 | tf_op jit(solution)/shard_map/ppermute | solution.py:128
  92.3 4.0 collective-permute-start.14
  97.0 6.9 collective-permute-done.14
  120.7 22.5 %collective-permute-done.16 = bf16[256,768]{1,0:T(8,128)(2,1)S(1)} collective-permute-done((bf16[256,768]{1,0:T(8,128)(2,1)S(1)}, bf16[256,768]{1,0:T(8,128)(2,1)S(1)}, u32[]{:S(2)}, u32[]{:S(2)}) %collective-permute-start.16) | collective-permute-done | bytes 393248 | tf_op jit(solution)/shard_map/ppermute | solution.py:128
  146.5 22.8 %collective-permute-done.20 = bf16[256,768]{1,0:T(8,128)(2,1)S(1)} collective-permute-done((bf16[256,768]{1,0:T(8,128)(2,1)S(1)}, bf16[256,768]{1,0:T(8,128)(2,1)S(1)}, u32[]{:S(2)}, u32[]{:S(2)}) %collective-permute-start.20) | collective-permute-done | bytes 393248 | tf_op jit(solution)/shard_map/ppermute | solution.py:128
  169.4 5.9 collective-permute-start.21
  176.0 24.1 %collective-permute-done.21 = bf16[256,768]{1,0:T(8,128)(2,1)S(1)} collective-permute-done((bf16[256,768]{1,0:T(8,128)(2,1)S(1)}, bf16[256,768]{1,0:T(8,128)(2,1)S(1)}, u32[]{:S(2)}, u32[]{:S(2)}) %collective-permute-start.21) | collective-permute-done | bytes 393248 | tf_op jit(solution)/shard_map/ppermute | solution.py:128
  202.6 9.9 %all-gather.3.cloned.1.call-done = bf16[20480,640]{1,0:T(8,128)(2,1)} async-done(((bf16[640,640]{1,0:T(8,128)(2,1)}), bf16[20480,640]{1,0:T(8,128)(2,1)}) %all-gather.3.cloned.1.call-update) | async-done | bytes 26214416 | tf_op jit(solution)/shard_map/all_gather | solution.py:275
  225.9 4.2 fusion.186
  230.1 4.3 concatenate.169
  234.4 6.4 fusion.185
  240.8 12.4 %fusion.184 = (bf16[8,1,160,320]{3,2,1,0:T(8,128)(2,1)}, bf16[8,1,160,320]{3,2,1,0:T(8,128)(2,1)}, bf16[8,1,160,320]{3,2,1,0:T(8,128)(2,1)}, bf16[8,1,160,320]{3...) fusion(bf16[8,4,640,640]{3,2,1,0:T(8,128)(2,1)} %bitcast.418), kind=kLoop, calls=%fused_computation.615 | loop fusion | bytes 31129600 | tf_op jit(solution)/shard_map/slice | solution.py:283
  253.2 6.7 concatenate.172
  260.0 6.7 concatenate.171
  266.7 6.5 concatenate.170
  273.3 6.8 concatenate.175
  282.3 4.3 fusion.196
  287.0 4.9 fusion.31
  298.5 6.8 concatenate.174
  305.3 4.0 fusion.14
  311.5 6.8 concatenate.173
  318.3 4.0 convolution_convert_fusion.19
  324.4 6.8 concatenate.176
  334.9 3.9 convolution_convert_fusion.25
  345.1 4.0 fusion.188
  351.3 6.2 fusion.187
  357.6 6.7 fusion.189
  377.8 6.7 concatenate.181
  384.5 4.5 fusion.175
  389.0 6.9 concatenate.182
  395.9 6.6 fusion.200
  442.1 4.1 multiply_reduce_fusion.7
  477.4 5.7 fusion.5
  539.4 6.1 pad_maximum_fusion
  548.8 20.2 %collective-permute-done.34 = bf16[64,1280]{1,0:T(8,128)(2,1)S(1)} collective-permute-done((bf16[64,1280]{1,0:T(8,128)(2,1)S(1)}, bf16[64,1280]{1,0:T(8,128)(2,1)S(1)}, u32[]{:S(2)}, u32[]{:S(2)}) %collective-permute-start.34) | collective-permute-done | bytes 163872 | tf_op jit(solution)/shard_map/ppermute | solution.py:128
  609.0 5.3 multiply_reduce_fusion.1
  627.1 4.3 collective-permute-done.46
  633.1 4.3 collective-permute-done.47
  637.5 4.4 collective-permute-start.48
  693.8 6.0 collective-permute-start.64
  721.6 16.2 %collective-permute-done.67 = f32[62,128]{1,0:T(8,128)S(1)} collective-permute-done((f32[62,128]{1,0:T(8,128)S(1)}, f32[62,128]{1,0:T(8,128)S(1)}, u32[]{:S(2)}, u32[]{:S(2)}) %collective-permute-start.67) | collective-permute-done | bytes 31776 | tf_op jit(solution)/shard_map/ppermute | solution.py:128
  744.4 12.9 %collective-permute-done.60 = bf16[160,2304]{1,0:T(8,128)(2,1)} collective-permute-done((bf16[160,2304]{1,0:T(8,128)(2,1)S(1)}, bf16[160,2304]{1,0:T(8,128)(2,1)}, u32[]{:S(2)}, u32[]{:S(2)}) %collective-permute-start.60) | collective-permute-done | bytes 737312 | tf_op jit(solution)/shard_map/ppermute | solution.py:128
  772.4 24.7 %collective-permute-done.62 = bf16[160,1280]{1,0:T(8,128)(2,1)S(1)} collective-permute-done((bf16[160,1280]{1,0:T(8,128)(2,1)}, bf16[160,1280]{1,0:T(8,128)(2,1)S(1)}, u32[]{:S(2)}, u32[]{:S(2)}) %collective-permute-start.62) | collective-permute-done | bytes 409632 | tf_op jit(solution)/shard_map/ppermute | solution.py:128
  797.1 4.0 collective-permute-done.63
  (862 shorter events, 402.7 us)
Async XLA Ops:
  7.2 205.3 %all-gather.3.cloned.1.call-start = ((), (), s32[]{:S(2)}) async-start(), calls=%async_computation.3 | async-start | bytes 27033600 | tf_op jit(solution)/shard_map/all_gather | solution.py:275
  11.8 332.2 %all-gather.5.cloned.1.call-start = ((), (), s32[]{:S(2)}) async-start(), calls=%async_computation.4 | async-start | bytes 18382848 | tf_op jit(solution)/shard_map/all_gather | solution.py:275
  19.9 11.6 %collective-permute-start.4 = (bf16[272,480]{1,0:T(8,128)(2,1)}, bf16[272,480]{1,0:T(8,128)(2,1)S(1)}, u32[]{:S(2)}, u32[]{:S(2)}) collective-permute-start(bf16[272,480]{1,0:T(8,128)(2,1)} %get-tuple-element.44), channel_id=1, source_target_pairs={{0,8},{4,12},{8,0},{12,4},{16,24},{20,28},{24,16},{28,20},{1,9},{5... | collective-permute-start | bytes 783368 | tf_op jit(solution)/shard_map/ppermute | solution.py:129
  20.0 17.3 %collective-permute-start.3 = (bf16[272,480]{1,0:T(8,128)(2,1)}, bf16[272,480]{1,0:T(8,128)(2,1)}, u32[]{:S(2)}, u32[]{:S(2)}) collective-permute-start(bf16[272,480]{1,0:T(8,128)(2,1)} %get-tuple-element.44), channel_id=1, source_target_pairs={{0,4},{4,0},{8,12},{12,8},{16,20},{20,16},{24,28},{28,24},{1,5},{5... | collective-permute-start | bytes 783368 | tf_op jit(solution)/shard_map/ppermute | solution.py:129
  22.0 14.6 %collective-permute-start.6 = (bf16[272,480]{1,0:T(8,128)(2,1)}, bf16[272,480]{1,0:T(8,128)(2,1)S(1)}, u32[]{:S(2)}, u32[]{:S(2)}) collective-permute-start(bf16[272,480]{1,0:T(8,128)(2,1)} %get-tuple-element.44), channel_id=1, source_target_pairs={{0,16},{4,20},{8,24},{12,28},{16,0},{20,4},{24,8},{28,12},{1,17},{... | collective-permute-start | bytes 783368 | tf_op jit(solution)/shard_map/ppermute | solution.py:129
  31.5 9.9 %collective-permute-start.8 = (bf16[272,480]{1,0:T(8,128)(2,1)S(1)}, bf16[272,480]{1,0:T(8,128)(2,1)S(1)}, u32[]{:S(2)}, u32[]{:S(2)}) collective-permute-start(bf16[272,480]{1,0:T(8,128)(2,1)S(1)} %collective-permute-done.4), channel_id=1, source_target_pairs={{0,16},{4,20},{8,24},{12,28},{16,0},{20,4},{24,8},{28,12},{1,17},{... | collective-permute-start | bytes 783368 | tf_op jit(solution)/shard_map/ppermute | solution.py:129
  32.9 10.3 %collective-permute-start.5 = (bf16[272,480]{1,0:T(8,128)(2,1)S(1)}, bf16[272,480]{1,0:T(8,128)(2,1)S(1)}, u32[]{:S(2)}, u32[]{:S(2)}) collective-permute-start(bf16[272,480]{1,0:T(8,128)(2,1)S(1)} %collective-permute-done.4), channel_id=1, source_target_pairs={{0,4},{4,0},{8,12},{12,8},{16,20},{20,16},{24,28},{28,24},{1,5},{5... | collective-permute-start | bytes 783368 | tf_op jit(solution)/shard_map/ppermute | solution.py:129
  36.7 6.5 collective-permute-start.7
  53.6 7.9 collective-permute-start.10
  54.6 12.2 %collective-permute-start.12 = (bf16[64,768]{1,0:T(8,128)(2,1)S(1)}, bf16[64,768]{1,0:T(8,128)(2,1)S(1)}, u32[]{:S(2)}, u32[]{:S(2)}) collective-permute-start(bf16[64,768]{1,0:T(8,128)(2,1)S(1)} %get-tuple-element.172), channel_id=1, source_target_pairs={{0,3},{1,0},{2,1},{3,2},{4,7},{5,4},{6,5},{7,6},{8,11},{9,8},{10,9... | collective-permute-start | bytes 294920 | tf_op jit(solution)/shard_map/ppermute | solution.py:128
  55.1 17.8 %collective-permute-start.11 = (bf16[64,768]{1,0:T(8,128)(2,1)S(1)}, bf16[64,768]{1,0:T(8,128)(2,1)S(1)}, u32[]{:S(2)}, u32[]{:S(2)}) collective-permute-start(bf16[64,768]{1,0:T(8,128)(2,1)S(1)} %get-tuple-element.173), channel_id=1, source_target_pairs={{0,2},{1,3},{2,0},{3,1},{4,6},{5,7},{6,4},{7,5},{8,10},{9,11},{10,... | collective-permute-start | bytes 294920 | tf_op jit(solution)/shard_map/ppermute | solution.py:128
  73.7 22.6 %collective-permute-start.13 = (bf16[64,768]{1,0:T(8,128)(2,1)}, bf16[64,768]{1,0:T(8,128)(2,1)S(1)}, u32[]{:S(2)}, u32[]{:S(2)}) collective-permute-start(bf16[64,768]{1,0:T(8,128)(2,1)} %get-tuple-element.42), channel_id=1, source_target_pairs={{0,3},{1,0},{2,1},{3,2},{4,7},{5,4},{6,5},{7,6},{8,11},{9,8},{10,9... | collective-permute-start | bytes 294920 | tf_op jit(solution)/shard_map/ppermute | solution.py:128
  80.7 23.8 %collective-permute-start.15 = (bf16[64,768]{1,0:T(8,128)(2,1)}, bf16[64,768]{1,0:T(8,128)(2,1)S(1)}, u32[]{:S(2)}, u32[]{:S(2)}) collective-permute-start(bf16[64,768]{1,0:T(8,128)(2,1)} %get-tuple-element.42), channel_id=1, source_target_pairs={{0,1},{1,2},{2,3},{3,0},{4,5},{5,6},{6,7},{7,4},{8,9},{9,10},{10,1... | collective-permute-start | bytes 294920 | tf_op jit(solution)/shard_map/ppermute | solution.py:128
  92.3 11.5 %collective-permute-start.14 = (bf16[64,768]{1,0:T(8,128)(2,1)}, bf16[64,768]{1,0:T(8,128)(2,1)S(1)}, u32[]{:S(2)}, u32[]{:S(2)}) collective-permute-start(bf16[64,768]{1,0:T(8,128)(2,1)} %get-tuple-element.42), channel_id=1, source_target_pairs={{0,2},{1,3},{2,0},{3,1},{4,6},{5,7},{6,4},{7,5},{8,10},{9,11},{10,... | collective-permute-start | bytes 294920 | tf_op jit(solution)/shard_map/ppermute | solution.py:128
  112.2 8.4 %collective-permute-start.18 = (f32[2,4,256]{2,1,0:T(4,128)S(1)}, f32[2,4,256]{2,1,0:T(4,128)S(1)}, u32[]{:S(2)}, u32[]{:S(2)}) collective-permute-start(f32[2,4,256]{2,1,0:T(4,128)S(1)} %get-tuple-element.226), channel_id=1, source_target_pairs={{0,2},{1,3},{2,0},{3,1},{4,6},{5,7},{6,4},{7,5},{8,10},{9,11},{10,... | collective-permute-start | bytes 24584 | tf_op jit(solution)/shard_map/ppermute | solution.py:128
  119.7 23.6 %collective-permute-start.16 = (bf16[256,768]{1,0:T(8,128)(2,1)S(1)}, bf16[256,768]{1,0:T(8,128)(2,1)S(1)}, u32[]{:S(2)}, u32[]{:S(2)}) collective-permute-start(bf16[256,768]{1,0:T(8,128)(2,1)S(1)} %dynamic-slice_bitcast_fusion), channel_id=1, source_target_pairs={{0,1},{1,2},{2,3},{3,0},{4,5},{5,6},{6,7},{7,4},{8,9},{9,10},{10,1... | collective-permute-start | bytes 1179656 | tf_op jit(solution)/shard_map/ppermute | solution.py:128
  143.5 25.8 %collective-permute-start.20 = (bf16[256,768]{1,0:T(8,128)(2,1)S(1)}, bf16[256,768]{1,0:T(8,128)(2,1)S(1)}, u32[]{:S(2)}, u32[]{:S(2)}) collective-permute-start(bf16[256,768]{1,0:T(8,128)(2,1)S(1)} %fusion.87), channel_id=1, source_target_pairs={{0,1},{1,2},{2,3},{3,0},{4,5},{5,6},{6,7},{7,4},{8,9},{9,10},{10,1... | collective-permute-start | bytes 1179656 | tf_op jit(solution)/shard_map/ppermute | solution.py:128
  169.4 30.6 %collective-permute-start.21 = (bf16[256,768]{1,0:T(8,128)(2,1)S(1)}, bf16[256,768]{1,0:T(8,128)(2,1)S(1)}, u32[]{:S(2)}, u32[]{:S(2)}) collective-permute-start(bf16[256,768]{1,0:T(8,128)(2,1)S(1)} %fusion.85), channel_id=1, source_target_pairs={{0,1},{1,2},{2,3},{3,0},{4,5},{5,6},{6,7},{7,4},{8,9},{9,10},{10,1... | collective-permute-start | bytes 1179656 | tf_op jit(solution)/shard_map/ppermute | solution.py:128
  216.7 439.2 %reduce-scatter.8.cloned.1.call-start = ((), (), s32[]{:S(2)}) async-start(), calls=%async_computation.7 | async-start | bytes 6856704 | tf_op jit(solution)/shard_map/reduce_scatter | solution.py:469
  366.9 49.1 %collective-permute-start.27 = (bf16[262,512]{1,0:T(8,128)(2,1)}, bf16[262,512]{1,0:T(8,128)(2,1)S(1)}, u32[]{:S(2)}, u32[]{:S(2)}) collective-permute-start(bf16[262,512]{1,0:T(8,128)(2,1)} %get-tuple-element.114), channel_id=1, source_target_pairs={{0,1},{1,2},{2,3},{3,0},{4,5},{5,6},{6,7},{7,4},{8,9},{9,10},{10,1... | collective-permute-start | bytes 804872 | tf_op jit(solution)/shard_map/ppermute | solution.py:128
  369.1 45.9 %collective-permute-start.26 = (bf16[262,512]{1,0:T(8,128)(2,1)}, bf16[262,512]{1,0:T(8,128)(2,1)}, u32[]{:S(2)}, u32[]{:S(2)}) collective-permute-start(bf16[262,512]{1,0:T(8,128)(2,1)} %get-tuple-element.115), channel_id=1, source_target_pairs={{0,2},{1,3},{2,0},{3,1},{4,6},{5,7},{6,4},{7,5},{8,10},{9,11},{10,... | collective-permute-start | bytes 804872 | tf_op jit(solution)/shard_map/ppermute | solution.py:128
  372.2 41.8 %collective-permute-start.25 = (bf16[262,512]{1,0:T(8,128)(2,1)}, bf16[262,512]{1,0:T(8,128)(2,1)}, u32[]{:S(2)}, u32[]{:S(2)}) collective-permute-start(bf16[262,512]{1,0:T(8,128)(2,1)} %get-tuple-element.116), channel_id=1, source_target_pairs={{0,3},{1,0},{2,1},{3,2},{4,7},{5,4},{6,5},{7,6},{8,11},{9,8},{10,9... | collective-permute-start | bytes 804872 | tf_op jit(solution)/shard_map/ppermute | solution.py:128
  441.4 236.2 %reduce-scatter.6.cloned.1.call-start = ((), (), s32[]{:S(2)}) async-start(), calls=%async_computation.6 | async-start | bytes 26542080 | tf_op jit(solution)/shard_map/reduce_scatter | solution.py:469
  494.5 265.2 %reduce-scatter.4.cloned.1.call-start = ((), (), s32[]{:S(2)}) async-start(), calls=%async_computation.5 | async-start | bytes 14745600 | tf_op jit(solution)/shard_map/reduce_scatter | solution.py:469
  502.4 34.2 %collective-permute-start.24 = (bf16[262,512]{1,0:T(8,128)(2,1)S(1)}, bf16[262,512]{1,0:T(8,128)(2,1)S(1)}, u32[]{:S(2)}, u32[]{:S(2)}) collective-permute-start(bf16[262,512]{1,0:T(8,128)(2,1)S(1)} %get-tuple-element.117), channel_id=1, source_target_pairs={{0,1},{1,2},{2,3},{3,0},{4,5},{5,6},{6,7},{7,4},{8,9},{9,10},{10,1... | collective-permute-start | bytes 804872 | tf_op jit(solution)/shard_map/ppermute | solution.py:128
  505.0 30.1 %collective-permute-start.23 = (bf16[262,512]{1,0:T(8,128)(2,1)S(1)}, bf16[262,512]{1,0:T(8,128)(2,1)S(1)}, u32[]{:S(2)}, u32[]{:S(2)}) collective-permute-start(bf16[262,512]{1,0:T(8,128)(2,1)S(1)} %get-tuple-element.119), channel_id=1, source_target_pairs={{0,2},{1,3},{2,0},{3,1},{4,6},{5,7},{6,4},{7,5},{8,10},{9,11},{10,... | collective-permute-start | bytes 804872 | tf_op jit(solution)/shard_map/ppermute | solution.py:128
  507.1 27.8 %collective-permute-start.22 = (bf16[262,512]{1,0:T(8,128)(2,1)S(1)}, bf16[262,512]{1,0:T(8,128)(2,1)S(1)}, u32[]{:S(2)}, u32[]{:S(2)}) collective-permute-start(bf16[262,512]{1,0:T(8,128)(2,1)S(1)} %get-tuple-element.120), channel_id=1, source_target_pairs={{0,3},{1,0},{2,1},{3,2},{4,7},{5,4},{6,5},{7,6},{8,11},{9,8},{10,9... | collective-permute-start | bytes 804872 | tf_op jit(solution)/shard_map/ppermute | solution.py:128
  531.1 46.6 %collective-permute-start.30 = (bf16[256,768]{1,0:T(8,128)(2,1)}, bf16[256,768]{1,0:T(8,128)(2,1)S(1)}, u32[]{:S(2)}, u32[]{:S(2)}) collective-permute-start(bf16[256,768]{1,0:T(8,128)(2,1)} %get-tuple-element.259), channel_id=1, source_target_pairs={{0,1},{1,2},{2,3},{3,0},{4,5},{5,6},{6,7},{7,4},{8,9},{9,10},{10,1... | collective-permute-start | bytes 1179656 | tf_op jit(solution)/shard_map/ppermute | solution.py:128
  532.3 44.6 %collective-permute-start.29 = (bf16[256,768]{1,0:T(8,128)(2,1)}, bf16[256,768]{1,0:T(8,128)(2,1)S(1)}, u32[]{:S(2)}, u32[]{:S(2)}) collective-permute-start(bf16[256,768]{1,0:T(8,128)(2,1)} %get-tuple-element.259), channel_id=1, source_target_pairs={{0,2},{1,3},{2,0},{3,1},{4,6},{5,7},{6,4},{7,5},{8,10},{9,11},{10,... | collective-permute-start | bytes 1179656 | tf_op jit(solution)/shard_map/ppermute | solution.py:128
  534.9 41.2 %collective-permute-start.28 = (bf16[256,768]{1,0:T(8,128)(2,1)}, bf16[256,768]{1,0:T(8,128)(2,1)S(1)}, u32[]{:S(2)}, u32[]{:S(2)}) collective-permute-start(bf16[256,768]{1,0:T(8,128)(2,1)} %get-tuple-element.259), channel_id=1, source_target_pairs={{0,3},{1,0},{2,1},{3,2},{4,7},{5,4},{6,5},{7,6},{8,11},{9,8},{10,9... | collective-permute-start | bytes 1179656 | tf_op jit(solution)/shard_map/ppermute | solution.py:128
  535.0 34.0 %collective-permute-start.34 = (bf16[64,1280]{1,0:T(8,128)(2,1)S(1)}, bf16[64,1280]{1,0:T(8,128)(2,1)S(1)}, u32[]{:S(2)}, u32[]{:S(2)}) collective-permute-start(bf16[64,1280]{1,0:T(8,128)(2,1)S(1)} %constant_dynamic-slice_fusion.65), channel_id=1, source_target_pairs={{0,1},{1,2},{2,3},{3,0},{4,5},{5,6},{6,7},{7,4},{8,9},{9,10},{10,1... | collective-permute-start | bytes 491528 | tf_op jit(solution)/shard_map/ppermute | solution.py:128
  575.0 41.0 %collective-permute-start.36 = (bf16[64,1280]{1,0:T(8,128)(2,1)S(1)}, bf16[64,1280]{1,0:T(8,128)(2,1)S(1)}, u32[]{:S(2)}, u32[]{:S(2)}) collective-permute-start(bf16[64,1280]{1,0:T(8,128)(2,1)S(1)} %add_convert_fusion.5), channel_id=1, source_target_pairs={{0,1},{1,2},{2,3},{3,0},{4,5},{5,6},{6,7},{7,4},{8,9},{9,10},{10,1... | collective-permute-start | bytes 491528 | tf_op jit(solution)/shard_map/ppermute | solution.py:128
  588.7 6.6 collective-permute-start.33
  617.5 7.2 collective-permute-start.43
  619.5 7.5 collective-permute-start.37
  632.1 9.7 %collective-permute-start.38 = (bf16[64,320]{1,0:T(8,128)(2,1)S(1)}, bf16[64,320]{1,0:T(8,128)(2,1)S(1)}, u32[]{:S(2)}, u32[]{:S(2)}) collective-permute-start(bf16[64,320]{1,0:T(8,128)(2,1)S(1)} %select_convert_fusion.4), channel_id=1, source_target_pairs={{0,8},{4,12},{8,0},{12,4},{16,24},{20,28},{24,16},{28,20},{1,9},{5... | collective-permute-start | bytes 122888 | tf_op jit(solution)/shard_map/ppermute | solution.py:129
  644.9 70.3 %collective-permute-start.39 = (bf16[64,160]{1,0:T(8,128)(2,1)}, bf16[64,160]{1,0:T(8,128)(2,1)}, u32[]{:S(2)}, u32[]{:S(2)}) collective-permute-start(bf16[64,160]{1,0:T(8,128)(2,1)} %select_convert_fusion.5), channel_id=1, source_target_pairs={{0,4},{4,0},{8,12},{12,8},{16,20},{20,16},{24,28},{28,24},{1,5},{5... | collective-permute-start | bytes 61448 | tf_op jit(solution)/shard_map/ppermute | solution.py:129
  655.8 34.6 %collective-permute-start.51 = (bf16[64,1280]{1,0:T(8,128)(2,1)}, bf16[64,1280]{1,0:T(8,128)(2,1)}, u32[]{:S(2)}, u32[]{:S(2)}) collective-permute-start(bf16[64,1280]{1,0:T(8,128)(2,1)} %add_convert_fusion.3), channel_id=1, source_target_pairs={{0,1},{1,2},{2,3},{3,0},{4,5},{5,6},{6,7},{7,4},{8,9},{9,10},{10,1... | collective-permute-start | bytes 491528 | tf_op jit(solution)/shard_map/ppermute | solution.py:128
  690.0 13.6 %collective-permute-start.58 = (bf16[160,2304]{1,0:T(8,128)(2,1)S(1)}, bf16[160,2304]{1,0:T(8,128)(2,1)S(1)}, u32[]{:S(2)}, u32[]{:S(2)}) collective-permute-start(bf16[160,2304]{1,0:T(8,128)(2,1)S(1)} %concatenate.197), channel_id=1, source_target_pairs={{0,1},{1,2},{2,3},{3,0},{4,5},{5,6},{6,7},{7,4},{8,9},{9,10},{10,1... | collective-permute-start | bytes 2211848 | tf_op jit(solution)/shard_map/ppermute | solution.py:128
  693.8 6.9 collective-permute-start.64
  703.8 36.3 %collective-permute-start.59 = (bf16[160,2304]{1,0:T(8,128)(2,1)S(1)}, bf16[160,2304]{1,0:T(8,128)(2,1)S(1)}, u32[]{:S(2)}, u32[]{:S(2)}) collective-permute-start(bf16[160,2304]{1,0:T(8,128)(2,1)S(1)} %add_convert_fusion.1), channel_id=1, source_target_pairs={{0,1},{1,2},{2,3},{3,0},{4,5},{5,6},{6,7},{7,4},{8,9},{9,10},{10,1... | collective-permute-start | bytes 2211848 | tf_op jit(solution)/shard_map/ppermute | solution.py:128
  709.3 9.9 %collective-permute-start.69 = (f32[62,128]{1,0:T(8,128)S(1)}, f32[62,128]{1,0:T(8,128)S(1)}, u32[]{:S(2)}, u32[]{:S(2)}) collective-permute-start(f32[62,128]{1,0:T(8,128)S(1)} %add.919), channel_id=1, source_target_pairs={{0,1},{1,2},{2,3},{3,0},{4,5},{5,6},{6,7},{7,4},{8,9},{9,10},{10,1... | collective-permute-start | bytes 95240 | tf_op jit(solution)/shard_map/ppermute | solution.py:128
  712.9 8.7 %collective-permute-start.68 = (f32[62,128]{1,0:T(8,128)S(1)}, f32[62,128]{1,0:T(8,128)S(1)}, u32[]{:S(2)}, u32[]{:S(2)}) collective-permute-start(f32[62,128]{1,0:T(8,128)S(1)} %add.919), channel_id=1, source_target_pairs={{0,2},{1,3},{2,0},{3,1},{4,6},{5,7},{6,4},{7,5},{8,10},{9,11},{10,... | collective-permute-start | bytes 95240 | tf_op jit(solution)/shard_map/ppermute | solution.py:128
  713.9 23.9 %collective-permute-start.67 = (f32[62,128]{1,0:T(8,128)S(1)}, f32[62,128]{1,0:T(8,128)S(1)}, u32[]{:S(2)}, u32[]{:S(2)}) collective-permute-start(f32[62,128]{1,0:T(8,128)S(1)} %add.919), channel_id=1, source_target_pairs={{0,3},{1,0},{2,1},{3,2},{4,7},{5,4},{6,5},{7,6},{8,11},{9,8},{10,9... | collective-permute-start | bytes 95240 | tf_op jit(solution)/shard_map/ppermute | solution.py:128
  740.3 16.9 %collective-permute-start.60 = (bf16[160,2304]{1,0:T(8,128)(2,1)S(1)}, bf16[160,2304]{1,0:T(8,128)(2,1)}, u32[]{:S(2)}, u32[]{:S(2)}) collective-permute-start(bf16[160,2304]{1,0:T(8,128)(2,1)S(1)} %add_convert_fusion), channel_id=1, source_target_pairs={{0,1},{1,2},{2,3},{3,0},{4,5},{5,6},{6,7},{7,4},{8,9},{9,10},{10,1... | collective-permute-start | bytes 2211848 | tf_op jit(solution)/shard_map/ppermute | solution.py:128
  763.3 9.2 %collective-permute-start.61 = (bf16[160,1280]{1,0:T(8,128)(2,1)}, bf16[160,1280]{1,0:T(8,128)(2,1)}, u32[]{:S(2)}, u32[]{:S(2)}) collective-permute-start(bf16[160,1280]{1,0:T(8,128)(2,1)} %concatenate.202), channel_id=1, source_target_pairs={{0,1},{1,2},{2,3},{3,0},{4,5},{5,6},{6,7},{7,4},{8,9},{9,10},{10,1... | collective-permute-start | bytes 1228808 | tf_op jit(solution)/shard_map/ppermute | solution.py:128
  764.6 32.6 %collective-permute-start.62 = (bf16[160,1280]{1,0:T(8,128)(2,1)}, bf16[160,1280]{1,0:T(8,128)(2,1)S(1)}, u32[]{:S(2)}, u32[]{:S(2)}) collective-permute-start(bf16[160,1280]{1,0:T(8,128)(2,1)} %concatenate.203), channel_id=1, source_target_pairs={{0,2},{1,3},{2,0},{3,1},{4,6},{5,7},{6,4},{7,5},{8,10},{9,11},{10,... | collective-permute-start | bytes 1228808 | tf_op jit(solution)/shard_map/ppermute | solution.py:128
  766.5 34.7 %collective-permute-start.63 = (bf16[160,1280]{1,0:T(8,128)(2,1)}, bf16[160,1280]{1,0:T(8,128)(2,1)}, u32[]{:S(2)}, u32[]{:S(2)}) collective-permute-start(bf16[160,1280]{1,0:T(8,128)(2,1)} %concatenate.204), channel_id=1, source_target_pairs={{0,3},{1,0},{2,1},{3,2},{4,7},{5,4},{6,5},{7,6},{8,11},{9,8},{10,9... | collective-permute-start | bytes 1228808 | tf_op jit(solution)/shard_map/ppermute | solution.py:128
  (209 other events, 1354.9 us)
Sparse Core Ops, SparseCore 0:
  11.9 200.5 all-gather.2
  216.8 119.6 all-gather.4
  441.5 60.9 reduce-scatter.7
  506.0 152.2 reduce-scatter.5
  662.2 96.4 reduce-scatter.3

commit v4 on v3

--- a/solution.py
+++ b/solution.py
@@ -602,7 +602,7 @@
         return links.sum_ring(lambda t: by_own_rows(value, t))
 
     g_xq, g_dq, g_do, g_voc = rows_a
-    g_xq = columns([g_xq])
+    g_xq = last_columns([g_xq])
     g_sq = links.free(rows_task([g_dq, g_do, g_voc]))
     after = (nothing_of(g_sq) + nothing_of(g_xq)).astype(BF)
     g_b = columns([term + after for term in rows_b])

time: 824 us -> 826 us (level)
    ppermute x51, starting transfers between devices: 88.4 us -> 97.6 us  [send(): return lax.ppermute(value, 'mp', pairs)]
  transfers between devices with their start and end apart: 75 -> 75, of which waited for: 35 -> 38; matrix products, arithmetic and copies ran while one was open for 43% -> 43% of each run, Pallas kernels for 0% -> 0%
where the time goes in v4:
time: 826 us; the launch traced here: 815 us
  local copies, waits for them, and re-layouts  231 us (28%)
  waiting for transfers between devices  225 us (27%)
  matrix products  144 us (17%)
  starting transfers between devices  124 us (15%)
  other arithmetic  66.5 us (8%)
  between operations  23.5 us (3%)
    ppermute x51, waiting for transfers between devices, send(): return lax.ppermute(value, 'mp', pairs)  186 us
    ppermute x51, starting transfers between devices, send(): return lax.ppermute(value, 'mp', pairs)  97.6 us
    concatenate x10, local copies, waits for them, and re-layouts, beside(): return jnp.concatenate([part.reshape(dn * size, wide) for part in parts], 1)  65.1 us
    unnamed x407, local copies, waits for them, and re-layouts  49.1 us
    dot_general x19, matrix products, dot_tn(): lax.dot_general(left, right, (((0,), (0,)), ((), ())), preferred_element_...  40 us
    dot_general x19, matrix products, dot(): return jnp.dot(left, right, preferred_element_type=F32)  36.4 us
    slice x5, local copies, waits for them, and re-layouts, beside(): parts = [got[:, m, row:row + size, col:col + wide] for m in range(mn)]  36 us
    dot_general x19, matrix products, dot_t(): lax.dot_general(left, right, (((left.ndim - 1,), (right.ndim - 1,)), ((),...  35.9 us
  transfers between devices with their start and end apart: 75, of which 38 were waited for; matrix products, arithmetic and copies ran while one was open for 43% of the time, Pallas kernels for 0%

profile of v4, /device:TPU:11, one launch (start us, length us, event | category | flops | bytes accessed | tf_op | source)
XLA Modules:
  0.0 814.6 jit_solution(16181830245321021490)
XLA Ops:
  24.6 6.9 collective-permute-done.4
  61.5 5.3 collective-permute-done.12
  66.8 6.1 collective-permute-done.11
  73.6 4.5 collective-permute-start.13
  80.7 11.6 %collective-permute-start.15 = (bf16[64,768]{1,0:T(8,128)(2,1)}, bf16[64,768]{1,0:T(8,128)(2,1)S(1)}, u32[]{:S(2)}, u32[]{:S(2)}) collective-permute-start(bf16[64,768]{1,0:T(8,128)(2,1)} %get-tuple-element.42), channel_id=1, source_target_pairs={{0,1},{1,2},{2,3},{3,0},{4,5},{5,6},{6,7},{7,4},{8,9},{9,10},{10,1... | collective-permute-start | bytes 294920 | tf_op jit(solution)/shard_map/ppermute | solution.py:128
  92.3 4.0 collective-permute-start.14
  96.9 7.0 collective-permute-done.14
  120.6 22.7 %collective-permute-done.16 = bf16[256,768]{1,0:T(8,128)(2,1)S(1)} collective-permute-done((bf16[256,768]{1,0:T(8,128)(2,1)S(1)}, bf16[256,768]{1,0:T(8,128)(2,1)S(1)}, u32[]{:S(2)}, u32[]{:S(2)}) %collective-permute-start.16) | collective-permute-done | bytes 393248 | tf_op jit(solution)/shard_map/ppermute | solution.py:128
  146.3 22.9 %collective-permute-done.20 = bf16[256,768]{1,0:T(8,128)(2,1)S(1)} collective-permute-done((bf16[256,768]{1,0:T(8,128)(2,1)S(1)}, bf16[256,768]{1,0:T(8,128)(2,1)S(1)}, u32[]{:S(2)}, u32[]{:S(2)}) %collective-permute-start.20) | collective-permute-done | bytes 393248 | tf_op jit(solution)/shard_map/ppermute | solution.py:128
  169.4 5.8 collective-permute-start.21
  175.9 24.1 %collective-permute-done.21 = bf16[256,768]{1,0:T(8,128)(2,1)S(1)} collective-permute-done((bf16[256,768]{1,0:T(8,128)(2,1)S(1)}, bf16[256,768]{1,0:T(8,128)(2,1)S(1)}, u32[]{:S(2)}, u32[]{:S(2)}) %collective-permute-start.21) | collective-permute-done | bytes 393248 | tf_op jit(solution)/shard_map/ppermute | solution.py:128
  202.5 10.0 %all-gather.3.cloned.1.call-done = bf16[20480,640]{1,0:T(8,128)(2,1)} async-done(((bf16[640,640]{1,0:T(8,128)(2,1)}), bf16[20480,640]{1,0:T(8,128)(2,1)}) %all-gather.3.cloned.1.call-update) | async-done | bytes 26214416 | tf_op jit(solution)/shard_map/all_gather | solution.py:275
  225.9 4.2 fusion.186
  230.1 4.3 concatenate.169
  234.4 6.4 fusion.185
  240.8 12.5 %fusion.184 = (bf16[8,1,160,320]{3,2,1,0:T(8,128)(2,1)}, bf16[8,1,160,320]{3,2,1,0:T(8,128)(2,1)}, bf16[8,1,160,320]{3,2,1,0:T(8,128)(2,1)}, bf16[8,1,160,320]{3...) fusion(bf16[8,4,640,640]{3,2,1,0:T(8,128)(2,1)} %bitcast.418), kind=kLoop, calls=%fused_computation.615 | loop fusion | bytes 31129600 | tf_op jit(solution)/shard_map/slice | solution.py:283
  253.4 6.7 concatenate.172
  260.1 6.7 concatenate.171
  266.8 6.5 concatenate.170
  273.4 6.8 concatenate.175
  282.4 4.3 fusion.196
  287.1 4.9 fusion.31
  298.6 6.8 concatenate.174
  305.3 4.0 fusion.14
  311.5 6.8 concatenate.173
  318.3 4.0 convolution_convert_fusion.19
  324.5 6.8 concatenate.176
  345.1 4.0 fusion.188
  351.4 6.3 fusion.187
  357.6 6.6 fusion.189
  377.9 6.7 concatenate.181
  384.6 4.5 fusion.175
  389.1 6.9 concatenate.182
  396.0 6.6 fusion.200
  442.1 4.1 multiply_reduce_fusion.7
  477.5 5.8 fusion.5
  540.6 6.1 pad_maximum_fusion
  550.1 18.5 %collective-permute-done.34 = bf16[64,1280]{1,0:T(8,128)(2,1)S(1)} collective-permute-done((bf16[64,1280]{1,0:T(8,128)(2,1)S(1)}, bf16[64,1280]{1,0:T(8,128)(2,1)S(1)}, u32[]{:S(2)}, u32[]{:S(2)}) %collective-permute-start.34) | collective-permute-done | bytes 163872 | tf_op jit(solution)/shard_map/ppermute | solution.py:128
  608.3 5.3 multiply_reduce_fusion.1
  638.3 5.0 collective-permute-done.47
  663.7 4.0 collective-permute-start.55
  691.1 4.5 collective-permute-start.58
  704.9 6.0 collective-permute-done.58
  729.7 6.2 collective-permute-done.67
  742.9 13.7 %collective-permute-done.60 = bf16[160,2304]{1,0:T(8,128)(2,1)} collective-permute-done((bf16[160,2304]{1,0:T(8,128)(2,1)S(1)}, bf16[160,2304]{1,0:T(8,128)(2,1)}, u32[]{:S(2)}, u32[]{:S(2)}) %collective-permute-start.60) | collective-permute-done | bytes 737312 | tf_op jit(solution)/shard_map/ppermute | solution.py:128
  763.9 4.0 collective-permute-start.62
  773.5 23.8 %collective-permute-done.62 = bf16[160,1280]{1,0:T(8,128)(2,1)S(1)} collective-permute-done((bf16[160,1280]{1,0:T(8,128)(2,1)}, bf16[160,1280]{1,0:T(8,128)(2,1)S(1)}, u32[]{:S(2)}, u32[]{:S(2)}) %collective-permute-start.62) | collective-permute-done | bytes 409632 | tf_op jit(solution)/shard_map/ppermute | solution.py:128
  797.3 6.2 collective-permute-done.63
  (860 shorter events, 413.7 us)
Async XLA Ops:
  7.2 205.3 %all-gather.3.cloned.1.call-start = ((), (), s32[]{:S(2)}) async-start(), calls=%async_computation.3 | async-start | bytes 27033600 | tf_op jit(solution)/shard_map/all_gather | solution.py:275
  11.8 332.2 %all-gather.5.cloned.1.call-start = ((), (), s32[]{:S(2)}) async-start(), calls=%async_computation.4 | async-start | bytes 18382848 | tf_op jit(solution)/shard_map/all_gather | solution.py:275
  19.9 11.6 %collective-permute-start.4 = (bf16[272,480]{1,0:T(8,128)(2,1)}, bf16[272,480]{1,0:T(8,128)(2,1)S(1)}, u32[]{:S(2)}, u32[]{:S(2)}) collective-permute-start(bf16[272,480]{1,0:T(8,128)(2,1)} %get-tuple-element.44), channel_id=1, source_target_pairs={{0,8},{4,12},{8,0},{12,4},{16,24},{20,28},{24,16},{28,20},{1,9},{5... | collective-permute-start | bytes 783368 | tf_op jit(solution)/shard_map/ppermute | solution.py:129
  20.0 17.3 %collective-permute-start.3 = (bf16[272,480]{1,0:T(8,128)(2,1)}, bf16[272,480]{1,0:T(8,128)(2,1)}, u32[]{:S(2)}, u32[]{:S(2)}) collective-permute-start(bf16[272,480]{1,0:T(8,128)(2,1)} %get-tuple-element.44), channel_id=1, source_target_pairs={{0,4},{4,0},{8,12},{12,8},{16,20},{20,16},{24,28},{28,24},{1,5},{5... | collective-permute-start | bytes 783368 | tf_op jit(solution)/shard_map/ppermute | solution.py:129
  22.0 14.6 %collective-permute-start.6 = (bf16[272,480]{1,0:T(8,128)(2,1)}, bf16[272,480]{1,0:T(8,128)(2,1)S(1)}, u32[]{:S(2)}, u32[]{:S(2)}) collective-permute-start(bf16[272,480]{1,0:T(8,128)(2,1)} %get-tuple-element.44), channel_id=1, source_target_pairs={{0,16},{4,20},{8,24},{12,28},{16,0},{20,4},{24,8},{28,12},{1,17},{... | collective-permute-start | bytes 783368 | tf_op jit(solution)/shard_map/ppermute | solution.py:129
  31.5 9.9 %collective-permute-start.8 = (bf16[272,480]{1,0:T(8,128)(2,1)S(1)}, bf16[272,480]{1,0:T(8,128)(2,1)S(1)}, u32[]{:S(2)}, u32[]{:S(2)}) collective-permute-start(bf16[272,480]{1,0:T(8,128)(2,1)S(1)} %collective-permute-done.4), channel_id=1, source_target_pairs={{0,16},{4,20},{8,24},{12,28},{16,0},{20,4},{24,8},{28,12},{1,17},{... | collective-permute-start | bytes 783368 | tf_op jit(solution)/shard_map/ppermute | solution.py:129
  32.9 10.3 %collective-permute-start.5 = (bf16[272,480]{1,0:T(8,128)(2,1)S(1)}, bf16[272,480]{1,0:T(8,128)(2,1)S(1)}, u32[]{:S(2)}, u32[]{:S(2)}) collective-permute-start(bf16[272,480]{1,0:T(8,128)(2,1)S(1)} %collective-permute-done.4), channel_id=1, source_target_pairs={{0,4},{4,0},{8,12},{12,8},{16,20},{20,16},{24,28},{28,24},{1,5},{5... | collective-permute-start | bytes 783368 | tf_op jit(solution)/shard_map/ppermute | solution.py:129
  53.6 7.9 collective-permute-start.10
  54.6 12.2 %collective-permute-start.12 = (bf16[64,768]{1,0:T(8,128)(2,1)S(1)}, bf16[64,768]{1,0:T(8,128)(2,1)S(1)}, u32[]{:S(2)}, u32[]{:S(2)}) collective-permute-start(bf16[64,768]{1,0:T(8,128)(2,1)S(1)} %get-tuple-element.175), channel_id=1, source_target_pairs={{0,3},{1,0},{2,1},{3,2},{4,7},{5,4},{6,5},{7,6},{8,11},{9,8},{10,9... | collective-permute-start | bytes 294920 | tf_op jit(solution)/shard_map/ppermute | solution.py:128
  55.1 17.8 %collective-permute-start.11 = (bf16[64,768]{1,0:T(8,128)(2,1)S(1)}, bf16[64,768]{1,0:T(8,128)(2,1)S(1)}, u32[]{:S(2)}, u32[]{:S(2)}) collective-permute-start(bf16[64,768]{1,0:T(8,128)(2,1)S(1)} %get-tuple-element.176), channel_id=1, source_target_pairs={{0,2},{1,3},{2,0},{3,1},{4,6},{5,7},{6,4},{7,5},{8,10},{9,11},{10,... | collective-permute-start | bytes 294920 | tf_op jit(solution)/shard_map/ppermute | solution.py:128
  73.6 22.6 %collective-permute-start.13 = (bf16[64,768]{1,0:T(8,128)(2,1)}, bf16[64,768]{1,0:T(8,128)(2,1)S(1)}, u32[]{:S(2)}, u32[]{:S(2)}) collective-permute-start(bf16[64,768]{1,0:T(8,128)(2,1)} %get-tuple-element.42), channel_id=1, source_target_pairs={{0,3},{1,0},{2,1},{3,2},{4,7},{5,4},{6,5},{7,6},{8,11},{9,8},{10,9... | collective-permute-start | bytes 294920 | tf_op jit(solution)/shard_map/ppermute | solution.py:128
  80.7 23.8 %collective-permute-start.15 = (bf16[64,768]{1,0:T(8,128)(2,1)}, bf16[64,768]{1,0:T(8,128)(2,1)S(1)}, u32[]{:S(2)}, u32[]{:S(2)}) collective-permute-start(bf16[64,768]{1,0:T(8,128)(2,1)} %get-tuple-element.42), channel_id=1, source_target_pairs={{0,1},{1,2},{2,3},{3,0},{4,5},{5,6},{6,7},{7,4},{8,9},{9,10},{10,1... | collective-permute-start | bytes 294920 | tf_op jit(solution)/shard_map/ppermute | solution.py:128
  92.3 11.6 %collective-permute-start.14 = (bf16[64,768]{1,0:T(8,128)(2,1)}, bf16[64,768]{1,0:T(8,128)(2,1)S(1)}, u32[]{:S(2)}, u32[]{:S(2)}) collective-permute-start(bf16[64,768]{1,0:T(8,128)(2,1)} %get-tuple-element.42), channel_id=1, source_target_pairs={{0,2},{1,3},{2,0},{3,1},{4,6},{5,7},{6,4},{7,5},{8,10},{9,11},{10,... | collective-permute-start | bytes 294920 | tf_op jit(solution)/shard_map/ppermute | solution.py:128
  112.1 8.4 %collective-permute-start.18 = (f32[2,4,256]{2,1,0:T(4,128)S(1)}, f32[2,4,256]{2,1,0:T(4,128)S(1)}, u32[]{:S(2)}, u32[]{:S(2)}) collective-permute-start(f32[2,4,256]{2,1,0:T(4,128)S(1)} %get-tuple-element.229), channel_id=1, source_target_pairs={{0,2},{1,3},{2,0},{3,1},{4,6},{5,7},{6,4},{7,5},{8,10},{9,11},{10,... | collective-permute-start | bytes 24584 | tf_op jit(solution)/shard_map/ppermute | solution.py:128
  119.6 23.7 %collective-permute-start.16 = (bf16[256,768]{1,0:T(8,128)(2,1)S(1)}, bf16[256,768]{1,0:T(8,128)(2,1)S(1)}, u32[]{:S(2)}, u32[]{:S(2)}) collective-permute-start(bf16[256,768]{1,0:T(8,128)(2,1)S(1)} %dynamic-slice_bitcast_fusion), channel_id=1, source_target_pairs={{0,1},{1,2},{2,3},{3,0},{4,5},{5,6},{6,7},{7,4},{8,9},{9,10},{10,1... | collective-permute-start | bytes 1179656 | tf_op jit(solution)/shard_map/ppermute | solution.py:128
  143.5 25.7 %collective-permute-start.20 = (bf16[256,768]{1,0:T(8,128)(2,1)S(1)}, bf16[256,768]{1,0:T(8,128)(2,1)S(1)}, u32[]{:S(2)}, u32[]{:S(2)}) collective-permute-start(bf16[256,768]{1,0:T(8,128)(2,1)S(1)} %fusion.87), channel_id=1, source_target_pairs={{0,1},{1,2},{2,3},{3,0},{4,5},{5,6},{6,7},{7,4},{8,9},{9,10},{10,1... | collective-permute-start | bytes 1179656 | tf_op jit(solution)/shard_map/ppermute | solution.py:128
  169.4 30.6 %collective-permute-start.21 = (bf16[256,768]{1,0:T(8,128)(2,1)S(1)}, bf16[256,768]{1,0:T(8,128)(2,1)S(1)}, u32[]{:S(2)}, u32[]{:S(2)}) collective-permute-start(bf16[256,768]{1,0:T(8,128)(2,1)S(1)} %fusion.85), channel_id=1, source_target_pairs={{0,1},{1,2},{2,3},{3,0},{4,5},{5,6},{6,7},{7,4},{8,9},{9,10},{10,1... | collective-permute-start | bytes 1179656 | tf_op jit(solution)/shard_map/ppermute | solution.py:128
  216.7 439.6 %reduce-scatter.8.cloned.1.call-start = ((), (), s32[]{:S(2)}) async-start(), calls=%async_computation.7 | async-start | bytes 6856704 | tf_op jit(solution)/shard_map/reduce_scatter | solution.py:469
  366.9 49.3 %collective-permute-start.27 = (bf16[262,512]{1,0:T(8,128)(2,1)}, bf16[262,512]{1,0:T(8,128)(2,1)S(1)}, u32[]{:S(2)}, u32[]{:S(2)}) collective-permute-start(bf16[262,512]{1,0:T(8,128)(2,1)} %get-tuple-element.114), channel_id=1, source_target_pairs={{0,1},{1,2},{2,3},{3,0},{4,5},{5,6},{6,7},{7,4},{8,9},{9,10},{10,1... | collective-permute-start | bytes 804872 | tf_op jit(solution)/shard_map/ppermute | solution.py:128
  369.1 46.1 %collective-permute-start.26 = (bf16[262,512]{1,0:T(8,128)(2,1)}, bf16[262,512]{1,0:T(8,128)(2,1)}, u32[]{:S(2)}, u32[]{:S(2)}) collective-permute-start(bf16[262,512]{1,0:T(8,128)(2,1)} %get-tuple-element.115), channel_id=1, source_target_pairs={{0,2},{1,3},{2,0},{3,1},{4,6},{5,7},{6,4},{7,5},{8,10},{9,11},{10,... | collective-permute-start | bytes 804872 | tf_op jit(solution)/shard_map/ppermute | solution.py:128
  372.3 41.8 %collective-permute-start.25 = (bf16[262,512]{1,0:T(8,128)(2,1)}, bf16[262,512]{1,0:T(8,128)(2,1)}, u32[]{:S(2)}, u32[]{:S(2)}) collective-permute-start(bf16[262,512]{1,0:T(8,128)(2,1)} %get-tuple-element.116), channel_id=1, source_target_pairs={{0,3},{1,0},{2,1},{3,2},{4,7},{5,4},{6,5},{7,6},{8,11},{9,8},{10,9... | collective-permute-start | bytes 804872 | tf_op jit(solution)/shard_map/ppermute | solution.py:128
  441.4 238.3 %reduce-scatter.6.cloned.1.call-start = ((), (), s32[]{:S(2)}) async-start(), calls=%async_computation.6 | async-start | bytes 26542080 | tf_op jit(solution)/shard_map/reduce_scatter | solution.py:469
  494.8 264.2 %reduce-scatter.4.cloned.1.call-start = ((), (), s32[]{:S(2)}) async-start(), calls=%async_computation.5 | async-start | bytes 14745600 | tf_op jit(solution)/shard_map/reduce_scatter | solution.py:469
  502.7 35.1 %collective-permute-start.24 = (bf16[262,512]{1,0:T(8,128)(2,1)S(1)}, bf16[262,512]{1,0:T(8,128)(2,1)S(1)}, u32[]{:S(2)}, u32[]{:S(2)}) collective-permute-start(bf16[262,512]{1,0:T(8,128)(2,1)S(1)} %get-tuple-element.117), channel_id=1, source_target_pairs={{0,1},{1,2},{2,3},{3,0},{4,5},{5,6},{6,7},{7,4},{8,9},{9,10},{10,1... | collective-permute-start | bytes 804872 | tf_op jit(solution)/shard_map/ppermute | solution.py:128
  505.4 30.8 %collective-permute-start.23 = (bf16[262,512]{1,0:T(8,128)(2,1)S(1)}, bf16[262,512]{1,0:T(8,128)(2,1)S(1)}, u32[]{:S(2)}, u32[]{:S(2)}) collective-permute-start(bf16[262,512]{1,0:T(8,128)(2,1)S(1)} %get-tuple-element.119), channel_id=1, source_target_pairs={{0,2},{1,3},{2,0},{3,1},{4,6},{5,7},{6,4},{7,5},{8,10},{9,11},{10,... | collective-permute-start | bytes 804872 | tf_op jit(solution)/shard_map/ppermute | solution.py:128
  507.4 28.7 %collective-permute-start.22 = (bf16[262,512]{1,0:T(8,128)(2,1)S(1)}, bf16[262,512]{1,0:T(8,128)(2,1)S(1)}, u32[]{:S(2)}, u32[]{:S(2)}) collective-permute-start(bf16[262,512]{1,0:T(8,128)(2,1)S(1)} %get-tuple-element.120), channel_id=1, source_target_pairs={{0,3},{1,0},{2,1},{3,2},{4,7},{5,4},{6,5},{7,6},{8,11},{9,8},{10,9... | collective-permute-start | bytes 804872 | tf_op jit(solution)/shard_map/ppermute | solution.py:128
  531.2 46.2 %collective-permute-start.30 = (bf16[256,768]{1,0:T(8,128)(2,1)}, bf16[256,768]{1,0:T(8,128)(2,1)S(1)}, u32[]{:S(2)}, u32[]{:S(2)}) collective-permute-start(bf16[256,768]{1,0:T(8,128)(2,1)} %get-tuple-element.262), channel_id=1, source_target_pairs={{0,1},{1,2},{2,3},{3,0},{4,5},{5,6},{6,7},{7,4},{8,9},{9,10},{10,1... | collective-permute-start | bytes 1179656 | tf_op jit(solution)/shard_map/ppermute | solution.py:128
  532.4 44.2 %collective-permute-start.29 = (bf16[256,768]{1,0:T(8,128)(2,1)}, bf16[256,768]{1,0:T(8,128)(2,1)S(1)}, u32[]{:S(2)}, u32[]{:S(2)}) collective-permute-start(bf16[256,768]{1,0:T(8,128)(2,1)} %get-tuple-element.262), channel_id=1, source_target_pairs={{0,2},{1,3},{2,0},{3,1},{4,6},{5,7},{6,4},{7,5},{8,10},{9,11},{10,... | collective-permute-start | bytes 1179656 | tf_op jit(solution)/shard_map/ppermute | solution.py:128
  536.1 39.6 %collective-permute-start.28 = (bf16[256,768]{1,0:T(8,128)(2,1)}, bf16[256,768]{1,0:T(8,128)(2,1)S(1)}, u32[]{:S(2)}, u32[]{:S(2)}) collective-permute-start(bf16[256,768]{1,0:T(8,128)(2,1)} %get-tuple-element.262), channel_id=1, source_target_pairs={{0,3},{1,0},{2,1},{3,2},{4,7},{5,4},{6,5},{7,6},{8,11},{9,8},{10,9... | collective-permute-start | bytes 1179656 | tf_op jit(solution)/shard_map/ppermute | solution.py:128
  536.3 32.4 %collective-permute-start.34 = (bf16[64,1280]{1,0:T(8,128)(2,1)S(1)}, bf16[64,1280]{1,0:T(8,128)(2,1)S(1)}, u32[]{:S(2)}, u32[]{:S(2)}) collective-permute-start(bf16[64,1280]{1,0:T(8,128)(2,1)S(1)} %constant_dynamic-slice_fusion.67), channel_id=1, source_target_pairs={{0,1},{1,2},{2,3},{3,0},{4,5},{5,6},{6,7},{7,4},{8,9},{9,10},{10,1... | collective-permute-start | bytes 491528 | tf_op jit(solution)/shard_map/ppermute | solution.py:128
  574.7 39.4 %collective-permute-start.36 = (bf16[64,1280]{1,0:T(8,128)(2,1)S(1)}, bf16[64,1280]{1,0:T(8,128)(2,1)S(1)}, u32[]{:S(2)}, u32[]{:S(2)}) collective-permute-start(bf16[64,1280]{1,0:T(8,128)(2,1)S(1)} %add_convert_fusion.5), channel_id=1, source_target_pairs={{0,1},{1,2},{2,3},{3,0},{4,5},{5,6},{6,7},{7,4},{8,9},{9,10},{10,1... | collective-permute-start | bytes 491528 | tf_op jit(solution)/shard_map/ppermute | solution.py:128
  602.0 11.7 %collective-permute-start.40 = (bf16[128,768]{1,0:T(8,128)(2,1)S(1)}, bf16[128,768]{1,0:T(8,128)(2,1)S(1)}, u32[]{:S(2)}, u32[]{:S(2)}) collective-permute-start(bf16[128,768]{1,0:T(8,128)(2,1)S(1)} %select_convert_fusion), channel_id=1, source_target_pairs={{0,4},{4,0},{8,12},{12,8},{16,20},{20,16},{24,28},{28,24},{1,5},{5... | collective-permute-start | bytes 589832 | tf_op jit(solution)/shard_map/ppermute | solution.py:129
  621.9 8.0 collective-permute-start.43
  647.9 74.7 %collective-permute-start.39 = (bf16[64,160]{1,0:T(8,128)(2,1)}, bf16[64,160]{1,0:T(8,128)(2,1)}, u32[]{:S(2)}, u32[]{:S(2)}) collective-permute-start(bf16[64,160]{1,0:T(8,128)(2,1)} %select_convert_fusion.5), channel_id=1, source_target_pairs={{0,4},{4,0},{8,12},{12,8},{16,20},{20,16},{24,28},{28,24},{1,5},{5... | collective-permute-start | bytes 61448 | tf_op jit(solution)/shard_map/ppermute | solution.py:129
  662.2 33.4 %collective-permute-start.51 = (bf16[64,1280]{1,0:T(8,128)(2,1)}, bf16[64,1280]{1,0:T(8,128)(2,1)}, u32[]{:S(2)}, u32[]{:S(2)}) collective-permute-start(bf16[64,1280]{1,0:T(8,128)(2,1)} %add_convert_fusion.3), channel_id=1, source_target_pairs={{0,1},{1,2},{2,3},{3,0},{4,5},{5,6},{6,7},{7,4},{8,9},{9,10},{10,1... | collective-permute-start | bytes 491528 | tf_op jit(solution)/shard_map/ppermute | solution.py:128
  663.7 8.4 %collective-permute-start.55 = (bf16[96,512]{1,0:T(8,128)(2,1)S(1)}, bf16[96,512]{1,0:T(8,128)(2,1)S(1)}, u32[]{:S(2)}, u32[]{:S(2)}) collective-permute-start(bf16[96,512]{1,0:T(8,128)(2,1)S(1)} %get-tuple-element.169), channel_id=1, source_target_pairs={{0,1},{1,2},{2,3},{3,0},{4,5},{5,6},{6,7},{7,4},{8,9},{9,10},{10,1... | collective-permute-start | bytes 294920 | tf_op jit(solution)/shard_map/ppermute | solution.py:128
  667.7 7.0 collective-permute-start.57
  669.1 7.6 collective-permute-start.56
  691.1 19.7 %collective-permute-start.58 = (bf16[160,2304]{1,0:T(8,128)(2,1)S(1)}, bf16[160,2304]{1,0:T(8,128)(2,1)S(1)}, u32[]{:S(2)}, u32[]{:S(2)}) collective-permute-start(bf16[160,2304]{1,0:T(8,128)(2,1)S(1)} %concatenate.197), channel_id=1, source_target_pairs={{0,1},{1,2},{2,3},{3,0},{4,5},{5,6},{6,7},{7,4},{8,9},{9,10},{10,1... | collective-permute-start | bytes 2211848 | tf_op jit(solution)/shard_map/ppermute | solution.py:128
  703.1 8.2 %collective-permute-start.65 = (f32[62,128]{1,0:T(8,128)}, f32[62,128]{1,0:T(8,128)}, u32[]{:S(2)}, u32[]{:S(2)}) collective-permute-start(f32[62,128]{1,0:T(8,128)} %fusion.306), channel_id=1, source_target_pairs={{0,8},{4,12},{8,0},{12,4},{16,24},{20,28},{24,16},{28,20},{1,9},{5... | collective-permute-start | bytes 95240 | tf_op jit(solution)/shard_map/ppermute | solution.py:129
  711.1 27.6 %collective-permute-start.59 = (bf16[160,2304]{1,0:T(8,128)(2,1)S(1)}, bf16[160,2304]{1,0:T(8,128)(2,1)S(1)}, u32[]{:S(2)}, u32[]{:S(2)}) collective-permute-start(bf16[160,2304]{1,0:T(8,128)(2,1)S(1)} %add_convert_fusion.1), channel_id=1, source_target_pairs={{0,1},{1,2},{2,3},{3,0},{4,5},{5,6},{6,7},{7,4},{8,9},{9,10},{10,1... | collective-permute-start | bytes 2211848 | tf_op jit(solution)/shard_map/ppermute | solution.py:128
  716.2 11.3 %collective-permute-start.69 = (f32[62,128]{1,0:T(8,128)S(1)}, f32[62,128]{1,0:T(8,128)S(1)}, u32[]{:S(2)}, u32[]{:S(2)}) collective-permute-start(f32[62,128]{1,0:T(8,128)S(1)} %add.919), channel_id=1, source_target_pairs={{0,1},{1,2},{2,3},{3,0},{4,5},{5,6},{6,7},{7,4},{8,9},{9,10},{10,1... | collective-permute-start | bytes 95240 | tf_op jit(solution)/shard_map/ppermute | solution.py:128
  717.4 12.3 %collective-permute-start.68 = (f32[62,128]{1,0:T(8,128)S(1)}, f32[62,128]{1,0:T(8,128)S(1)}, u32[]{:S(2)}, u32[]{:S(2)}) collective-permute-start(f32[62,128]{1,0:T(8,128)S(1)} %add.919), channel_id=1, source_target_pairs={{0,2},{1,3},{2,0},{3,1},{4,6},{5,7},{6,4},{7,5},{8,10},{9,11},{10,... | collective-permute-start | bytes 95240 | tf_op jit(solution)/shard_map/ppermute | solution.py:128
  721.2 14.7 %collective-permute-start.67 = (f32[62,128]{1,0:T(8,128)S(1)}, f32[62,128]{1,0:T(8,128)S(1)}, u32[]{:S(2)}, u32[]{:S(2)}) collective-permute-start(f32[62,128]{1,0:T(8,128)S(1)} %add.919), channel_id=1, source_target_pairs={{0,3},{1,0},{2,1},{3,2},{4,7},{5,4},{6,5},{7,6},{8,11},{9,8},{10,9... | collective-permute-start | bytes 95240 | tf_op jit(solution)/shard_map/ppermute | solution.py:128
  738.9 17.7 %collective-permute-start.60 = (bf16[160,2304]{1,0:T(8,128)(2,1)S(1)}, bf16[160,2304]{1,0:T(8,128)(2,1)}, u32[]{:S(2)}, u32[]{:S(2)}) collective-permute-start(bf16[160,2304]{1,0:T(8,128)(2,1)S(1)} %add_convert_fusion), channel_id=1, source_target_pairs={{0,1},{1,2},{2,3},{3,0},{4,5},{5,6},{6,7},{7,4},{8,9},{9,10},{10,1... | collective-permute-start | bytes 2211848 | tf_op jit(solution)/shard_map/ppermute | solution.py:128
  762.6 10.9 %collective-permute-start.61 = (bf16[160,1280]{1,0:T(8,128)(2,1)}, bf16[160,1280]{1,0:T(8,128)(2,1)}, u32[]{:S(2)}, u32[]{:S(2)}) collective-permute-start(bf16[160,1280]{1,0:T(8,128)(2,1)} %concatenate.202), channel_id=1, source_target_pairs={{0,1},{1,2},{2,3},{3,0},{4,5},{5,6},{6,7},{7,4},{8,9},{9,10},{10,1... | collective-permute-start | bytes 1228808 | tf_op jit(solution)/shard_map/ppermute | solution.py:128
  763.9 33.4 %collective-permute-start.62 = (bf16[160,1280]{1,0:T(8,128)(2,1)}, bf16[160,1280]{1,0:T(8,128)(2,1)S(1)}, u32[]{:S(2)}, u32[]{:S(2)}) collective-permute-start(bf16[160,1280]{1,0:T(8,128)(2,1)} %concatenate.203), channel_id=1, source_target_pairs={{0,2},{1,3},{2,0},{3,1},{4,6},{5,7},{6,4},{7,5},{8,10},{9,11},{10,... | collective-permute-start | bytes 1228808 | tf_op jit(solution)/shard_map/ppermute | solution.py:128
  768.8 34.7 %collective-permute-start.63 = (bf16[160,1280]{1,0:T(8,128)(2,1)}, bf16[160,1280]{1,0:T(8,128)(2,1)}, u32[]{:S(2)}, u32[]{:S(2)}) collective-permute-start(bf16[160,1280]{1,0:T(8,128)(2,1)} %concatenate.204), channel_id=1, source_target_pairs={{0,3},{1,0},{2,1},{3,2},{4,7},{5,4},{6,5},{7,6},{8,11},{9,8},{10,9... | collective-permute-start | bytes 1228808 | tf_op jit(solution)/shard_map/ppermute | solution.py:128
  (209 other events, 1256.2 us)
Sparse Core Ops, SparseCore 0:
  11.9 200.5 all-gather.2
  216.8 119.7 all-gather.4
  441.6 60.9 reduce-scatter.7
  506.1 151.8 reduce-scatter.5
  661.8 96.2 reduce-scatter.3
